TPU v7x, 128 devices: a whole 4x4x4 slice. The times are simulated.
128 devices in a mesh: row: 16 (over z_hi, x, core), col: 8 (over y, z_lo).
Axes of the slice: x: 4, y: 4, z: 4 (z_hi: 2, z_lo: 2; z = z_hi * 2 + z_lo), core: 2. Of those that a mesh axis runs over, the one named last changes fastest.
Arguments:
- node_features: bfloat16 [8, 16, 1024, 256], P('col', 'row'), may hold values from -6 to 6
- weight: bfloat16 [256, 256], replicated, may hold values from -0.375 to 0.375
- bias: float32 [256], replicated, may hold values from -4 to 4
- adj_blocks: bfloat16 [16, 8, 192, 128, 128], P('row', 'col'), may hold values from -0.15625 to 0.15625
- block_row: int32 [16, 8, 192], P('row', 'col'), may hold values from 0 to 63, as said below
- block_col: int32 [16, 8, 192], P('row', 'col'), may hold values from 0 to 127
- slot_count: int32 [16, 8], P('row', 'col'), may hold values from 48 to 192, as said below
- cotangent: bfloat16 [16, 8, 1024, 256], P('row', 'col'), may hold values from -6 to 6
Outputs:
- layer_out: bfloat16 [16, 8, 1024, 256], P('row', 'col')
- grad_input: bfloat16 [8, 16, 1024, 256], P('col', 'row')
- grad_weight: float32 [256, 256], replicated
- grad_bias: float32 [256], replicated
Inputs may be any that keep to these rules, and one draw needn't show every extreme that they name: Within one grid cell the pairs (block_row, block_col) of all 192 slots are distinct; block_row lies in 0 to 63. `slot_count`: each cell holds 192, 96, 64 or 48 live slots; some cell holds 192 in every draw.
All inputs are finite; a program needn't handle non-finite values.
Results may differ from a plain program's by a relative error of at most 0.022.
Values may be sent and summed in bfloat16 or wider, within the bound.
No kernel may reach another device: no remote copies, remote signals or barrier semaphores. Data moves between devices by JAX's collectives and lax.ppermute only.
A program may use at most 128 MiB of HBM per device.

v0:
```python
import jax
import jax.numpy as jnp
from jax import lax
from jax.sharding import PartitionSpec as P


def cell_forward(blocks, row_ids, col_ids, live_slots, table, row_count):
    size = blocks.shape[-1]
    width = table.shape[-1]
    picked = table.reshape(-1, size, width)[col_ids]
    contrib = jnp.einsum("sbk,skf->sbf", blocks, picked, preferred_element_type=jnp.float32)
    targets = jnp.where(live_slots, row_ids, row_count)
    summed = jax.ops.segment_sum(contrib, targets, num_segments=row_count + 1)[:row_count]
    return summed.reshape(row_count * size, width)


def cell_backward(blocks, row_ids, col_ids, live_slots, table, col_count):
    size = blocks.shape[-1]
    width = table.shape[-1]
    picked = table.reshape(-1, size, width)[row_ids]
    contrib = jnp.einsum("sbk,sbf->skf", blocks, picked, preferred_element_type=jnp.float32)
    targets = jnp.where(live_slots, col_ids, col_count)
    summed = jax.ops.segment_sum(contrib, targets, num_segments=col_count + 1)[:col_count]
    return summed.reshape(col_count * size, width)


def local(node_features, weight, bias, adj_blocks, block_row, block_col, slot_count, cotangent):
    node_rows = node_features.shape[2]
    width = node_features.shape[3]
    blocks = adj_blocks[0, 0]
    size = blocks.shape[-1]
    row_count = lax.axis_size("col") * node_rows // size
    col_count = lax.axis_size("row") * node_rows // size
    row_ids = block_row[0, 0]
    col_ids = block_col[0, 0]
    live_slots = jnp.arange(blocks.shape[0]) < slot_count[0, 0]
    own_input = node_features[0, 0]
    column_input = lax.all_gather(own_input, "row", axis=0, tiled=True)
    column_table = jnp.dot(column_input, weight, preferred_element_type=jnp.float32).astype(
        jnp.bfloat16
    )
    cell_sum = cell_forward(blocks, row_ids, col_ids, live_slots, column_table, row_count)
    aggregate = lax.psum_scatter(
        cell_sum.astype(jnp.bfloat16), "col", scatter_dimension=0, tiled=True
    ).astype(jnp.float32)
    pre = aggregate + bias
    layer_out = jax.nn.silu(pre).astype(jnp.bfloat16)
    sigma = jax.nn.sigmoid(pre)
    grad_pre = (cotangent[0, 0].astype(jnp.float32) * sigma * (1.0 + pre * (1.0 - sigma))).astype(
        jnp.bfloat16
    )
    row_table = lax.all_gather(grad_pre, "col", axis=0, tiled=True)
    cell_back = cell_backward(blocks, row_ids, col_ids, live_slots, row_table, col_count)
    grad_projected = lax.psum_scatter(
        cell_back.astype(jnp.bfloat16), "row", scatter_dimension=0, tiled=True
    )
    grad_input = lax.dot_general(
        grad_projected, weight, (((1,), (1,)), ((), ())), preferred_element_type=jnp.float32
    ).astype(jnp.bfloat16)
    weight_term = lax.dot_general(
        own_input, grad_projected, (((0,), (0,)), ((), ())), preferred_element_type=jnp.float32
    )
    bias_term = jnp.sum(grad_pre.astype(jnp.float32), axis=0)
    grad_weight, grad_bias = lax.psum((weight_term, bias_term), ("row", "col"))
    return (
        layer_out.reshape(1, 1, node_rows, width),
        grad_input.reshape(1, 1, node_rows, width),
        grad_weight,
        grad_bias,
    )


def solution(mesh):
    placed = (
        P("col", "row", None, None),
        P(),
        P(),
        P("row", "col", None, None, None),
        P("row", "col", None),
        P("row", "col", None),
        P("row", "col"),
        P("row", "col", None, None),
    )
    return jax.shard_map(
        local,
        mesh=mesh,
        in_specs=placed,
        out_specs=(P("row", "col", None, None), P("col", "row", None, None), P(), P()),
        check_vma=False,
    )
```

profile of v0, /device:TPU:1, one launch (start us, length us, event | category | flops | bytes accessed | tf_op | source)
XLA Modules:
  0.0 784.8 jit_solution(6394129753688853191)
XLA Ops:
  7.2 0.0 all-gather.6.cloned.1.call-start
  7.2 0.7 all-gather.6.cloned.1.call-update
  7.9 0.0 reduce-scatter.3.cloned.1.call-start
  8.6 0.7 compare_select_fusion
  9.3 77.6 %all-gather.6.cloned.1.call-done = bf16[1,1,16384,256]{3,2,1,0:T(8,128)(2,1)} async-done(((bf16[1,1,1024,256]{3,2,1,0:T(8,128)(2,1)}), bf16[1,1,16384,256]{3,2,1,0:T(8,128)(2,1)}) %all-gather.6.cloned.1.call-update) | async-done | bytes 8388624 | tf_op jit(solution)/shard_map/all_gather | solution.py:38
  86.9 8.9 %convolution_convert_fusion = bf16[16384,256]{1,0:T(8,128)(2,1)} fusion(bf16[256,256]{1,0:T(8,128)(2,1)S(1)} %copy-done, bf16[1,1,16384,256]{3,2,1,0:T(8,128)(2,1)} %all-gather.6.cloned.1.call-done), kind=kOutput, calls=%fused_computation.4 | convolution fusion | flops 2151677952 | bytes 16908288 | tf_op jit(solution)/shard_map/dot_general | solution.py:39
  95.8 11.6 %gather_fusion = bf16[192,128,256]{2,1,0:T(8,128)(2,1)} fusion(bf16[128,128,256]{2,1,0:T(8,128)(2,1)} %bitcast.47, s32[1024]{0:T(1024)S(1)} %pad_clamp_fusion.1), kind=kCustom, calls=%fused_computation | custom fusion | bytes 25166592 | tf_op jit(solution)/shard_map/gather | solution.py:10
  107.4 13.8 %convolution_bitcast_fusion.1 = f32[192,128,256]{1,2,0:T(8,128)} fusion(bf16[192,128,256]{2,1,0:T(8,128)(2,1)} %gather_fusion, bf16[1,1,192,128,128]{4,3,2,1,0:T(8,128)(2,1)} %param.11), kind=kOutput, calls=%fused_computation.7 | convolution fusion | flops 1610612736 | bytes 44040192 | tf_op jit(solution)/shard_map/sbk,skf->sbf/dot_general | solution.py:11
  121.2 24.7 %copy.16 = f32[192,128,256]{2,1,0:T(8,128)} copy(f32[192,128,256]{1,2,0:T(8,128)} %convolution_bitcast_fusion.1) | data formatting | bytes 50331648 | tf_op jit(solution)/shard_map/sbk,skf->sbf/dot_general | solution.py:11
  145.9 4.3 broadcast_in_dim.16
  150.2 57.3 %scatter_fusion = f32[65,128,256]{2,1,0:T(8,128)} fusion(f32[65,128,256]{2,1,0:T(8,128)} %broadcast_in_dim.16, s32[192]{0:T(256)S(1)} %bitcast.52, f32[192,128,256]{2,1,0:T(8,128)} %copy.16), kind=kCustom, calls=%fused_computation.2 | custom fusion | flops 6291456 | bytes 75498240 | tf_op jit(solution)/shard_map/scatter-add | solution.py:13
  207.5 6.0 slice.19
  213.5 0.0 reduce-scatter.3.cloned.1.call-update
  213.5 0.0 all-gather.4.cloned.1.call-start
  213.6 92.4 %reduce-scatter.3.cloned.1.call-done = bf16[1024,256]{1,0:T(8,128)(2,1)} async-done(((bf16[8192,256]{1,0:T(8,128)(2,1)}), bf16[1024,256]{1,0:T(8,128)(2,1)}) %reduce-scatter.3.cloned.1.call-update) | async-done | bytes 524304 | tf_op jit(solution)/shard_map/reduce_scatter | solution.py:43
  306.0 2.5 convert_reduce_fusion
  308.5 0.0 all-gather.4.cloned.1.call-update
  308.5 0.2 reduce-scatter.5.cloned.1.call-start
  308.8 90.6 %all-gather.4.cloned.1.call-done = bf16[8192,256]{1,0:T(8,128)(2,1)} async-done(((bf16[1024,256]{1,0:T(8,128)(2,1)}), bf16[8192,256]{1,0:T(8,128)(2,1)}) %all-gather.4.cloned.1.call-update) | async-done | bytes 4194320 | tf_op jit(solution)/shard_map/all_gather | solution.py:52
  399.4 10.4 %gather_fusion.1 = bf16[192,128,256]{2,1,0:T(8,128)(2,1)} fusion(bf16[64,128,256]{2,1,0:T(8,128)(2,1)} %bitcast.48, s32[1024]{0:T(1024)S(1)} %pad_clamp_fusion), kind=kCustom, calls=%fused_computation.1 | custom fusion | bytes 25166592 | tf_op jit(solution)/shard_map/gather | solution.py:20
  409.8 15.2 %convolution_bitcast_fusion = f32[192,128,256]{1,2,0:T(8,128)} fusion(bf16[192,128,256]{2,1,0:T(8,128)(2,1)} %gather_fusion.1, bf16[1,1,192,128,128]{4,3,2,1,0:T(8,128)(2,1)} %param.11), kind=kOutput, calls=%fused_computation.6 | convolution fusion | flops 1610612736 | bytes 44040192 | tf_op jit(solution)/shard_map/sbk,sbf->skf/dot_general | solution.py:21
  425.0 24.7 %copy.18 = f32[192,128,256]{2,1,0:T(8,128)} copy(f32[192,128,256]{1,2,0:T(8,128)} %convolution_bitcast_fusion) | data formatting | bytes 50331648 | tf_op jit(solution)/shard_map/sbk,sbf->skf/dot_general | solution.py:21
  449.6 7.9 %broadcast_in_dim.18 = f32[129,128,256]{2,1,0:T(8,128)} broadcast(f32[]{:T(128)} %constant.5.clone.1), dimensions={} | broadcast | bytes 16908292 | tf_op jit(solution)/shard_map/broadcast_in_dim | solution.py:23
  457.5 58.0 %scatter_fusion.1 = f32[129,128,256]{2,1,0:T(8,128)} fusion(f32[129,128,256]{2,1,0:T(8,128)} %broadcast_in_dim.18, s32[192]{0:T(256)S(1)} %bitcast.51, f32[192,128,256]{2,1,0:T(8,128)} %copy.18), kind=kCustom, calls=%fused_computation.3 | custom fusion | flops 6291456 | bytes 75498240 | tf_op jit(solution)/shard_map/scatter-add | solution.py:23
  515.5 9.1 %slice.18 = bf16[128,128,256]{2,1,0:T(8,128)(2,1)} slice(f32[129,128,256]{2,1,0:T(8,128)} %scatter_fusion.1), slice={[0:128], [0:128], [0:256]} | slice | bytes 16777216 | tf_op jit(solution)/shard_map/slice | solution.py:23
  524.6 0.0 all-reduce.2.cloned.1.call-start
  524.6 68.0 %psum.15 = f32[256]{0:T(256)} all-reduce(f32[256]{0:T(256)S(1)} %get-tuple-element.12), channel_id=1, replica_groups=mesh['row'=16,'col'=8] {'row','col'}, use_global_device_ids=true, to_apply=%region_6.7 | all-reduce | flops 256 | bytes 2048 | tf_op jit(solution)/shard_map/psum | solution.py:64
  592.6 37.1 %reduce-scatter.5.cloned.1.call-done = bf16[1024,256]{1,0:T(8,128)(2,1)} async-done(((bf16[16384,256]{1,0:T(8,128)(2,1)}), bf16[1024,256]{1,0:T(8,128)(2,1)}) %reduce-scatter.5.cloned.1.call-update) | async-done | bytes 524304 | tf_op jit(solution)/shard_map/reduce_scatter | solution.py:54
  629.8 2.1 convolution_bitcast_fusion.2
  631.9 2.2 fusion.3
  634.0 142.4 %all-reduce.2.cloned.1.call-done = f32[256,256]{0,1:T(8,128)} async-done(((f32[256,256]{0,1:T(8,128)}), f32[256,256]{0,1:T(8,128)}) %all-reduce.2.cloned.1.call-update) | async-done | bytes 262160 | tf_op jit(solution)/shard_map/psum | solution.py:64
  776.5 1.8 copy.19
  (12 shorter events, 0.1 us)
Async XLA Ops:
  7.2 79.7 %copy-start = (bf16[256,256]{1,0:T(8,128)(2,1)S(1)}, bf16[256,256]{1,0:T(8,128)(2,1)}, u32[]{:S(2)}) copy-start(bf16[256,256]{1,0:T(8,128)(2,1)} %param.9) | copy-start | bytes 393220
  7.2 79.7 %all-gather.6.cloned.1.call-start = ((), (), s32[]{:S(2)}) async-start(), calls=%async_computation.6 | async-start | bytes 8912896 | tf_op jit(solution)/shard_map/all_gather | solution.py:38
  7.9 298.1 %reduce-scatter.3.cloned.1.call-start = ((), (), s32[]{:S(2)}) async-start(), calls=%async_computation.2 | async-start | bytes 4718592 | tf_op jit(solution)/shard_map/reduce_scatter | solution.py:43
  207.5 98.5 %copy-start.2 = (bf16[1,1,1024,256]{3,2,1,0:T(8,128)(2,1)S(1)}, bf16[1,1,1024,256]{3,2,1,0:T(8,128)(2,1)}, u32[]{:S(2)}) copy-start(bf16[1,1,1024,256]{3,2,1,0:T(8,128)(2,1)} %param.15) | copy-start | bytes 1572868
  207.5 98.5 %copy-start.3 = (f32[256]{0:T(256)S(1)}, f32[256]{0:T(256)}, u32[]{:S(2)}) copy-start(f32[256]{0:T(256)} %param.10) | copy-start | bytes 3076
  213.5 185.8 %all-gather.4.cloned.1.call-start = ((), (), s32[]{:S(2)}) async-start(), calls=%async_computation.3 | async-start | bytes 4718592 | tf_op jit(solution)/shard_map/all_gather | solution.py:52
  308.5 321.2 %reduce-scatter.5.cloned.1.call-start = ((), (), s32[]{:S(2)}) async-start(), calls=%async_computation.4 | async-start | bytes 8912896 | tf_op jit(solution)/shard_map/reduce_scatter | solution.py:54
  515.5 114.3 %copy-start.1 = (bf16[1,1,1024,256]{3,2,1,0:T(8,128)(2,1)S(1)}, bf16[1,1,1024,256]{3,2,1,0:T(8,128)(2,1)}, u32[]{:S(2)}) copy-start(bf16[1,1,1024,256]{3,2,1,0:T(8,128)(2,1)} %param.8) | copy-start | bytes 1572868
  524.6 251.9 %all-reduce.2.cloned.1.call-start = ((), (), s32[]{:S(2)}) async-start(), calls=%async_computation.5 | async-start | bytes 524288 | tf_op jit(solution)/shard_map/psum | solution.py:64
Sparse Core Ops, SparseCore 0:
  10.5 76.3 all-gather.5
  213.7 92.2 reduce-scatter.2
  308.7 90.6 all-gather.3
  524.7 104.9 reduce-scatter.4
  634.9 141.4 all-reduce.1
where the time goes:
time: 786 us; the launch traced here: 785 us
  waiting for transfers between devices  441 us (56%)
  other arithmetic  119 us (15%)
  local copies, waits for them, and re-layouts  100 us (13%)
  blocking collectives  68 us (9%)
  matrix products  42.1 us (5%)
  between operations  14.5 us (2%)
    psum x1, waiting for transfers between devices, local(): grad_weight, grad_bias = lax.psum((weight_term, bias_term), ('row', 'col'))  142 us
    reduce_scatter x1, waiting for transfers between devices, local(): lax.psum_scatter(cell_sum.astype(jnp.bfloat16), 'col', scatter_dimension=...  92.4 us
    all_gather x1, waiting for transfers between devices, local(): row_table = lax.all_gather(grad_pre, 'col', axis=0, tiled=True)  90.6 us
    all_gather x1, waiting for transfers between devices, local(): column_input = lax.all_gather(own_input, 'row', axis=0, tiled=True)  77.6 us
    psum x1, blocking collectives, local(): grad_weight, grad_bias = lax.psum((weight_term, bias_term), ('row', 'col'))  68 us
    scatter-add x1, other arithmetic, cell_backward(): jax.ops.segment_sum(contrib, targets, num_segments=col_count + 1)  58 us
    scatter-add x1, other arithmetic, cell_forward(): jax.ops.segment_sum(contrib, targets, num_segments=row_count + 1)  57.3 us
    reduce_scatter x1, waiting for transfers between devices, local(): lax.psum_scatter(cell_back.astype(jnp.bfloat16), 'row', scatter_dimension...  37.1 us
  transfers between devices with their start and end apart: 5, of which 5 were waited for; matrix products, arithmetic and copies ran while one was open for 0% of the time, Pallas kernels for 0%

commit v1 on v0

v1 whole, which is shorter than its diff:
```python
import functools

import jax
import jax.numpy as jnp
from jax import lax
from jax.experimental import pallas as pl
from jax.experimental.pallas import tpu as pltpu
from jax.sharding import PartitionSpec as P

BLK = 128
UNROLL = 8
CHUNK = 16


def row_index(zh, x, c):
    return zh * 8 + x * 2 + c


def row_perm(move):
    return [
        (row_index(zh, x, c), row_index(*move(zh, x, c)))
        for zh in range(2)
        for x in range(4)
        for c in range(2)
    ]


def col_perm(move):
    def index(zl, y):
        return y * 2 + zl

    return [(index(zl, y), index(*move(zl, y))) for zl in range(2) for y in range(4)]


ROW_RING = {d: row_perm(lambda zh, x, c, d=d: (zh, (x + d) % 4, c)) for d in (1, 2, 3)}
ROW_PAIR = row_perm(lambda zh, x, c: (1 - zh, x, c))
ROW_CORE = row_perm(lambda zh, x, c: (zh, x, 1 - c))
COL_RING = {d: col_perm(lambda zl, y, d=d: (zl, (y + d) % 4)) for d in (1, 2, 3)}
COL_PAIR = col_perm(lambda zl, y: (1 - zl, y))


def gather(own, axis, ring, pair):
    def go(v, perm):
        return lax.ppermute(v, axis, perm)

    got = {(0, 0): own}
    got[1, 0] = go(own, pair)
    got[0, 3] = go(own, ring[1])
    got[0, 1] = go(own, ring[3])
    got[0, 2] = go(own, ring[2])
    got[1, 3] = go(got[1, 0], ring[1])
    got[1, 1] = go(got[1, 0], ring[3])
    got[1, 2] = go(got[0, 2], pair)
    return got


def scatter(parts, axis, ring, pair):
    def go(v, perm):
        return lax.ppermute(v.astype(jnp.bfloat16), axis, perm).astype(jnp.float32)

    up = go(parts(1, 1), ring[1])
    down = go(parts(1, 3), ring[3])
    far = go(parts(1, 2), pair)
    up_own = go(parts(0, 1), ring[1])
    down_own = go(parts(0, 3), ring[3])
    across = go(parts(1, 0) + up + down, pair)
    far_own = go(parts(0, 2) + far, ring[2])
    return parts(0, 0) + up_own + down_own + across + far_own


def sparse_kernel(transpose, n_in, n_out, rows, cols, count, adj, *refs):
    pieces = refs[:n_in]
    outs = refs[n_in : n_in + n_out]
    table, acc, blocks, piece_sem, block_sem = refs[n_in + n_out :]
    n_slots = adj.shape[0]
    n_chunks = n_slots // CHUNK
    piece_rows = pieces[0].shape[0]
    piece_copies = [
        pltpu.make_async_copy(
            pieces[i], table.at[pl.ds(i * piece_rows, piece_rows)], piece_sem.at[i]
        )
        for i in range(n_in)
    ]
    block_copies = [
        pltpu.make_async_copy(
            adj.at[pl.ds(i * CHUNK, CHUNK)], blocks.at[pl.ds(i * CHUNK, CHUNK)], block_sem.at[i]
        )
        for i in range(n_chunks)
    ]
    for copy in piece_copies + block_copies:
        copy.start()
    live = count[0]

    @pl.loop(0, acc.shape[0] // 256)
    def _(i):
        acc[pl.ds(pl.multiple_of(i * 256, 256), 256), :] = jnp.zeros((256, acc.shape[1]), acc.dtype)

    for copy in piece_copies + block_copies:
        copy.wait()

    @pl.loop(0, live // UNROLL)
    def _(step):
        base = step * UNROLL
        for u in range(UNROLL):
            slot = base + u
            a = blocks[slot]
            out_at = pl.multiple_of(rows[slot] * BLK, BLK)
            in_at = pl.multiple_of(cols[slot] * BLK, BLK)
            t = table[pl.ds(in_at, BLK), :]
            dims = (((0,), (0,)), ((), ())) if transpose else (((1,), (0,)), ((), ()))
            prod = lax.dot_general(a, t, dims, preferred_element_type=jnp.float32)
            acc[pl.ds(out_at, BLK), :] += prod

    for i, out in enumerate(outs):

        @pl.loop(0, piece_rows // 128)
        def _(j):
            at = pl.multiple_of(j * 128, 128)
            out[pl.ds(at, 128), :] = acc[pl.ds(i * piece_rows + at, 128), :].astype(out.dtype)


def sparse(transpose, rows, cols, count, adj, pieces, n_out):
    n_in = len(pieces)
    piece_rows, width = pieces[0].shape
    n_slots = adj.shape[0]
    out_shape = [jax.ShapeDtypeStruct((piece_rows, width), jnp.bfloat16)] * n_out
    return pl.pallas_call(
        functools.partial(sparse_kernel, transpose, n_in, n_out),
        out_shape=out_shape,
        in_specs=[pl.BlockSpec(memory_space=pltpu.SMEM)] * 3
        + [pl.BlockSpec(memory_space=pl.ANY)] * (1 + n_in),
        out_specs=[pl.BlockSpec(memory_space=pltpu.VMEM)] * n_out,
        scratch_shapes=[
            pltpu.VMEM((n_in * piece_rows, width), jnp.bfloat16),
            pltpu.VMEM((n_out * piece_rows, width), jnp.float32),
            pltpu.VMEM((n_slots, BLK, BLK), jnp.bfloat16),
            pltpu.SemaphoreType.DMA((n_in,)),
            pltpu.SemaphoreType.DMA((n_slots // CHUNK,)),
        ],
        compiler_params=pltpu.CompilerParams(vmem_limit_bytes=48 * 1024 * 1024),
        cost_estimate=pl.CostEstimate(
            flops=2 * n_slots * BLK * BLK * width,
            bytes_accessed=n_slots * BLK * BLK * 2 + (n_in + n_out) * piece_rows * width * 2,
            transcendentals=0,
        ),
        name="sparse_back" if transpose else "sparse_forward",
    )(rows, cols, count, adj, *pieces)


def all_sum(v):
    half = v.shape[0] // 2
    core = lax.axis_index("row") % 2
    v = v + lax.ppermute(v, "row", ROW_CORE)
    part = lax.dynamic_slice_in_dim(v, core * half, half, 0)
    part = part + lax.ppermute(part, "row", ROW_PAIR)
    for bit in (1, 2):
        part = part + lax.ppermute(part, "row", row_perm(lambda zh, x, c: (zh, x ^ bit, c)))
    part = part + lax.ppermute(part, "col", COL_PAIR)
    for bit in (1, 2):
        part = part + lax.ppermute(part, "col", col_perm(lambda zl, y: (zl, y ^ bit)))
    other = lax.ppermute(part, "row", ROW_CORE)
    first = jnp.where(core == 0, part, other)
    second = jnp.where(core == 0, other, part)
    return jnp.concatenate([first, second], axis=0)


def local(node_features, weight, bias, adj_blocks, block_row, block_col, slot_count, cotangent):
    node_rows, width = node_features.shape[2:]
    per = node_rows // BLK
    adj = adj_blocks[0, 0]
    count = slot_count[0]
    me_row = lax.axis_index("row")
    me_col = lax.axis_index("col")
    zh, x, c = me_row // 8, (me_row // 2) % 4, me_row % 2
    y, zl = me_col // 2, me_col % 2

    owner = block_col[0, 0] // per
    rel_c = (owner % 2) ^ c
    rel_x = ((owner // 2) % 4 - x) % 4
    rel_zh = (owner // 8) ^ zh
    in_ids = (rel_c * 8 + rel_zh * 4 + rel_x) * per + block_col[0, 0] % per
    owner = block_row[0, 0] // per
    rel_zl = (owner % 2) ^ zl
    rel_y = (owner // 2 - y) % 4
    out_ids = (rel_zl * 4 + rel_y) * per + block_row[0, 0] % per

    own_input = node_features[0, 0]
    got = gather(own_input, "row", ROW_RING, ROW_PAIR)
    mine = [got[p, r] for p in range(2) for r in range(4)]
    swapped = {k: lax.ppermute(v, "row", ROW_CORE) for k, v in got.items()}
    theirs = [swapped[p, r] for p in range(2) for r in range(4)]
    sums = sparse(False, out_ids, in_ids, count, adj, mine + theirs, 8)
    aggregate = scatter(
        lambda p, r: sums[p * 4 + r].astype(jnp.float32), "col", COL_RING, COL_PAIR
    ).astype(jnp.bfloat16)

    pre = jnp.dot(aggregate, weight, preferred_element_type=jnp.float32) + bias
    sigma = jax.nn.sigmoid(pre)
    layer_out = (pre * sigma).astype(jnp.bfloat16)
    grad_pre = (cotangent[0, 0].astype(jnp.float32) * sigma * (1.0 + pre * (1.0 - sigma))).astype(
        jnp.bfloat16
    )

    got = gather(grad_pre, "col", COL_RING, COL_PAIR)
    pieces = [got[p, r] for p in range(2) for r in range(4)]
    weight_term = lax.dot_general(
        aggregate, grad_pre, (((0,), (0,)), ((), ())), preferred_element_type=jnp.float32
    )
    bias_term = jnp.sum(grad_pre.astype(jnp.float32), axis=0)
    both = jnp.concatenate(
        [weight_term, bias_term[None], jnp.zeros((15, width), jnp.float32)], axis=0
    )
    total = all_sum(both)

    backs = sparse(True, in_ids, out_ids, count, adj, pieces, 16)

    def summed(p, r):
        k = p * 4 + r
        other = lax.ppermute(backs[8 + k], "row", ROW_CORE)
        return backs[k].astype(jnp.float32) + other.astype(jnp.float32)

    grad_projected = scatter(summed, "row", ROW_RING, ROW_PAIR).astype(jnp.bfloat16)
    grad_input = lax.dot_general(
        grad_projected, weight, (((1,), (1,)), ((), ())), preferred_element_type=jnp.float32
    ).astype(jnp.bfloat16)
    return (
        layer_out.reshape(1, 1, node_rows, width),
        grad_input.reshape(1, 1, node_rows, width),
        total[:width],
        total[width],
    )


def solution(mesh):
    placed = (
        P("col", "row", None, None),
        P(),
        P(),
        P("row", "col", None, None, None),
        P("row", "col", None),
        P("row", "col", None),
        P("row", "col"),
        P("row", "col", None, None),
    )
    return jax.shard_map(
        local,
        mesh=mesh,
        in_specs=placed,
        out_specs=(P("row", "col", None, None), P("col", "row", None, None), P(), P()),
        check_vma=False,
    )
```

time: 786 us -> 233 us (0.30)
  waiting for transfers between devices: 441 us -> 127 us
  other arithmetic: 119 us -> 3.73 us
  local copies, waits for them, and re-layouts: 100 us -> 2.82 us
  starting transfers between devices: 0.38 us -> 72.1 us
  blocking collectives: 68 us -> 0 us
  matrix products: 42.1 us -> 4.82 us
  Pallas kernels: 0 us -> 19 us
  between operations: 14.5 us -> 1.69 us
    all_gather x2 -> x0, waiting for transfers between devices: 168 us -> none  [the longest x1 90.6 us: local(): row_table = lax.all_gather(grad_pre, 'col', axis=0, tiled=True)]
    psum x1 -> x0, waiting for transfers between devices: 142 us -> none  [local(): grad_weight, grad_bias = lax.psum((weight_term, bias_term), ('row', 'col'))]
    reduce_scatter x2 -> x0, waiting for transfers between devices: 130 us -> none  [the longest x1 92.4 us: local(): lax.psum_scatter(cell_sum.astype(jnp.bfloat16), 'col', scatter_dimension=...]
    ppermute x0 -> x52, waiting for transfers between devices: none -> 127 us  [the longest x14 50.5 us: go(): return lax.ppermute(v, axis, perm)]
    scatter-add x2 -> x0, other arithmetic: 115 us -> none  [the longest x1 58 us: cell_backward(): jax.ops.segment_sum(contrib, targets, num_segments=col_count + 1)]
    ppermute x0 -> x52, starting transfers between devices: none -> 72.1 us  [the longest x14 23.8 us: go(): return lax.ppermute(v.astype(jnp.bfloat16), axis, perm).astype(jnp.float32)]
    psum x1 -> x0, blocking collectives: 68 us -> none  [local(): grad_weight, grad_bias = lax.psum((weight_term, bias_term), ('row', 'col'))]
    dot_general x2 -> x0, local copies, waits for them, and re-layouts: 49.3 us -> none  [the longest x1 24.7 us: cell_forward(): jnp.einsum('sbk,skf->sbf', blocks, picked, preferred_element_type=jnp.flo...]
  transfers between devices with their start and end apart: 5 -> 52, of which waited for: 5 -> 23; matrix products, arithmetic and copies ran while one was open for 0% -> 2% of each run, Pallas kernels for 0% -> 4%
where the time goes in v1:
time: 233 us; the launch traced here: 232 us
  waiting for transfers between devices  127 us (55%)
  starting transfers between devices  72.1 us (31%)
  Pallas kernels  19 us (8%)
  matrix products  4.82 us (2%)
  other arithmetic  3.73 us (2%)
  local copies, waits for them, and re-layouts  2.82 us (1%)
    ppermute x14, waiting for transfers between devices, go(): return lax.ppermute(v, axis, perm)  50.5 us
    ppermute x14, waiting for transfers between devices, go(): return lax.ppermute(v.astype(jnp.bfloat16), axis, perm).astype(jnp.float32)  47.2 us
    ppermute x14, starting transfers between devices, go(): return lax.ppermute(v.astype(jnp.bfloat16), axis, perm).astype(jnp.float32)  23.8 us
    ppermute x14, starting transfers between devices, go(): return lax.ppermute(v, axis, perm)  20.3 us
    pallas_call x2, Pallas kernels, sparse(): pl.pallas_call(functools.partial(sparse_kernel, transpose, n_in, n_out),...  19 us
    ppermute x1, waiting for transfers between devices, all_sum(): part = part + lax.ppermute(part, 'row', ROW_PAIR)  14.9 us
    ppermute x8, starting transfers between devices, summed(): other = lax.ppermute(backs[8 + k], 'row', ROW_CORE)  14.5 us
    ppermute x2, waiting for transfers between devices, all_sum(): lax.ppermute(part, 'col', col_perm(lambda zl, y: (zl, y ^ bit)))  7.02 us
  transfers between devices with their start and end apart: 52, of which 23 were waited for; matrix products, arithmetic and copies ran while one was open for 2% of the time, Pallas kernels for 4%

profile of v1, /device:TPU:1, one launch (start us, length us, event | category | flops | bytes accessed | tf_op | source)
XLA Modules:
  0.0 231.7 jit_solution(8657088664944753918)
XLA Ops:
  0.6 4.5 %collective-permute-start.3 = (bf16[1024,256]{1,0:T(8,128)(2,1)}, bf16[1024,256]{1,0:T(8,128)(2,1)S(1)}, u32[]{:S(2)}, u32[]{:S(2)}) collective-permute-start(bf16[1024,256]{1,0:T(8,128)(2,1)} %bitcast.22), channel_id=1, source_target_pairs={{0,64},{8,72},{16,80},{24,88},{32,96},{40,104},{48,112},{56,120},{... | collective-permute-start | bytes 1572872 | tf_op jit(solution)/shard_map/ppermute | solution.py:44
  7.3 2.5 %collective-permute-start.1 = (bf16[1024,256]{1,0:T(8,128)(2,1)}, bf16[1024,256]{1,0:T(8,128)(2,1)S(1)}, u32[]{:S(2)}, u32[]{:S(2)}) collective-permute-start(bf16[1024,256]{1,0:T(8,128)(2,1)} %bitcast.25), channel_id=1, source_target_pairs={{0,32},{8,40},{16,48},{24,56},{32,0},{40,8},{48,16},{56,24},{64,96... | collective-permute-start | bytes 1572872 | tf_op jit(solution)/shard_map/ppermute | solution.py:44
  10.9 6.1 %collective-permute-done.3.refs_4_ = bf16[1024,256]{1,0:T(8,128)(2,1)S(1)} collective-permute-done((bf16[1024,256]{1,0:T(8,128)(2,1)}, bf16[1024,256]{1,0:T(8,128)(2,1)S(1)}, u32[]{:S(2)}, u32[]{:S(2)}) %collective-permute-start.3) | collective-permute-done | bytes 524320 | tf_op jit(solution)/shard_map/ppermute | solution.py:44
  22.4 11.0 %collective-permute-done.1.refs_2_ = bf16[1024,256]{1,0:T(8,128)(2,1)S(1)} collective-permute-done((bf16[1024,256]{1,0:T(8,128)(2,1)}, bf16[1024,256]{1,0:T(8,128)(2,1)S(1)}, u32[]{:S(2)}, u32[]{:S(2)}) %collective-permute-start.1) | collective-permute-done | bytes 524320 | tf_op jit(solution)/shard_map/ppermute | solution.py:44
  34.7 9.7 %collective-permute-done.6.refs_7_ = bf16[1024,256]{1,0:T(8,128)(2,1)} collective-permute-done((bf16[1024,256]{1,0:T(8,128)(2,1)S(1)}, bf16[1024,256]{1,0:T(8,128)(2,1)}, u32[]{:S(2)}, u32[]{:S(2)}) %collective-permute-start.6) | collective-permute-done | bytes 524320 | tf_op jit(solution)/shard_map/ppermute | solution.py:44
  45.6 4.1 %collective-permute-done.5.refs_6_ = bf16[1024,256]{1,0:T(8,128)(2,1)} collective-permute-done((bf16[1024,256]{1,0:T(8,128)(2,1)S(1)}, bf16[1024,256]{1,0:T(8,128)(2,1)}, u32[]{:S(2)}, u32[]{:S(2)}) %collective-permute-start.5) | collective-permute-done | bytes 524320 | tf_op jit(solution)/shard_map/ppermute | solution.py:44
  53.4 8.7 %sparse_forward.1 = (bf16[1024,256]{1,0:T(8,128)(2,1)S(1)}, bf16[1024,256]{1,0:T(8,128)(2,1)S(1)}, bf16[1024,256]{1,0:T(8,128)(2,1)S(1)}, bf16[1024,256]{1,0:T(8...) custom-call(s32[192]{0:T(256)S(1)} %get-tuple-element.57.rows.cols, ...), custom_call_target="tpu_custom_call" | custom-call | flops 1610612736 | bytes 18874368 | tf_op jit(solution)/shard_map/sparse_forward/pallas_call | solution.py:127
  62.2 2.6 %collective-permute-start.17 = (bf16[1024,256]{1,0:T(8,128)(2,1)S(1)}, bf16[1024,256]{1,0:T(8,128)(2,1)S(1)}, u32[]{:S(2)}, u32[]{:S(2)}) collective-permute-start(bf16[1024,256]{1,0:T(8,128)(2,1)S(1)} %get-tuple-element.32), channel_id=1, source_target_pairs={{0,2},{2,4},{4,6},{6,0},{1,3},{3,5},{5,7},{7,1},{8,10},{10,12},{12... | collective-permute-start | bytes 1572872 | tf_op jit(solution)/shard_map/ppermute | solution.py:59
  64.9 4.1 %collective-permute-start.20 = (bf16[1024,256]{1,0:T(8,128)(2,1)S(1)}, bf16[1024,256]{1,0:T(8,128)(2,1)S(1)}, u32[]{:S(2)}, u32[]{:S(2)}) collective-permute-start(bf16[1024,256]{1,0:T(8,128)(2,1)S(1)} %get-tuple-element.35), channel_id=1, source_target_pairs={{0,1},{2,3},{4,5},{6,7},{1,0},{3,2},{5,4},{7,6},{8,9},{10,11},{12,... | collective-permute-start | bytes 1572872 | tf_op jit(solution)/shard_map/ppermute | solution.py:59
  73.5 1.8 collective-permute-done.18
  75.6 7.7 %collective-permute-start.19 = (bf16[1024,256]{1,0:T(8,128)(2,1)S(1)}, bf16[1024,256]{1,0:T(8,128)(2,1)S(1)}, u32[]{:S(2)}, u32[]{:S(2)}) collective-permute-start(bf16[1024,256]{1,0:T(8,128)(2,1)S(1)} %add_convert_fusion.10), channel_id=1, source_target_pairs={{0,1},{2,3},{4,5},{6,7},{1,0},{3,2},{5,4},{7,6},{8,9},{10,11},{12,... | collective-permute-start | bytes 1572872 | tf_op jit(solution)/shard_map/ppermute | solution.py:59
  84.8 1.8 collective-permute-done.16
  86.6 8.0 %collective-permute-done.19 = bf16[1024,256]{1,0:T(8,128)(2,1)S(1)} collective-permute-done((bf16[1024,256]{1,0:T(8,128)(2,1)S(1)}, bf16[1024,256]{1,0:T(8,128)(2,1)S(1)}, u32[]{:S(2)}, u32[]{:S(2)}) %collective-permute-start.19) | collective-permute-done | bytes 524320 | tf_op jit(solution)/shard_map/ppermute | solution.py:59
  94.6 4.5 %collective-permute-done.21 = bf16[1024,256]{1,0:T(8,128)(2,1)S(1)} collective-permute-done((bf16[1024,256]{1,0:T(8,128)(2,1)S(1)}, bf16[1024,256]{1,0:T(8,128)(2,1)S(1)}, u32[]{:S(2)}, u32[]{:S(2)}) %collective-permute-start.21) | collective-permute-done | bytes 524320 | tf_op jit(solution)/shard_map/ppermute | solution.py:59
  101.4 1.9 collective-permute-start.44
  104.0 2.4 %collective-permute-start.23 = (bf16[1024,256]{1,0:T(8,128)(2,1)S(1)}, bf16[1024,256]{1,0:T(8,128)(2,1)S(1)}, u32[]{:S(2)}, u32[]{:S(2)}) collective-permute-start(bf16[1024,256]{1,0:T(8,128)(2,1)S(1)} %get-tuple-element.53.refs_0_), channel_id=1, source_target_pairs={{0,4},{2,6},{4,0},{6,2},{1,5},{3,7},{5,1},{7,3},{8,12},{10,14},{12... | collective-permute-start | bytes 1572872 | tf_op jit(solution)/shard_map/ppermute | solution.py:44
  106.4 3.0 %collective-permute-start.45 = (f32[136,256]{1,0:T(8,128)S(1)}, f32[136,256]{1,0:T(8,128)S(1)}, u32[]{:S(2)}, u32[]{:S(2)}) collective-permute-start(f32[136,256]{1,0:T(8,128)S(1)} %dynamic-slice_add_fusion), channel_id=1, source_target_pairs={{0,64},{8,72},{16,80},{24,88},{32,96},{40,104},{48,112},{56,120},{... | collective-permute-start | bytes 417800 | tf_op jit(solution)/shard_map/ppermute | solution.py:155
  109.4 14.9 %collective-permute-done.45 = f32[136,256]{1,0:T(8,128)S(1)} collective-permute-done((f32[136,256]{1,0:T(8,128)S(1)}, f32[136,256]{1,0:T(8,128)S(1)}, u32[]{:S(2)}, u32[]{:S(2)}) %collective-permute-start.45) | collective-permute-done | bytes 139296 | tf_op jit(solution)/shard_map/ppermute | solution.py:155
  127.2 2.7 %collective-permute-start.26 = (bf16[1024,256]{1,0:T(8,128)(2,1)S(1)}, bf16[1024,256]{1,0:T(8,128)(2,1)S(1)}, u32[]{:S(2)}, u32[]{:S(2)}) collective-permute-start(bf16[1024,256]{1,0:T(8,128)(2,1)S(1)} %collective-permute-done.25.refs_4_), channel_id=1, source_target_pairs={{0,6},{2,0},{4,2},{6,4},{1,7},{3,1},{5,3},{7,5},{8,14},{10,8},{12,... | collective-permute-start | bytes 1572872 | tf_op jit(solution)/shard_map/ppermute | solution.py:44
  129.9 8.4 %collective-permute-done.24.refs_3_ = bf16[1024,256]{1,0:T(8,128)(2,1)S(1)} collective-permute-done((bf16[1024,256]{1,0:T(8,128)(2,1)S(1)}, bf16[1024,256]{1,0:T(8,128)(2,1)S(1)}, u32[]{:S(2)}, u32[]{:S(2)}) %collective-permute-start.24) | collective-permute-done | bytes 524320 | tf_op jit(solution)/shard_map/ppermute | solution.py:44
  139.9 9.6 %collective-permute-done.28.refs_7_ = bf16[1024,256]{1,0:T(8,128)(2,1)S(1)} collective-permute-done((bf16[1024,256]{1,0:T(8,128)(2,1)S(1)}, bf16[1024,256]{1,0:T(8,128)(2,1)S(1)}, u32[]{:S(2)}, u32[]{:S(2)}) %collective-permute-start.28) | collective-permute-done | bytes 524320 | tf_op jit(solution)/shard_map/ppermute | solution.py:44
  150.6 10.3 %sparse_back.1 = (bf16[1024,256]{1,0:T(8,128)(2,1)S(1)}, bf16[1024,256]{1,0:T(8,128)(2,1)S(1)}, bf16[1024,256]{1,0:T(8,128)(2,1)S(1)}, bf16[1024,256]{1,0:T(8,12...) custom-call(s32[192]{0:T(256)S(1)} %get-tuple-element.58.cols.rows, ...), custom_call_target="tpu_custom_call" | custom-call | flops 1610612736 | bytes 18874368 | tf_op jit(solution)/shard_map/sparse_back/pallas_call | solution.py:127
  161.0 7.2 %collective-permute-start.30 = (bf16[1024,256]{1,0:T(8,128)(2,1)S(1)}, bf16[1024,256]{1,0:T(8,128)(2,1)S(1)}, u32[]{:S(2)}, u32[]{:S(2)}) collective-permute-start(bf16[1024,256]{1,0:T(8,128)(2,1)S(1)} %get-tuple-element.39), channel_id=1, source_target_pairs={{0,8},{8,0},{16,24},{24,16},{32,40},{40,32},{48,56},{56,48},{64,72... | collective-permute-start | bytes 1572872 | tf_op jit(solution)/shard_map/ppermute | solution.py:219
  168.3 5.3 %collective-permute-done.48 = f32[136,256]{1,0:T(8,128)S(1)} collective-permute-done((f32[136,256]{1,0:T(8,128)S(1)}, f32[136,256]{1,0:T(8,128)S(1)}, u32[]{:S(2)}, u32[]{:S(2)}) %collective-permute-start.48) | collective-permute-done | bytes 139296 | tf_op jit(solution)/shard_map/ppermute | solution.py:158
  174.6 3.5 %collective-permute-done.49 = f32[136,256]{1,0:T(8,128)S(1)} collective-permute-done((f32[136,256]{1,0:T(8,128)S(1)}, f32[136,256]{1,0:T(8,128)S(1)}, u32[]{:S(2)}, u32[]{:S(2)}) %collective-permute-start.49) | collective-permute-done | bytes 139296 | tf_op jit(solution)/shard_map/ppermute | solution.py:160
  180.1 3.5 %collective-permute-done.50 = f32[136,256]{1,0:T(8,128)S(1)} collective-permute-done((f32[136,256]{1,0:T(8,128)S(1)}, f32[136,256]{1,0:T(8,128)S(1)}, u32[]{:S(2)}, u32[]{:S(2)}) %collective-permute-start.50) | collective-permute-done | bytes 139296 | tf_op jit(solution)/shard_map/ppermute | solution.py:160
  183.6 2.8 %collective-permute-start.37 = (bf16[1024,256]{1,0:T(8,128)(2,1)}, bf16[1024,256]{1,0:T(8,128)(2,1)S(1)}, u32[]{:S(2)}, u32[]{:S(2)}) collective-permute-start(bf16[1024,256]{1,0:T(8,128)(2,1)} %get-tuple-element.47), channel_id=1, source_target_pairs={{0,8},{8,0},{16,24},{24,16},{32,40},{40,32},{48,56},{56,48},{64,72... | collective-permute-start | bytes 1572872 | tf_op jit(solution)/shard_map/ppermute | solution.py:219
  193.3 9.3 %collective-permute-done.36 = bf16[1024,256]{1,0:T(8,128)(2,1)S(1)} collective-permute-done((bf16[1024,256]{1,0:T(8,128)(2,1)S(1)}, bf16[1024,256]{1,0:T(8,128)(2,1)S(1)}, u32[]{:S(2)}, u32[]{:S(2)}) %collective-permute-start.36) | collective-permute-done | bytes 524320 | tf_op jit(solution)/shard_map/ppermute | solution.py:59
  204.1 2.7 %collective-permute-start.33 = (bf16[1024,256]{1,0:T(8,128)(2,1)S(1)}, bf16[1024,256]{1,0:T(8,128)(2,1)}, u32[]{:S(2)}, u32[]{:S(2)}) collective-permute-start(bf16[1024,256]{1,0:T(8,128)(2,1)S(1)} %add_convert_fusion.6), channel_id=1, source_target_pairs={{0,48},{8,56},{16,0},{24,8},{32,16},{40,24},{48,32},{56,40},{64,11... | collective-permute-start | bytes 1572872 | tf_op jit(solution)/shard_map/ppermute | solution.py:59
  209.5 10.3 %collective-permute-done.31 = bf16[1024,256]{1,0:T(8,128)(2,1)} collective-permute-done((bf16[1024,256]{1,0:T(8,128)(2,1)S(1)}, bf16[1024,256]{1,0:T(8,128)(2,1)}, u32[]{:S(2)}, u32[]{:S(2)}) %collective-permute-start.31) | collective-permute-done | bytes 524320 | tf_op jit(solution)/shard_map/ppermute | solution.py:59
  219.8 8.9 %collective-permute-done.33 = bf16[1024,256]{1,0:T(8,128)(2,1)} collective-permute-done((bf16[1024,256]{1,0:T(8,128)(2,1)S(1)}, bf16[1024,256]{1,0:T(8,128)(2,1)}, u32[]{:S(2)}, u32[]{:S(2)}) %collective-permute-start.33) | collective-permute-done | bytes 524320 | tf_op jit(solution)/shard_map/ppermute | solution.py:59
  228.6 3.0 %fusion = bf16[1,1,1024,256]{3,2,1,0:T(8,128)(2,1)} fusion(bf16[256,256]{1,0:T(8,128)(2,1)S(1)} %copy-done, bf16[1024,256]{1,0:T(8,128)(2,1)} %collective-permute-done.43, bf16[1024,256]{1,0:T(8,128)(2,1)} %collective-permute-done.39, bf16[1024,256]{1,0:T(8,128)(2,1)} %collective-permute-done.33, bf16[1024,256]{1,0:T(8,128)(2,1)} %collective-permute-done.31, ...), kind=kOutput, calls=%fused_computation.2 | convolution fusion | flops 137625600 | bytes 3801088 | tf_op jit(solution)/shard_map/dot_general | solution.py:223
  (135 shorter events, 43.2 us)
Async XLA Ops:
  0.6 16.4 %collective-permute-start.3 = (bf16[1024,256]{1,0:T(8,128)(2,1)}, bf16[1024,256]{1,0:T(8,128)(2,1)S(1)}, u32[]{:S(2)}, u32[]{:S(2)}) collective-permute-start(bf16[1024,256]{1,0:T(8,128)(2,1)} %bitcast.22), channel_id=1, source_target_pairs={{0,64},{8,72},{16,80},{24,88},{32,96},{40,104},{48,112},{56,120},{... | collective-permute-start | bytes 1572872 | tf_op jit(solution)/shard_map/ppermute | solution.py:44
  6.1 15.0 %collective-permute-start.2 = (bf16[1024,256]{1,0:T(8,128)(2,1)}, bf16[1024,256]{1,0:T(8,128)(2,1)S(1)}, u32[]{:S(2)}, u32[]{:S(2)}) collective-permute-start(bf16[1024,256]{1,0:T(8,128)(2,1)} %bitcast.24), channel_id=1, source_target_pairs={{0,16},{8,24},{16,32},{24,40},{32,48},{40,56},{48,0},{56,8},{64,80... | collective-permute-start | bytes 1572872 | tf_op jit(solution)/shard_map/ppermute | solution.py:44
  7.3 26.0 %collective-permute-start.1 = (bf16[1024,256]{1,0:T(8,128)(2,1)}, bf16[1024,256]{1,0:T(8,128)(2,1)S(1)}, u32[]{:S(2)}, u32[]{:S(2)}) collective-permute-start(bf16[1024,256]{1,0:T(8,128)(2,1)} %bitcast.25), channel_id=1, source_target_pairs={{0,32},{8,40},{16,48},{24,56},{32,0},{40,8},{48,16},{56,24},{64,96... | collective-permute-start | bytes 1572872 | tf_op jit(solution)/shard_map/ppermute | solution.py:44
  9.8 24.7 %collective-permute-start = (bf16[1024,256]{1,0:T(8,128)(2,1)}, bf16[1024,256]{1,0:T(8,128)(2,1)S(1)}, u32[]{:S(2)}, u32[]{:S(2)}) collective-permute-start(bf16[1024,256]{1,0:T(8,128)(2,1)} %bitcast.26), channel_id=1, source_target_pairs={{0,48},{8,56},{16,0},{24,8},{32,16},{40,24},{48,32},{56,40},{64,11... | collective-permute-start | bytes 1572872 | tf_op jit(solution)/shard_map/ppermute | solution.py:44
  17.0 17.5 %collective-permute-start.11 = (bf16[1024,256]{1,0:T(8,128)(2,1)S(1)}, bf16[1024,256]{1,0:T(8,128)(2,1)S(1)}, u32[]{:S(2)}, u32[]{:S(2)}) collective-permute-start(bf16[1024,256]{1,0:T(8,128)(2,1)S(1)} %collective-permute-done.3.refs_4_), channel_id=1, source_target_pairs={{0,8},{8,0},{16,24},{24,16},{32,40},{40,32},{48,56},{56,48},{64,72... | collective-permute-start | bytes 1572872 | tf_op jit(solution)/shard_map/ppermute | solution.py:190
  18.3 26.2 %collective-permute-start.6 = (bf16[1024,256]{1,0:T(8,128)(2,1)S(1)}, bf16[1024,256]{1,0:T(8,128)(2,1)}, u32[]{:S(2)}, u32[]{:S(2)}) collective-permute-start(bf16[1024,256]{1,0:T(8,128)(2,1)S(1)} %collective-permute-done.3.refs_4_), channel_id=1, source_target_pairs={{0,16},{8,24},{16,32},{24,40},{32,48},{40,56},{48,0},{56,8},{64,80... | collective-permute-start | bytes 1572872 | tf_op jit(solution)/shard_map/ppermute | solution.py:44
  21.1 24.0 %collective-permute-start.4 = (bf16[1024,256]{1,0:T(8,128)(2,1)S(1)}, bf16[1024,256]{1,0:T(8,128)(2,1)}, u32[]{:S(2)}, u32[]{:S(2)}) collective-permute-start(bf16[1024,256]{1,0:T(8,128)(2,1)S(1)} %collective-permute-done.3.refs_4_), channel_id=1, source_target_pairs={{0,48},{8,56},{16,0},{24,8},{32,16},{40,24},{48,32},{56,40},{64,11... | collective-permute-start | bytes 1572872 | tf_op jit(solution)/shard_map/ppermute | solution.py:44
  34.5 15.2 %collective-permute-start.5 = (bf16[1024,256]{1,0:T(8,128)(2,1)S(1)}, bf16[1024,256]{1,0:T(8,128)(2,1)}, u32[]{:S(2)}, u32[]{:S(2)}) collective-permute-start(bf16[1024,256]{1,0:T(8,128)(2,1)S(1)} %collective-permute-done.1.refs_2_), channel_id=1, source_target_pairs={{0,64},{8,72},{16,80},{24,88},{32,96},{40,104},{48,112},{56,120},{... | collective-permute-start | bytes 1572872 | tf_op jit(solution)/shard_map/ppermute | solution.py:44
  34.5 17.3 %collective-permute-start.9 = (bf16[1024,256]{1,0:T(8,128)(2,1)S(1)}, bf16[1024,256]{1,0:T(8,128)(2,1)}, u32[]{:S(2)}, u32[]{:S(2)}) collective-permute-start(bf16[1024,256]{1,0:T(8,128)(2,1)S(1)} %collective-permute-done.1.refs_2_), channel_id=1, source_target_pairs={{0,8},{8,0},{16,24},{24,16},{32,40},{40,32},{48,56},{56,48},{64,72... | collective-permute-start | bytes 1572872 | tf_op jit(solution)/shard_map/ppermute | solution.py:190
  64.9 18.5 %collective-permute-start.20 = (bf16[1024,256]{1,0:T(8,128)(2,1)S(1)}, bf16[1024,256]{1,0:T(8,128)(2,1)S(1)}, u32[]{:S(2)}, u32[]{:S(2)}) collective-permute-start(bf16[1024,256]{1,0:T(8,128)(2,1)S(1)} %get-tuple-element.35), channel_id=1, source_target_pairs={{0,1},{2,3},{4,5},{6,7},{1,0},{3,2},{5,4},{7,6},{8,9},{10,11},{12,... | collective-permute-start | bytes 1572872 | tf_op jit(solution)/shard_map/ppermute | solution.py:59
  69.1 15.7 %collective-permute-start.15 = (bf16[1024,256]{1,0:T(8,128)(2,1)S(1)}, bf16[1024,256]{1,0:T(8,128)(2,1)S(1)}, u32[]{:S(2)}, u32[]{:S(2)}) collective-permute-start(bf16[1024,256]{1,0:T(8,128)(2,1)S(1)} %get-tuple-element.29), channel_id=1, source_target_pairs={{0,2},{2,4},{4,6},{6,0},{1,3},{3,5},{5,7},{7,1},{8,10},{10,12},{12... | collective-permute-start | bytes 1572872 | tf_op jit(solution)/shard_map/ppermute | solution.py:59
  70.5 16.1 %collective-permute-start.16 = (bf16[1024,256]{1,0:T(8,128)(2,1)S(1)}, bf16[1024,256]{1,0:T(8,128)(2,1)S(1)}, u32[]{:S(2)}, u32[]{:S(2)}) collective-permute-start(bf16[1024,256]{1,0:T(8,128)(2,1)S(1)} %get-tuple-element.30), channel_id=1, source_target_pairs={{0,6},{2,0},{4,2},{6,4},{1,7},{3,1},{5,3},{7,5},{8,14},{10,8},{12,... | collective-permute-start | bytes 1572872 | tf_op jit(solution)/shard_map/ppermute | solution.py:59
  75.6 19.0 %collective-permute-start.19 = (bf16[1024,256]{1,0:T(8,128)(2,1)S(1)}, bf16[1024,256]{1,0:T(8,128)(2,1)S(1)}, u32[]{:S(2)}, u32[]{:S(2)}) collective-permute-start(bf16[1024,256]{1,0:T(8,128)(2,1)S(1)} %add_convert_fusion.10), channel_id=1, source_target_pairs={{0,1},{2,3},{4,5},{6,7},{1,0},{3,2},{5,4},{7,6},{8,9},{10,11},{12,... | collective-permute-start | bytes 1572872 | tf_op jit(solution)/shard_map/ppermute | solution.py:59
  83.5 15.6 %collective-permute-start.21 = (bf16[1024,256]{1,0:T(8,128)(2,1)S(1)}, bf16[1024,256]{1,0:T(8,128)(2,1)S(1)}, u32[]{:S(2)}, u32[]{:S(2)}) collective-permute-start(bf16[1024,256]{1,0:T(8,128)(2,1)S(1)} %add_convert_fusion.9), channel_id=1, source_target_pairs={{0,4},{2,6},{4,0},{6,2},{1,5},{3,7},{5,1},{7,3},{8,12},{10,14},{12... | collective-permute-start | bytes 1572872 | tf_op jit(solution)/shard_map/ppermute | solution.py:59
  103.3 23.9 %collective-permute-start.25 = (bf16[1024,256]{1,0:T(8,128)(2,1)S(1)}, bf16[1024,256]{1,0:T(8,128)(2,1)S(1)}, u32[]{:S(2)}, u32[]{:S(2)}) collective-permute-start(bf16[1024,256]{1,0:T(8,128)(2,1)S(1)} %get-tuple-element.53.refs_0_), channel_id=1, source_target_pairs={{0,1},{2,3},{4,5},{6,7},{1,0},{3,2},{5,4},{7,6},{8,9},{10,11},{12,... | collective-permute-start | bytes 1572872 | tf_op jit(solution)/shard_map/ppermute | solution.py:44
  104.0 23.1 %collective-permute-start.23 = (bf16[1024,256]{1,0:T(8,128)(2,1)S(1)}, bf16[1024,256]{1,0:T(8,128)(2,1)S(1)}, u32[]{:S(2)}, u32[]{:S(2)}) collective-permute-start(bf16[1024,256]{1,0:T(8,128)(2,1)S(1)} %get-tuple-element.53.refs_0_), channel_id=1, source_target_pairs={{0,4},{2,6},{4,0},{6,2},{1,5},{3,7},{5,1},{7,3},{8,12},{10,14},{12... | collective-permute-start | bytes 1572872 | tf_op jit(solution)/shard_map/ppermute | solution.py:44
  106.4 17.9 %collective-permute-start.45 = (f32[136,256]{1,0:T(8,128)S(1)}, f32[136,256]{1,0:T(8,128)S(1)}, u32[]{:S(2)}, u32[]{:S(2)}) collective-permute-start(f32[136,256]{1,0:T(8,128)S(1)} %dynamic-slice_add_fusion), channel_id=1, source_target_pairs={{0,64},{8,72},{16,80},{24,88},{32,96},{40,104},{48,112},{56,120},{... | collective-permute-start | bytes 417800 | tf_op jit(solution)/shard_map/ppermute | solution.py:155
  125.6 14.3 %collective-permute-start.22 = (bf16[1024,256]{1,0:T(8,128)(2,1)S(1)}, bf16[1024,256]{1,0:T(8,128)(2,1)S(1)}, u32[]{:S(2)}, u32[]{:S(2)}) collective-permute-start(bf16[1024,256]{1,0:T(8,128)(2,1)S(1)} %get-tuple-element.53.refs_0_), channel_id=1, source_target_pairs={{0,6},{2,0},{4,2},{6,4},{1,7},{3,1},{5,3},{7,5},{8,14},{10,8},{12,... | collective-permute-start | bytes 1572872 | tf_op jit(solution)/shard_map/ppermute | solution.py:44
  127.2 22.3 %collective-permute-start.28 = (bf16[1024,256]{1,0:T(8,128)(2,1)S(1)}, bf16[1024,256]{1,0:T(8,128)(2,1)S(1)}, u32[]{:S(2)}, u32[]{:S(2)}) collective-permute-start(bf16[1024,256]{1,0:T(8,128)(2,1)S(1)} %collective-permute-done.25.refs_4_), channel_id=1, source_target_pairs={{0,2},{2,4},{4,6},{6,0},{1,3},{3,5},{5,7},{7,1},{8,10},{10,12},{12... | collective-permute-start | bytes 1572872 | tf_op jit(solution)/shard_map/ppermute | solution.py:44
  127.2 22.3 %collective-permute-start.26 = (bf16[1024,256]{1,0:T(8,128)(2,1)S(1)}, bf16[1024,256]{1,0:T(8,128)(2,1)S(1)}, u32[]{:S(2)}, u32[]{:S(2)}) collective-permute-start(bf16[1024,256]{1,0:T(8,128)(2,1)S(1)} %collective-permute-done.25.refs_4_), channel_id=1, source_target_pairs={{0,6},{2,0},{4,2},{6,4},{1,7},{3,1},{5,3},{7,5},{8,14},{10,8},{12,... | collective-permute-start | bytes 1572872 | tf_op jit(solution)/shard_map/ppermute | solution.py:44
  129.9 19.7 %collective-permute-start.27 = (bf16[1024,256]{1,0:T(8,128)(2,1)S(1)}, bf16[1024,256]{1,0:T(8,128)(2,1)S(1)}, u32[]{:S(2)}, u32[]{:S(2)}) collective-permute-start(bf16[1024,256]{1,0:T(8,128)(2,1)S(1)} %collective-permute-done.23.refs_2_), channel_id=1, source_target_pairs={{0,1},{2,3},{4,5},{6,7},{1,0},{3,2},{5,4},{7,6},{8,9},{10,11},{12,... | collective-permute-start | bytes 1572872 | tf_op jit(solution)/shard_map/ppermute | solution.py:44
  138.3 30.0 %collective-permute-start.47 = (f32[136,256]{1,0:T(8,128)S(1)}, f32[136,256]{1,0:T(8,128)S(1)}, u32[]{:S(2)}, u32[]{:S(2)}) collective-permute-start(f32[136,256]{1,0:T(8,128)S(1)} %add.212), channel_id=1, source_target_pairs={{0,32},{8,40},{16,48},{24,56},{32,0},{40,8},{48,16},{56,24},{64,96... | collective-permute-start | bytes 417800 | tf_op jit(solution)/shard_map/ppermute | solution.py:157
  161.0 25.5 %collective-permute-start.30 = (bf16[1024,256]{1,0:T(8,128)(2,1)S(1)}, bf16[1024,256]{1,0:T(8,128)(2,1)S(1)}, u32[]{:S(2)}, u32[]{:S(2)}) collective-permute-start(bf16[1024,256]{1,0:T(8,128)(2,1)S(1)} %get-tuple-element.39), channel_id=1, source_target_pairs={{0,8},{8,0},{16,24},{24,16},{32,40},{40,32},{48,56},{56,48},{64,72... | collective-permute-start | bytes 1572872 | tf_op jit(solution)/shard_map/ppermute | solution.py:219
  186.5 17.6 %collective-permute-start.40 = (bf16[1024,256]{1,0:T(8,128)(2,1)S(1)}, bf16[1024,256]{1,0:T(8,128)(2,1)S(1)}, u32[]{:S(2)}, u32[]{:S(2)}) collective-permute-start(bf16[1024,256]{1,0:T(8,128)(2,1)S(1)} %get-tuple-element.49), channel_id=1, source_target_pairs={{0,8},{8,0},{16,24},{24,16},{32,40},{40,32},{48,56},{56,48},{64,72... | collective-permute-start | bytes 1572872 | tf_op jit(solution)/shard_map/ppermute | solution.py:219
  188.2 14.3 %collective-permute-start.36 = (bf16[1024,256]{1,0:T(8,128)(2,1)S(1)}, bf16[1024,256]{1,0:T(8,128)(2,1)S(1)}, u32[]{:S(2)}, u32[]{:S(2)}) collective-permute-start(bf16[1024,256]{1,0:T(8,128)(2,1)S(1)} %add_convert_fusion.5), channel_id=1, source_target_pairs={{0,16},{8,24},{16,32},{24,40},{32,48},{40,56},{48,0},{56,8},{64,80... | collective-permute-start | bytes 1572872 | tf_op jit(solution)/shard_map/ppermute | solution.py:59
  189.7 14.1 %collective-permute-start.38 = (bf16[1024,256]{1,0:T(8,128)(2,1)S(1)}, bf16[1024,256]{1,0:T(8,128)(2,1)S(1)}, u32[]{:S(2)}, u32[]{:S(2)}) collective-permute-start(bf16[1024,256]{1,0:T(8,128)(2,1)S(1)} %add_convert_fusion.4), channel_id=1, source_target_pairs={{0,48},{8,56},{16,0},{24,8},{32,16},{40,24},{48,32},{56,40},{64,11... | collective-permute-start | bytes 1572872 | tf_op jit(solution)/shard_map/ppermute | solution.py:59
  191.3 15.5 %collective-permute-start.42 = (bf16[1024,256]{1,0:T(8,128)(2,1)S(1)}, bf16[1024,256]{1,0:T(8,128)(2,1)S(1)}, u32[]{:S(2)}, u32[]{:S(2)}) collective-permute-start(bf16[1024,256]{1,0:T(8,128)(2,1)S(1)} %add_convert_fusion.2), channel_id=1, source_target_pairs={{0,64},{8,72},{16,80},{24,88},{32,96},{40,104},{48,112},{56,120},{... | collective-permute-start | bytes 1572872 | tf_op jit(solution)/shard_map/ppermute | solution.py:59
  192.2 17.3 %collective-permute-start.29 = (bf16[1024,256]{1,0:T(8,128)(2,1)S(1)}, bf16[1024,256]{1,0:T(8,128)(2,1)}, u32[]{:S(2)}, u32[]{:S(2)}) collective-permute-start(bf16[1024,256]{1,0:T(8,128)(2,1)S(1)} %get-tuple-element.37), channel_id=1, source_target_pairs={{0,8},{8,0},{16,24},{24,16},{32,40},{40,32},{48,56},{56,48},{64,72... | collective-permute-start | bytes 1572872 | tf_op jit(solution)/shard_map/ppermute | solution.py:219
  203.8 16.0 %collective-permute-start.31 = (bf16[1024,256]{1,0:T(8,128)(2,1)S(1)}, bf16[1024,256]{1,0:T(8,128)(2,1)}, u32[]{:S(2)}, u32[]{:S(2)}) collective-permute-start(bf16[1024,256]{1,0:T(8,128)(2,1)S(1)} %add_convert_fusion.7), channel_id=1, source_target_pairs={{0,16},{8,24},{16,32},{24,40},{32,48},{40,56},{48,0},{56,8},{64,80... | collective-permute-start | bytes 1572872 | tf_op jit(solution)/shard_map/ppermute | solution.py:59
  204.1 24.6 %collective-permute-start.33 = (bf16[1024,256]{1,0:T(8,128)(2,1)S(1)}, bf16[1024,256]{1,0:T(8,128)(2,1)}, u32[]{:S(2)}, u32[]{:S(2)}) collective-permute-start(bf16[1024,256]{1,0:T(8,128)(2,1)S(1)} %add_convert_fusion.6), channel_id=1, source_target_pairs={{0,48},{8,56},{16,0},{24,8},{32,16},{40,24},{48,32},{56,40},{64,11... | collective-permute-start | bytes 1572872 | tf_op jit(solution)/shard_map/ppermute | solution.py:59
  206.8 21.8 %collective-permute-start.39 = (bf16[1024,256]{1,0:T(8,128)(2,1)S(1)}, bf16[1024,256]{1,0:T(8,128)(2,1)}, u32[]{:S(2)}, u32[]{:S(2)}) collective-permute-start(bf16[1024,256]{1,0:T(8,128)(2,1)S(1)} %add_convert_fusion.3), channel_id=1, source_target_pairs={{0,64},{8,72},{16,80},{24,88},{32,96},{40,104},{48,112},{56,120},{... | collective-permute-start | bytes 1572872 | tf_op jit(solution)/shard_map/ppermute | solution.py:59
  207.1 21.6 %collective-permute-start.43 = (bf16[1024,256]{1,0:T(8,128)(2,1)S(1)}, bf16[1024,256]{1,0:T(8,128)(2,1)}, u32[]{:S(2)}, u32[]{:S(2)}) collective-permute-start(bf16[1024,256]{1,0:T(8,128)(2,1)S(1)} %add_convert_fusion.1), channel_id=1, source_target_pairs={{0,32},{8,40},{16,48},{24,56},{32,0},{40,8},{48,16},{56,24},{64,96... | collective-permute-start | bytes 1572872 | tf_op jit(solution)/shard_map/ppermute | solution.py:59
  (37 other events, 575.5 us)

commit v2 on v0

v2 whole, which is shorter than its diff:
```python
import functools

import jax
import jax.numpy as jnp
from jax import lax
from jax.experimental import pallas as pl
from jax.experimental.pallas import tpu as pltpu
from jax.sharding import PartitionSpec as P

BLK = 128
UNROLL = 8
CHUNK = 16


def both_perms(move):
    row = [
        (p * 8 + r * 2 + c, q * 8 + s * 2 + d)
        for p in range(2)
        for r in range(4)
        for c in range(2)
        for q, s, d in [move(p, r, c)]
    ]
    col = [
        (((c * 4 + r) * 2 + p), ((d * 4 + s) * 2 + q))
        for p in range(2)
        for r in range(4)
        for c in range(2)
        for q, s, d in [move(p, r, c)]
    ]
    return row, col


def over(v, perm, kind):
    if kind == "row":
        return lax.ppermute(v, "row", perm[0])
    pairs = [
        ((high * 2 + a // 8) * 8 + a % 8, (high * 2 + b // 8) * 8 + b % 8)
        for high in range(8)
        for a, b in perm[1]
    ]
    return lax.ppermute(v, ("row", "col"), pairs)


PAIR = both_perms(lambda p, r, c: (1 - p, r, c))
CORE = both_perms(lambda p, r, c: (p, r, 1 - c))
OUT = both_perms(lambda p, r, c: (p, (r + 1 - 2 * c) % 4, c))
BACK = both_perms(lambda p, r, c: (p, (r - 1 + 2 * c) % 4, c))


def wide(v):
    return v.astype(jnp.float32)


def narrow(v):
    return v.astype(jnp.bfloat16)


def meet(*arrays):
    return lax.optimization_barrier(arrays)


def direct_side():
    return jnp.where(lax.axis_index("row") % 2 == 0, 3, 1)


def row_place(pair, ring, core):
    side = jnp.where(ring == direct_side(), 4 + pair * 2 + core, 9 + pair * 2 - core)
    return jnp.where(
        ring == 0, pair * 2 + core, jnp.where(ring == 2, 12 + core * 2 + pair, side)
    )


def col_place(pair, ring):
    side = jnp.where(ring == direct_side(), 2 + pair, 4 + pair)
    return jnp.where(ring == 0, pair, jnp.where(ring == 2, 6 + pair, side))


ROW_SIZES = (1, 1, 1, 1, 1, 1, 1, 1, 2, 2, 2, 2)


class Summer:
    def __init__(self, v):
        self.half = v.shape[0] // 2
        self.core = lax.axis_index("row") % 2
        self.part = v
        bits = [(p, b) for p in (0,) for b in (1, 2)]
        rings = [both_perms(lambda p, r, c, b=b: (p, r ^ b, c)) for _, b in bits]
        self.todo = [(CORE, "row"), (PAIR, "row"), (rings[0], "row"), (rings[1], "row")]
        self.todo += [(PAIR, "col"), (rings[0], "col"), (rings[1], "col")]
        self.got = over(v, *self.todo.pop(0))

    def step(self, *events):
        got, *events = meet(self.got, *events)
        self.part = self.part + got
        if len(self.todo) == 6:
            self.part = lax.dynamic_slice_in_dim(self.part, self.core * self.half, self.half, 0)
        if self.todo:
            self.got = over(self.part, *self.todo.pop(0))
        return events

    def result(self):
        other = over(self.part, CORE, "row")
        first = jnp.where(self.core == 0, self.part, other)
        second = jnp.where(self.core == 0, other, self.part)
        return jnp.concatenate([first, second], axis=0)


def gather(own, kind, extra=(), summer=None):
    step = (lambda *v: summer().step(*v)) if summer else meet
    far = over(own, PAIR, kind)
    near_a = over(own, OUT, kind)
    other = over(own, CORE, kind)
    near_b = over(other, OUT, kind)
    near_a, *extra = step(near_a, *extra)
    across = over(near_a, OUT, kind)
    near_b, far, _ = meet(near_b, far, near_a)
    far_other = over(far, CORE, kind)
    far_a = over(far, OUT, kind)
    far_b = over(far_other, OUT, kind)
    across, _ = step(across, far_other)
    across_far = over(across, PAIR, kind)
    near_b_swapped = over(near_b, CORE, kind)
    if kind == "row":
        near_a_swapped = over(near_a, CORE, kind)
        across_swapped = over(across, CORE, kind)
        far_a, _ = meet(far_a, across)
        far_a_swapped = over(far_a, CORE, kind)
    far_b, across_far = step(far_b, across_far)
    far_b_swapped = over(far_b, CORE, kind)
    if kind == "row":
        across_far_swapped = over(across_far, CORE, kind)
        pieces = [own, other, far, far_other, near_a, near_b, far_a, far_b]
        pieces += [near_a_swapped, near_b_swapped, far_a_swapped, far_b_swapped]
        pieces += [across, across_far, across_swapped, across_far_swapped]
    else:
        pieces = [own, far, near_a, far_a, near_b_swapped, far_b_swapped, across, across_far]
    return pieces, extra


def scatter(parts, kind, summer=None):
    step = (lambda *v: summer.step(*v)) if summer else meet
    parts = list(parts)
    if kind == "row":
        own, other, far, far_other, near_a, near_b, far_a, far_b = parts[:8]
        side_near, side_far, across, across_other = parts[8:]
        rows = own.shape[0]
        turned = over(across_other, CORE, kind)
        turned_far = over(side_far, CORE, kind)
        turned_near = over(side_near, CORE, kind)
        across_near = wide(across[:rows]) + wide(turned[:rows])
        across_far = narrow(wide(across[rows:]) + wide(turned[rows:]))
        far_a = narrow(wide(far_a) + wide(turned_far[:rows]))
        far_b = narrow(wide(far_b) + wide(turned_far[rows:]))
        near_a = wide(near_a) + wide(turned_near[:rows])
        near_b = narrow(wide(near_b) + wide(turned_near[rows:]))
    else:
        own, far, near_a, far_a, side_near, side_far, across_near, across_far = parts
        far_b = over(side_far, CORE, kind)
        near_b = over(side_near, CORE, kind)
        across_near, near_a = wide(across_near), wide(near_a)
        other = far_other = None

    def plus(v, w):
        return w if v is None else narrow(wide(v) + wide(w))

    got_far_b = over(far_b, BACK, kind)
    passed_far = over(across_far, PAIR, kind)
    got_far_a = over(far_a, BACK, kind)
    (got_far_b,) = step(got_far_b)
    core_far = over(plus(far_other, got_far_b), CORE, kind)
    passed_far, _ = step(passed_far, got_far_b)
    across_sum = narrow(across_near + wide(passed_far))
    passed = over(across_sum, BACK, kind)
    near_b, got_far_a, _ = meet(near_b, got_far_a, across_sum)
    got_near_b = over(near_b, BACK, kind)
    far_sum = narrow(wide(far) + wide(got_far_a) + wide(core_far))
    back_far = over(far_sum, PAIR, kind)
    passed, _ = step(passed, far_sum)
    got_near_a = over(narrow(near_a + wide(passed)), BACK, kind)
    got_near_b, _ = step(got_near_b, passed)
    core_near = over(plus(other, got_near_b), CORE, kind)
    got_near_a, back_far, core_near = meet(got_near_a, back_far, core_near)
    return wide(own) + wide(got_near_a) + wide(back_far) + wide(core_near)


def sparse_kernel(transpose, n_in, rows, cols, count, adj, *refs):
    pieces = refs[:n_in]
    outs = refs[n_in:-5]
    table, acc, blocks, piece_sem, block_sem = refs[-5:]
    piece_copies = []
    at = 0
    for i, piece in enumerate(pieces):
        part = table.at[pl.ds(at, piece.shape[0])]
        piece_copies.append(pltpu.make_async_copy(piece, part, piece_sem.at[i]))
        at += piece.shape[0]
    for copy in piece_copies:
        copy.start()
    n_chunks = count[0] // CHUNK

    def block_copy(i):
        part = pl.ds(i * CHUNK, CHUNK)
        return pltpu.make_async_copy(adj.at[part], blocks.at[part], block_sem.at[i])

    @pl.loop(0, n_chunks)
    def _(i):
        block_copy(i).start()

    @pl.loop(0, acc.shape[0] // 256)
    def _(i):
        acc[pl.ds(pl.multiple_of(i * 256, 256), 256), :] = jnp.zeros((256, acc.shape[1]), acc.dtype)

    for copy in piece_copies:
        copy.wait()

    @pl.loop(0, n_chunks)
    def _(i):
        block_copy(i).wait()

        @pl.loop(0, CHUNK // UNROLL)
        def _(step):
            for u in range(UNROLL):
                slot = i * CHUNK + step * UNROLL + u
                out_at = pl.multiple_of(rows[slot] * BLK, BLK)
                in_at = pl.multiple_of(cols[slot] * BLK, BLK)
                dims = (((0,), (0,)), ((), ())) if transpose else (((1,), (0,)), ((), ()))
                acc[pl.ds(out_at, BLK), :] += lax.dot_general(
                    blocks[slot],
                    table[pl.ds(in_at, BLK), :],
                    dims,
                    preferred_element_type=jnp.float32,
                )

    at = 0
    for out in outs:

        @pl.loop(0, out.shape[0] // BLK)
        def _(j, at=at, out=out):
            here = pl.multiple_of(j * BLK, BLK)
            out[pl.ds(here, BLK), :] = acc[pl.ds(at + here, BLK), :].astype(out.dtype)

        at += out.shape[0]


def sparse(transpose, rows, cols, count, adj, pieces, sizes):
    n_in = len(pieces)
    width = pieces[0].shape[1]
    in_rows = sum(piece.shape[0] for piece in pieces)
    n_slots = adj.shape[0]
    return pl.pallas_call(
        functools.partial(sparse_kernel, transpose, n_in),
        out_shape=[jax.ShapeDtypeStruct((size, width), jnp.bfloat16) for size in sizes],
        in_specs=[pl.BlockSpec(memory_space=pltpu.SMEM)] * 3
        + [pl.BlockSpec(memory_space=pltpu.HBM)]
        + [pl.BlockSpec(memory_space=pl.ANY)] * n_in,
        out_specs=[pl.BlockSpec(memory_space=pltpu.VMEM)] * len(sizes),
        scratch_shapes=[
            pltpu.VMEM((in_rows, width), jnp.bfloat16),
            pltpu.VMEM((sum(sizes), width), jnp.float32),
            pltpu.VMEM((n_slots, BLK, BLK), jnp.bfloat16),
            pltpu.SemaphoreType.DMA((n_in,)),
            pltpu.SemaphoreType.DMA((n_slots // CHUNK,)),
        ],
        compiler_params=pltpu.CompilerParams(vmem_limit_bytes=(38 if transpose else 30) * 1024 * 1024),
        cost_estimate=pl.CostEstimate(
            flops=2 * n_slots * BLK * BLK * width,
            bytes_accessed=n_slots * BLK * BLK * 2 + (in_rows + sum(sizes)) * width * 2,
            transcendentals=0,
        ),
        name="sparse_back" if transpose else "sparse_forward",
    )(rows, cols, count, adj, *pieces)


def local(node_features, weight, bias, adj_blocks, block_row, block_col, slot_count, cotangent):
    node_rows, width = node_features.shape[2:]
    per = node_rows // BLK
    adj = adj_blocks[0, 0]
    count = slot_count[0]
    me_row = lax.axis_index("row")
    me_col = lax.axis_index("col")

    owner = block_col[0, 0] // per
    place = row_place(
        (owner // 8) ^ (me_row // 8), (owner // 2 - me_row // 2) % 4, (owner ^ me_row) % 2
    )
    in_ids = place * per + block_col[0, 0] % per
    owner = block_row[0, 0] // per
    place = col_place((owner ^ me_col) % 2, (owner // 2 - me_col // 2) % 4)
    out_ids = place * per + block_row[0, 0] % per

    pieces, (in_ids, out_ids) = gather(node_features[0, 0], "row", (in_ids, out_ids))
    sums = sparse(False, out_ids, in_ids, count, adj, pieces, [node_rows] * 8)
    aggregate = narrow(scatter(sums, "col"))

    pre = jnp.dot(aggregate, weight, preferred_element_type=jnp.float32) + bias
    sigma = jax.nn.sigmoid(pre)
    layer_out = narrow(pre * sigma)
    grad_pre = narrow(wide(cotangent[0, 0]) * sigma * (1.0 + pre * (1.0 - sigma)))

    made = []

    def summer():
        if not made:
            weight_term = lax.dot_general(
                aggregate, grad_pre, (((0,), (0,)), ((), ())), preferred_element_type=jnp.float32
            )
            bias_term = jnp.sum(wide(grad_pre), axis=0)
            spare = jnp.zeros((15, width), jnp.float32)
            made.append(Summer(jnp.concatenate([weight_term, bias_term[None], spare], axis=0)))
        return made[0]

    pieces, _ = gather(grad_pre, "col", (), summer)
    backs = sparse(
        True, in_ids, out_ids, count, adj, pieces, [node_rows * size for size in ROW_SIZES]
    )
    grad_projected = narrow(scatter(backs, "row", summer()))
    grad_input = narrow(
        lax.dot_general(
            grad_projected, weight, (((1,), (1,)), ((), ())), preferred_element_type=jnp.float32
        )
    )
    summed = summer().result()
    return (
        layer_out.reshape(1, 1, node_rows, width),
        grad_input.reshape(1, 1, node_rows, width),
        summed[:width],
        summed[width],
    )


def solution(mesh):
    placed = (
        P("col", "row", None, None),
        P(),
        P(),
        P("row", "col", None, None, None),
        P("row", "col", None),
        P("row", "col", None),
        P("row", "col"),
        P("row", "col", None, None),
    )
    return jax.shard_map(
        local,
        mesh=mesh,
        in_specs=placed,
        out_specs=(P("row", "col", None, None), P("col", "row", None, None), P(), P()),
        check_vma=False,
    )
```

time: 786 us -> 200 us (0.25)
  waiting for transfers between devices: 441 us -> 95.8 us
  other arithmetic: 119 us -> 4.03 us
  local copies, waits for them, and re-layouts: 100 us -> 4.49 us
  starting transfers between devices: 0.38 us -> 80.1 us
  blocking collectives: 68 us -> 0 us
  matrix products: 42.1 us -> 3.03 us
  between operations: 14.5 us -> 1.55 us
  Pallas kernels: 0 us -> 10.4 us
    all_gather x2 -> x0, waiting for transfers between devices: 168 us -> none  [the longest x1 90.6 us: local(): row_table = lax.all_gather(grad_pre, 'col', axis=0, tiled=True)]
    psum x1 -> x0, waiting for transfers between devices: 142 us -> none  [local(): grad_weight, grad_bias = lax.psum((weight_term, bias_term), ('row', 'col'))]
    reduce_scatter x2 -> x0, waiting for transfers between devices: 130 us -> none  [the longest x1 92.4 us: local(): lax.psum_scatter(cell_sum.astype(jnp.bfloat16), 'col', scatter_dimension=...]
    scatter-add x2 -> x0, other arithmetic: 115 us -> none  [the longest x1 58 us: cell_backward(): jax.ops.segment_sum(contrib, targets, num_segments=col_count + 1)]
    ppermute x0 -> x57, waiting for transfers between devices: none -> 95.8 us  [the longest x32 51.4 us: over(): return lax.ppermute(v, 'row', perm[0])]
    ppermute x0 -> x57, starting transfers between devices: none -> 80.1 us  [the longest x32 49.8 us: over(): return lax.ppermute(v, 'row', perm[0])]
    psum x1 -> x0, blocking collectives: 68 us -> none  [local(): grad_weight, grad_bias = lax.psum((weight_term, bias_term), ('row', 'col'))]
    dot_general x2 -> x0, local copies, waits for them, and re-layouts: 49.3 us -> none  [the longest x1 24.7 us: cell_forward(): jnp.einsum('sbk,skf->sbf', blocks, picked, preferred_element_type=jnp.flo...]
  transfers between devices with their start and end apart: 5 -> 57, of which waited for: 5 -> 31; matrix products, arithmetic and copies ran while one was open for 0% -> 2% of each run, Pallas kernels for 0% -> 0%
where the time goes in v2:
time: 200 us; the launch traced here: 199 us
  waiting for transfers between devices  95.8 us (48%)
  starting transfers between devices  80.1 us (40%)
  Pallas kernels  10.4 us (5%)
  local copies, waits for them, and re-layouts  4.49 us (2%)
  other arithmetic  4.03 us (2%)
  matrix products  3.03 us (2%)
    ppermute x32, waiting for transfers between devices, over(): return lax.ppermute(v, 'row', perm[0])  51.4 us
    ppermute x32, starting transfers between devices, over(): return lax.ppermute(v, 'row', perm[0])  49.8 us
    ppermute x25, waiting for transfers between devices, over(): return lax.ppermute(v, ('row', 'col'), pairs)  44.4 us
    ppermute x25, starting transfers between devices, over(): return lax.ppermute(v, ('row', 'col'), pairs)  30.3 us
    pallas_call x2, Pallas kernels, sparse(): pl.pallas_call(functools.partial(sparse_kernel, transpose, n_in), out_sha...  10.4 us
  transfers between devices with their start and end apart: 57, of which 31 were waited for; matrix products, arithmetic and copies ran while one was open for 2% of the time, Pallas kernels for 0%

profile of v2, /device:TPU:1, one launch (start us, length us, event | category | flops | bytes accessed | tf_op | source)
XLA Modules:
  0.0 199.3 jit_solution(2417474540861067014)
XLA Ops:
  2.1 2.6 %collective-permute-start = (bf16[1024,256]{1,0:T(8,128)(2,1)}, bf16[1024,256]{1,0:T(8,128)(2,1)S(1)}, u32[]{:S(2)}, u32[]{:S(2)}) collective-permute-start(bf16[1024,256]{1,0:T(8,128)(2,1)} %bitcast.25), channel_id=1, source_target_pairs={{0,16},{8,56},{16,32},{24,8},{32,48},{40,24},{48,0},{56,40},{64,80... | collective-permute-start | bytes 1572872 | tf_op jit(solution)/shard_map/ppermute | solution.py:35
  4.7 3.6 %collective-permute-start.3 = (bf16[1024,256]{1,0:T(8,128)(2,1)}, bf16[1024,256]{1,0:T(8,128)(2,1)S(1)}, u32[]{:S(2)}, u32[]{:S(2)}) collective-permute-start(bf16[1024,256]{1,0:T(8,128)(2,1)} %bitcast.26), channel_id=1, source_target_pairs={{0,64},{8,72},{16,80},{24,88},{32,96},{40,104},{48,112},{56,120},{... | collective-permute-start | bytes 1572872 | tf_op jit(solution)/shard_map/ppermute | solution.py:35
  11.2 8.9 %collective-permute-done.3.refs_2_ = bf16[1024,256]{1,0:T(8,128)(2,1)S(1)} collective-permute-done((bf16[1024,256]{1,0:T(8,128)(2,1)}, bf16[1024,256]{1,0:T(8,128)(2,1)S(1)}, u32[]{:S(2)}, u32[]{:S(2)}) %collective-permute-start.3) | collective-permute-done | bytes 524320 | tf_op jit(solution)/shard_map/ppermute | solution.py:35
  23.5 4.8 %collective-permute-done.6.refs_12_ = bf16[1024,256]{1,0:T(8,128)(2,1)S(1)} collective-permute-done((bf16[1024,256]{1,0:T(8,128)(2,1)S(1)}, bf16[1024,256]{1,0:T(8,128)(2,1)S(1)}, u32[]{:S(2)}, u32[]{:S(2)}) %collective-permute-start.6) | collective-permute-done | bytes 524320 | tf_op jit(solution)/shard_map/ppermute | solution.py:35
  28.3 3.5 %collective-permute-start.8 = (bf16[1024,256]{1,0:T(8,128)(2,1)S(1)}, bf16[1024,256]{1,0:T(8,128)(2,1)S(1)}, u32[]{:S(2)}, u32[]{:S(2)}) collective-permute-start(bf16[1024,256]{1,0:T(8,128)(2,1)S(1)} %collective-permute-done.6.refs_12_), channel_id=1, source_target_pairs={{0,64},{8,72},{16,80},{24,88},{32,96},{40,104},{48,112},{56,120},{... | collective-permute-start | bytes 1572872 | tf_op jit(solution)/shard_map/ppermute | solution.py:35
  31.9 2.5 %collective-permute-start.9 = (bf16[1024,256]{1,0:T(8,128)(2,1)S(1)}, bf16[1024,256]{1,0:T(8,128)(2,1)S(1)}, u32[]{:S(2)}, u32[]{:S(2)}) collective-permute-start(bf16[1024,256]{1,0:T(8,128)(2,1)S(1)} %collective-permute-done.refs_4_), channel_id=1, source_target_pairs={{0,8},{8,0},{16,24},{24,16},{32,40},{40,32},{48,56},{56,48},{64,72... | collective-permute-start | bytes 1572872 | tf_op jit(solution)/shard_map/ppermute | solution.py:35
  36.5 3.0 %collective-permute-done.7.refs_7_ = bf16[1024,256]{1,0:T(8,128)(2,1)S(1)} collective-permute-done((bf16[1024,256]{1,0:T(8,128)(2,1)S(1)}, bf16[1024,256]{1,0:T(8,128)(2,1)S(1)}, u32[]{:S(2)}, u32[]{:S(2)}) %collective-permute-start.7) | collective-permute-done | bytes 524320 | tf_op jit(solution)/shard_map/ppermute | solution.py:35
  39.6 2.6 %collective-permute-start.11 = (bf16[1024,256]{1,0:T(8,128)(2,1)S(1)}, bf16[1024,256]{1,0:T(8,128)(2,1)S(1)}, u32[]{:S(2)}, u32[]{:S(2)}) collective-permute-start(bf16[1024,256]{1,0:T(8,128)(2,1)S(1)} %collective-permute-done.5.refs_6_), channel_id=1, source_target_pairs={{0,8},{8,0},{16,24},{24,16},{32,40},{40,32},{48,56},{56,48},{64,72... | collective-permute-start | bytes 1572872 | tf_op jit(solution)/shard_map/ppermute | solution.py:35
  42.2 2.6 %collective-permute-start.12 = (bf16[1024,256]{1,0:T(8,128)(2,1)S(1)}, bf16[1024,256]{1,0:T(8,128)(2,1)S(1)}, u32[]{:S(2)}, u32[]{:S(2)}) collective-permute-start(bf16[1024,256]{1,0:T(8,128)(2,1)S(1)} %collective-permute-done.7.refs_7_), channel_id=1, source_target_pairs={{0,8},{8,0},{16,24},{24,16},{32,40},{40,32},{48,56},{56,48},{64,72... | collective-permute-start | bytes 1572872 | tf_op jit(solution)/shard_map/ppermute | solution.py:35
  47.1 2.8 %copy-done.1 = bf16[1,1,192,128,128]{4,3,2,1,0:T(8,128)(2,1)S(1)} copy-done((bf16[1,1,192,128,128]{4,3,2,1,0:T(8,128)(2,1)S(1)}, bf16[1,1,192,128,128]{4,3,2,1,0:T(8,128)(2,1)}, u32[]{:S(2)}) %copy-start.1) | copy-done | bytes 6291480
  50.9 4.7 %sparse_forward.1 = (bf16[1024,256]{1,0:T(8,128)(2,1)S(1)}, bf16[1024,256]{1,0:T(8,128)(2,1)S(1)}, bf16[1024,256]{1,0:T(8,128)(2,1)S(1)}, bf16[1024,256]{1,0:T(8...) custom-call(s32[192]{0:T(256)S(1)} %get-tuple-element.63.rows.cols, ...), custom_call_target="tpu_custom_call" | custom-call | flops 1610612736 | bytes 18874368 | tf_op jit(solution)/shard_map/sparse_forward/pallas_call | solution.py:249
  58.2 6.5 %collective-permute-start.17 = (bf16[1024,256]{1,0:T(8,128)(2,1)S(1)}, bf16[1024,256]{1,0:T(8,128)(2,1)S(1)}, u32[]{:S(2)}, u32[]{:S(2)}) collective-permute-start(bf16[1024,256]{1,0:T(8,128)(2,1)S(1)} %collective-permute-done.16), channel_id=1, source_target_pairs={{0,6},{8,10},{2,0},{10,12},{4,2},{12,14},{6,4},{14,8},{1,7},{9,11}... | collective-permute-start | bytes 1572872 | tf_op jit(solution)/shard_map/ppermute | solution.py:41
  67.0 3.8 %collective-permute-done.17 = bf16[1024,256]{1,0:T(8,128)(2,1)S(1)} collective-permute-done((bf16[1024,256]{1,0:T(8,128)(2,1)S(1)}, bf16[1024,256]{1,0:T(8,128)(2,1)S(1)}, u32[]{:S(2)}, u32[]{:S(2)}) %collective-permute-start.17) | collective-permute-done | bytes 524320 | tf_op jit(solution)/shard_map/ppermute | solution.py:41
  72.5 4.8 %collective-permute-done.15 = bf16[1024,256]{1,0:T(8,128)(2,1)S(1)} collective-permute-done((bf16[1024,256]{1,0:T(8,128)(2,1)S(1)}, bf16[1024,256]{1,0:T(8,128)(2,1)S(1)}, u32[]{:S(2)}, u32[]{:S(2)}) %collective-permute-start.15) | collective-permute-done | bytes 524320 | tf_op jit(solution)/shard_map/ppermute | solution.py:41
  80.9 5.9 %collective-permute-done.18 = bf16[1024,256]{1,0:T(8,128)(2,1)S(1)} collective-permute-done((bf16[1024,256]{1,0:T(8,128)(2,1)S(1)}, bf16[1024,256]{1,0:T(8,128)(2,1)S(1)}, u32[]{:S(2)}, u32[]{:S(2)}) %collective-permute-start.18) | collective-permute-done | bytes 524320 | tf_op jit(solution)/shard_map/ppermute | solution.py:41
  88.2 4.2 %collective-permute-done.24 = bf16[1024,256]{1,0:T(8,128)(2,1)S(1)} collective-permute-done((bf16[1024,256]{1,0:T(8,128)(2,1)S(1)}, bf16[1024,256]{1,0:T(8,128)(2,1)S(1)}, u32[]{:S(2)}, u32[]{:S(2)}) %collective-permute-start.24) | collective-permute-done | bytes 524320 | tf_op jit(solution)/shard_map/ppermute | solution.py:41
  93.1 4.9 %collective-permute-done.22 = bf16[1024,256]{1,0:T(8,128)(2,1)S(1)} collective-permute-done((bf16[1024,256]{1,0:T(8,128)(2,1)S(1)}, bf16[1024,256]{1,0:T(8,128)(2,1)S(1)}, u32[]{:S(2)}, u32[]{:S(2)}) %collective-permute-start.22) | collective-permute-done | bytes 524320 | tf_op jit(solution)/shard_map/ppermute | solution.py:41
  106.5 2.7 %collective-permute-done.30.refs_2_ = bf16[1024,256]{1,0:T(8,128)(2,1)S(1)} collective-permute-done((bf16[1024,256]{1,0:T(8,128)(2,1)S(1)}, bf16[1024,256]{1,0:T(8,128)(2,1)S(1)}, u32[]{:S(2)}, u32[]{:S(2)}) %collective-permute-start.30) | collective-permute-done | bytes 524320 | tf_op jit(solution)/shard_map/ppermute | solution.py:41
  110.0 3.4 %collective-permute-done.28.refs_1_ = bf16[1024,256]{1,0:T(8,128)(2,1)S(1)} collective-permute-done((bf16[1024,256]{1,0:T(8,128)(2,1)S(1)}, bf16[1024,256]{1,0:T(8,128)(2,1)S(1)}, u32[]{:S(2)}, u32[]{:S(2)}) %collective-permute-start.28) | collective-permute-done | bytes 524320 | tf_op jit(solution)/shard_map/ppermute | solution.py:41
  116.6 3.7 %collective-permute-start.33 = (f32[136,256]{1,0:T(8,128)S(1)}, f32[136,256]{1,0:T(8,128)S(1)}, u32[]{:S(2)}, u32[]{:S(2)}) collective-permute-start(f32[136,256]{1,0:T(8,128)S(1)} %dynamic-slice_add_fusion), channel_id=1, source_target_pairs={{0,64},{8,72},{16,80},{24,88},{32,96},{40,104},{48,112},{56,120},{... | collective-permute-start | bytes 417800 | tf_op jit(solution)/shard_map/ppermute | solution.py:35
  120.3 4.0 %collective-permute-done.33 = f32[136,256]{1,0:T(8,128)S(1)} collective-permute-done((f32[136,256]{1,0:T(8,128)S(1)}, f32[136,256]{1,0:T(8,128)S(1)}, u32[]{:S(2)}, u32[]{:S(2)}) %collective-permute-start.33) | collective-permute-done | bytes 139296 | tf_op jit(solution)/shard_map/ppermute | solution.py:35
  127.3 4.9 %collective-permute-done.36 = f32[136,256]{1,0:T(8,128)S(1)} collective-permute-done((f32[136,256]{1,0:T(8,128)S(1)}, f32[136,256]{1,0:T(8,128)S(1)}, u32[]{:S(2)}, u32[]{:S(2)}) %collective-permute-start.36) | collective-permute-done | bytes 139296 | tf_op jit(solution)/shard_map/ppermute | solution.py:35
  132.2 5.0 %collective-permute-done.38.refs_7_ = bf16[1024,256]{1,0:T(8,128)(2,1)S(1)} collective-permute-done((bf16[1024,256]{1,0:T(8,128)(2,1)S(1)}, bf16[1024,256]{1,0:T(8,128)(2,1)S(1)}, u32[]{:S(2)}, u32[]{:S(2)}) %collective-permute-start.38) | collective-permute-done | bytes 524320 | tf_op jit(solution)/shard_map/ppermute | solution.py:41
  140.2 5.7 %sparse_back.1 = (bf16[1024,256]{1,0:T(8,128)(2,1)S(1)}, bf16[1024,256]{1,0:T(8,128)(2,1)S(1)}, bf16[1024,256]{1,0:T(8,128)(2,1)S(1)}, bf16[1024,256]{1,0:T(8,12...) custom-call(s32[192]{0:T(256)S(1)} %get-tuple-element.64.cols.rows, ...), custom_call_target="tpu_custom_call" | custom-call | flops 1610612736 | bytes 18874368 | tf_op jit(solution)/shard_map/sparse_back/pallas_call | solution.py:249
  145.9 2.7 %collective-permute-start.42 = (bf16[2048,256]{1,0:T(8,128)(2,1)S(1)}, bf16[2048,256]{1,0:T(8,128)(2,1)S(1)}, u32[]{:S(2)}, u32[]{:S(2)}) collective-permute-start(bf16[2048,256]{1,0:T(8,128)(2,1)S(1)} %get-tuple-element.101), channel_id=1, source_target_pairs={{0,8},{8,0},{16,24},{24,16},{32,40},{40,32},{48,56},{56,48},{64,72... | collective-permute-start | bytes 3145736 | tf_op jit(solution)/shard_map/ppermute | solution.py:35
  151.2 4.7 %collective-permute-start.43 = (bf16[1024,256]{1,0:T(8,128)(2,1)S(1)}, bf16[1024,256]{1,0:T(8,128)(2,1)S(1)}, u32[]{:S(2)}, u32[]{:S(2)}) collective-permute-start(bf16[1024,256]{1,0:T(8,128)(2,1)S(1)} %get-tuple-element.125), channel_id=1, source_target_pairs={{0,48},{8,24},{16,0},{24,40},{32,16},{40,56},{48,32},{56,8},{64,11... | collective-permute-start | bytes 1572872 | tf_op jit(solution)/shard_map/ppermute | solution.py:35
  156.1 6.3 %collective-permute-start.46 = (bf16[1024,256]{1,0:T(8,128)(2,1)S(1)}, bf16[1024,256]{1,0:T(8,128)(2,1)S(1)}, u32[]{:S(2)}, u32[]{:S(2)}) collective-permute-start(bf16[1024,256]{1,0:T(8,128)(2,1)S(1)} %add_convert_fusion.8), channel_id=1, source_target_pairs={{0,64},{8,72},{16,80},{24,88},{32,96},{40,104},{48,112},{56,120},{... | collective-permute-start | bytes 1572872 | tf_op jit(solution)/shard_map/ppermute | solution.py:35
  163.9 5.2 %collective-permute-done.41 = f32[136,256]{1,0:T(8,128)S(1)} collective-permute-done((f32[136,256]{1,0:T(8,128)S(1)}, f32[136,256]{1,0:T(8,128)S(1)}, u32[]{:S(2)}, u32[]{:S(2)}) %collective-permute-start.41) | collective-permute-done | bytes 139296 | tf_op jit(solution)/shard_map/ppermute | solution.py:35
  171.2 3.5 %collective-permute-done.46 = bf16[1024,256]{1,0:T(8,128)(2,1)S(1)} collective-permute-done((bf16[1024,256]{1,0:T(8,128)(2,1)S(1)}, bf16[1024,256]{1,0:T(8,128)(2,1)S(1)}, u32[]{:S(2)}, u32[]{:S(2)}) %collective-permute-start.46) | collective-permute-done | bytes 524320 | tf_op jit(solution)/shard_map/ppermute | solution.py:35
  179.4 2.3 %collective-permute-done.47 = f32[136,256]{1,0:T(8,128)S(1)} collective-permute-done((f32[136,256]{1,0:T(8,128)S(1)}, f32[136,256]{1,0:T(8,128)S(1)}, u32[]{:S(2)}, u32[]{:S(2)}) %collective-permute-start.47) | collective-permute-done | bytes 139296 | tf_op jit(solution)/shard_map/ppermute | solution.py:41
  181.8 4.8 %collective-permute-done.48 = bf16[1024,256]{1,0:T(8,128)(2,1)S(1)} collective-permute-done((bf16[1024,256]{1,0:T(8,128)(2,1)S(1)}, bf16[1024,256]{1,0:T(8,128)(2,1)S(1)}, u32[]{:S(2)}, u32[]{:S(2)}) %collective-permute-start.48) | collective-permute-done | bytes 524320 | tf_op jit(solution)/shard_map/ppermute | solution.py:35
  188.8 3.4 %collective-permute-done.54 = bf16[1024,256]{1,0:T(8,128)(2,1)S(1)} collective-permute-done((bf16[1024,256]{1,0:T(8,128)(2,1)S(1)}, bf16[1024,256]{1,0:T(8,128)(2,1)S(1)}, u32[]{:S(2)}, u32[]{:S(2)}) %collective-permute-start.54) | collective-permute-done | bytes 524320 | tf_op jit(solution)/shard_map/ppermute | solution.py:35
  (123 shorter events, 63.7 us)
Async XLA Ops:
  4.7 15.3 %collective-permute-start.3 = (bf16[1024,256]{1,0:T(8,128)(2,1)}, bf16[1024,256]{1,0:T(8,128)(2,1)S(1)}, u32[]{:S(2)}, u32[]{:S(2)}) collective-permute-start(bf16[1024,256]{1,0:T(8,128)(2,1)} %bitcast.26), channel_id=1, source_target_pairs={{0,64},{8,72},{16,80},{24,88},{32,96},{40,104},{48,112},{56,120},{... | collective-permute-start | bytes 1572872 | tf_op jit(solution)/shard_map/ppermute | solution.py:35
  8.3 11.7 %collective-permute-start.2 = (bf16[1024,256]{1,0:T(8,128)(2,1)S(1)}, bf16[1024,256]{1,0:T(8,128)(2,1)S(1)}, u32[]{:S(2)}, u32[]{:S(2)}) collective-permute-start(bf16[1024,256]{1,0:T(8,128)(2,1)S(1)} %collective-permute-done.1.refs_1_), channel_id=1, source_target_pairs={{0,16},{8,56},{16,32},{24,8},{32,48},{40,24},{48,0},{56,40},{64,80... | collective-permute-start | bytes 1572872 | tf_op jit(solution)/shard_map/ppermute | solution.py:35
  22.0 12.4 %collective-permute-start.5 = (bf16[1024,256]{1,0:T(8,128)(2,1)S(1)}, bf16[1024,256]{1,0:T(8,128)(2,1)S(1)}, u32[]{:S(2)}, u32[]{:S(2)}) collective-permute-start(bf16[1024,256]{1,0:T(8,128)(2,1)S(1)} %collective-permute-done.3.refs_2_), channel_id=1, source_target_pairs={{0,16},{8,56},{16,32},{24,8},{32,48},{40,24},{48,0},{56,40},{64,80... | collective-permute-start | bytes 1572872 | tf_op jit(solution)/shard_map/ppermute | solution.py:35
  22.2 17.3 %collective-permute-start.7 = (bf16[1024,256]{1,0:T(8,128)(2,1)S(1)}, bf16[1024,256]{1,0:T(8,128)(2,1)S(1)}, u32[]{:S(2)}, u32[]{:S(2)}) collective-permute-start(bf16[1024,256]{1,0:T(8,128)(2,1)S(1)} %collective-permute-done.4.refs_3_), channel_id=1, source_target_pairs={{0,16},{8,56},{16,32},{24,8},{32,48},{40,24},{48,0},{56,40},{64,80... | collective-permute-start | bytes 1572872 | tf_op jit(solution)/shard_map/ppermute | solution.py:35
  28.3 13.8 %collective-permute-start.8 = (bf16[1024,256]{1,0:T(8,128)(2,1)S(1)}, bf16[1024,256]{1,0:T(8,128)(2,1)S(1)}, u32[]{:S(2)}, u32[]{:S(2)}) collective-permute-start(bf16[1024,256]{1,0:T(8,128)(2,1)S(1)} %collective-permute-done.6.refs_12_), channel_id=1, source_target_pairs={{0,64},{8,72},{16,80},{24,88},{32,96},{40,104},{48,112},{56,120},{... | collective-permute-start | bytes 1572872 | tf_op jit(solution)/shard_map/ppermute | solution.py:35
  31.9 12.9 %collective-permute-start.9 = (bf16[1024,256]{1,0:T(8,128)(2,1)S(1)}, bf16[1024,256]{1,0:T(8,128)(2,1)S(1)}, u32[]{:S(2)}, u32[]{:S(2)}) collective-permute-start(bf16[1024,256]{1,0:T(8,128)(2,1)S(1)} %collective-permute-done.refs_4_), channel_id=1, source_target_pairs={{0,8},{8,0},{16,24},{24,16},{32,40},{40,32},{48,56},{56,48},{64,72... | collective-permute-start | bytes 1572872 | tf_op jit(solution)/shard_map/ppermute | solution.py:35
  34.4 11.0 %collective-permute-start.10 = (bf16[1024,256]{1,0:T(8,128)(2,1)S(1)}, bf16[1024,256]{1,0:T(8,128)(2,1)S(1)}, u32[]{:S(2)}, u32[]{:S(2)}) collective-permute-start(bf16[1024,256]{1,0:T(8,128)(2,1)S(1)} %collective-permute-done.2.refs_5_), channel_id=1, source_target_pairs={{0,8},{8,0},{16,24},{24,16},{32,40},{40,32},{48,56},{56,48},{64,72... | collective-permute-start | bytes 1572872 | tf_op jit(solution)/shard_map/ppermute | solution.py:35
  34.4 11.0 %collective-permute-start.13 = (bf16[1024,256]{1,0:T(8,128)(2,1)S(1)}, bf16[1024,256]{1,0:T(8,128)(2,1)S(1)}, u32[]{:S(2)}, u32[]{:S(2)}) collective-permute-start(bf16[1024,256]{1,0:T(8,128)(2,1)S(1)} %collective-permute-done.6.refs_12_), channel_id=1, source_target_pairs={{0,8},{8,0},{16,24},{24,16},{32,40},{40,32},{48,56},{56,48},{64,72... | collective-permute-start | bytes 1572872 | tf_op jit(solution)/shard_map/ppermute | solution.py:35
  58.2 12.6 %collective-permute-start.17 = (bf16[1024,256]{1,0:T(8,128)(2,1)S(1)}, bf16[1024,256]{1,0:T(8,128)(2,1)S(1)}, u32[]{:S(2)}, u32[]{:S(2)}) collective-permute-start(bf16[1024,256]{1,0:T(8,128)(2,1)S(1)} %collective-permute-done.16), channel_id=1, source_target_pairs={{0,6},{8,10},{2,0},{10,12},{4,2},{12,14},{6,4},{14,8},{1,7},{9,11}... | collective-permute-start | bytes 1572872 | tf_op jit(solution)/shard_map/ppermute | solution.py:41
  64.7 12.6 %collective-permute-start.15 = (bf16[1024,256]{1,0:T(8,128)(2,1)S(1)}, bf16[1024,256]{1,0:T(8,128)(2,1)S(1)}, u32[]{:S(2)}, u32[]{:S(2)}) collective-permute-start(bf16[1024,256]{1,0:T(8,128)(2,1)S(1)} %get-tuple-element.75), channel_id=1, source_target_pairs={{0,1},{8,9},{2,3},{10,11},{4,5},{12,13},{6,7},{14,15},{1,0},{9,8},... | collective-permute-start | bytes 1572872 | tf_op jit(solution)/shard_map/ppermute | solution.py:41
  64.7 15.0 %collective-permute-start.19 = (bf16[1024,256]{1,0:T(8,128)(2,1)S(1)}, bf16[1024,256]{1,0:T(8,128)(2,1)S(1)}, u32[]{:S(2)}, u32[]{:S(2)}) collective-permute-start(bf16[1024,256]{1,0:T(8,128)(2,1)S(1)} %get-tuple-element.79), channel_id=1, source_target_pairs={{0,8},{8,0},{2,10},{10,2},{4,12},{12,4},{6,14},{14,6},{1,9},{9,1},... | collective-permute-start | bytes 1572872 | tf_op jit(solution)/shard_map/ppermute | solution.py:41
  64.7 15.0 %collective-permute-start.20 = (bf16[1024,256]{1,0:T(8,128)(2,1)S(1)}, bf16[1024,256]{1,0:T(8,128)(2,1)S(1)}, u32[]{:S(2)}, u32[]{:S(2)}) collective-permute-start(bf16[1024,256]{1,0:T(8,128)(2,1)S(1)} %get-tuple-element.80), channel_id=1, source_target_pairs={{0,6},{8,10},{2,0},{10,12},{4,2},{12,14},{6,4},{14,8},{1,7},{9,11}... | collective-permute-start | bytes 1572872 | tf_op jit(solution)/shard_map/ppermute | solution.py:41
  77.4 9.3 %collective-permute-start.18 = (bf16[1024,256]{1,0:T(8,128)(2,1)S(1)}, bf16[1024,256]{1,0:T(8,128)(2,1)S(1)}, u32[]{:S(2)}, u32[]{:S(2)}) collective-permute-start(bf16[1024,256]{1,0:T(8,128)(2,1)S(1)} %add_convert_fusion.13), channel_id=1, source_target_pairs={{0,6},{8,10},{2,0},{10,12},{4,2},{12,14},{6,4},{14,8},{1,7},{9,11}... | collective-permute-start | bytes 1572872 | tf_op jit(solution)/shard_map/ppermute | solution.py:41
  79.7 12.7 %collective-permute-start.24 = (bf16[1024,256]{1,0:T(8,128)(2,1)S(1)}, bf16[1024,256]{1,0:T(8,128)(2,1)S(1)}, u32[]{:S(2)}, u32[]{:S(2)}) collective-permute-start(bf16[1024,256]{1,0:T(8,128)(2,1)S(1)} %collective-permute-done.19), channel_id=1, source_target_pairs={{0,6},{8,10},{2,0},{10,12},{4,2},{12,14},{6,4},{14,8},{1,7},{9,11}... | collective-permute-start | bytes 1572872 | tf_op jit(solution)/shard_map/ppermute | solution.py:41
  80.0 18.0 %collective-permute-start.23 = (bf16[1024,256]{1,0:T(8,128)(2,1)S(1)}, bf16[1024,256]{1,0:T(8,128)(2,1)S(1)}, u32[]{:S(2)}, u32[]{:S(2)}) collective-permute-start(bf16[1024,256]{1,0:T(8,128)(2,1)S(1)} %add_convert_fusion.12), channel_id=1, source_target_pairs={{0,1},{8,9},{2,3},{10,11},{4,5},{12,13},{6,7},{14,15},{1,0},{9,8},... | collective-permute-start | bytes 1572872 | tf_op jit(solution)/shard_map/ppermute | solution.py:41
  86.9 11.1 %collective-permute-start.22 = (bf16[1024,256]{1,0:T(8,128)(2,1)S(1)}, bf16[1024,256]{1,0:T(8,128)(2,1)S(1)}, u32[]{:S(2)}, u32[]{:S(2)}) collective-permute-start(bf16[1024,256]{1,0:T(8,128)(2,1)S(1)} %add_convert_fusion.11), channel_id=1, source_target_pairs={{0,6},{8,10},{2,0},{10,12},{4,2},{12,14},{6,4},{14,8},{1,7},{9,11}... | collective-permute-start | bytes 1572872 | tf_op jit(solution)/shard_map/ppermute | solution.py:41
  100.8 12.7 %collective-permute-start.28 = (bf16[1024,256]{1,0:T(8,128)(2,1)S(1)}, bf16[1024,256]{1,0:T(8,128)(2,1)S(1)}, u32[]{:S(2)}, u32[]{:S(2)}) collective-permute-start(bf16[1024,256]{1,0:T(8,128)(2,1)S(1)} %get-tuple-element.123.refs_0_), channel_id=1, source_target_pairs={{0,1},{8,9},{2,3},{10,11},{4,5},{12,13},{6,7},{14,15},{1,0},{9,8},... | collective-permute-start | bytes 1572872 | tf_op jit(solution)/shard_map/ppermute | solution.py:41
  102.2 12.6 %collective-permute-start.27 = (bf16[1024,256]{1,0:T(8,128)(2,1)S(1)}, bf16[1024,256]{1,0:T(8,128)(2,1)S(1)}, u32[]{:S(2)}, u32[]{:S(2)}) collective-permute-start(bf16[1024,256]{1,0:T(8,128)(2,1)S(1)} %collective-permute-done.26), channel_id=1, source_target_pairs={{0,2},{8,14},{2,4},{10,8},{4,6},{12,10},{6,0},{14,12},{1,3},{9,15}... | collective-permute-start | bytes 1572872 | tf_op jit(solution)/shard_map/ppermute | solution.py:41
  109.2 15.1 %collective-permute-start.34 = (bf16[1024,256]{1,0:T(8,128)(2,1)S(1)}, bf16[1024,256]{1,0:T(8,128)(2,1)S(1)}, u32[]{:S(2)}, u32[]{:S(2)}) collective-permute-start(bf16[1024,256]{1,0:T(8,128)(2,1)S(1)} %collective-permute-done.30.refs_2_), channel_id=1, source_target_pairs={{0,2},{8,14},{2,4},{10,8},{4,6},{12,10},{6,0},{14,12},{1,3},{9,15}... | collective-permute-start | bytes 1572872 | tf_op jit(solution)/shard_map/ppermute | solution.py:41
  114.8 9.5 %collective-permute-start.35 = (bf16[1024,256]{1,0:T(8,128)(2,1)S(1)}, bf16[1024,256]{1,0:T(8,128)(2,1)}, u32[]{:S(2)}, u32[]{:S(2)}) collective-permute-start(bf16[1024,256]{1,0:T(8,128)(2,1)S(1)} %collective-permute-done.28.refs_1_), channel_id=1, source_target_pairs={{0,8},{8,0},{2,10},{10,2},{4,12},{12,4},{6,14},{14,6},{1,9},{9,1},... | collective-permute-start | bytes 1572872 | tf_op jit(solution)/shard_map/ppermute | solution.py:41
  124.3 12.9 %collective-permute-start.38 = (bf16[1024,256]{1,0:T(8,128)(2,1)S(1)}, bf16[1024,256]{1,0:T(8,128)(2,1)S(1)}, u32[]{:S(2)}, u32[]{:S(2)}) collective-permute-start(bf16[1024,256]{1,0:T(8,128)(2,1)S(1)} %collective-permute-done.34.refs_6_), channel_id=1, source_target_pairs={{0,1},{8,9},{2,3},{10,11},{4,5},{12,13},{6,7},{14,15},{1,0},{9,8},... | collective-permute-start | bytes 1572872 | tf_op jit(solution)/shard_map/ppermute | solution.py:41
  125.1 12.2 %collective-permute-start.37 = (bf16[1024,256]{1,0:T(8,128)(2,1)}, bf16[1024,256]{1,0:T(8,128)(2,1)S(1)}, u32[]{:S(2)}, u32[]{:S(2)}) collective-permute-start(bf16[1024,256]{1,0:T(8,128)(2,1)} %collective-permute-done.35), channel_id=1, source_target_pairs={{0,2},{8,14},{2,4},{10,8},{4,6},{12,10},{6,0},{14,12},{1,3},{9,15}... | collective-permute-start | bytes 1572872 | tf_op jit(solution)/shard_map/ppermute | solution.py:41
  126.5 12.7 %collective-permute-start.31 = (bf16[1024,256]{1,0:T(8,128)(2,1)S(1)}, bf16[1024,256]{1,0:T(8,128)(2,1)S(1)}, u32[]{:S(2)}, u32[]{:S(2)}) collective-permute-start(bf16[1024,256]{1,0:T(8,128)(2,1)S(1)} %collective-permute-done.28.refs_1_), channel_id=1, source_target_pairs={{0,2},{8,14},{2,4},{10,8},{4,6},{12,10},{6,0},{14,12},{1,3},{9,15}... | collective-permute-start | bytes 1572872 | tf_op jit(solution)/shard_map/ppermute | solution.py:41
  126.6 12.1 %collective-permute-start.32 = (bf16[1024,256]{1,0:T(8,128)(2,1)S(1)}, bf16[1024,256]{1,0:T(8,128)(2,1)S(1)}, u32[]{:S(2)}, u32[]{:S(2)}) collective-permute-start(bf16[1024,256]{1,0:T(8,128)(2,1)S(1)} %collective-permute-done.27), channel_id=1, source_target_pairs={{0,8},{8,0},{2,10},{10,2},{4,12},{12,4},{6,14},{14,6},{1,9},{9,1},... | collective-permute-start | bytes 1572872 | tf_op jit(solution)/shard_map/ppermute | solution.py:41
  151.2 17.8 %collective-permute-start.43 = (bf16[1024,256]{1,0:T(8,128)(2,1)S(1)}, bf16[1024,256]{1,0:T(8,128)(2,1)S(1)}, u32[]{:S(2)}, u32[]{:S(2)}) collective-permute-start(bf16[1024,256]{1,0:T(8,128)(2,1)S(1)} %get-tuple-element.125), channel_id=1, source_target_pairs={{0,48},{8,24},{16,0},{24,40},{32,16},{40,56},{48,32},{56,8},{64,11... | collective-permute-start | bytes 1572872 | tf_op jit(solution)/shard_map/ppermute | solution.py:35
  156.0 21.3 %collective-permute-start.40 = (bf16[2048,256]{1,0:T(8,128)(2,1)S(1)}, bf16[2048,256]{1,0:T(8,128)(2,1)S(1)}, u32[]{:S(2)}, u32[]{:S(2)}) collective-permute-start(bf16[2048,256]{1,0:T(8,128)(2,1)S(1)} %get-tuple-element.98), channel_id=1, source_target_pairs={{0,8},{8,0},{16,24},{24,16},{32,40},{40,32},{48,56},{56,48},{64,72... | collective-permute-start | bytes 3145736 | tf_op jit(solution)/shard_map/ppermute | solution.py:35
  156.1 18.6 %collective-permute-start.46 = (bf16[1024,256]{1,0:T(8,128)(2,1)S(1)}, bf16[1024,256]{1,0:T(8,128)(2,1)S(1)}, u32[]{:S(2)}, u32[]{:S(2)}) collective-permute-start(bf16[1024,256]{1,0:T(8,128)(2,1)S(1)} %add_convert_fusion.8), channel_id=1, source_target_pairs={{0,64},{8,72},{16,80},{24,88},{32,96},{40,104},{48,112},{56,120},{... | collective-permute-start | bytes 1572872 | tf_op jit(solution)/shard_map/ppermute | solution.py:35
  163.1 14.4 %collective-permute-start.49 = (bf16[1024,256]{1,0:T(8,128)(2,1)S(1)}, bf16[1024,256]{1,0:T(8,128)(2,1)S(1)}, u32[]{:S(2)}, u32[]{:S(2)}) collective-permute-start(bf16[1024,256]{1,0:T(8,128)(2,1)S(1)} %get-tuple-element.124), channel_id=1, source_target_pairs={{0,48},{8,24},{16,0},{24,40},{32,16},{40,56},{48,32},{56,8},{64,11... | collective-permute-start | bytes 1572872 | tf_op jit(solution)/shard_map/ppermute | solution.py:35
  177.0 9.6 %collective-permute-start.48 = (bf16[1024,256]{1,0:T(8,128)(2,1)S(1)}, bf16[1024,256]{1,0:T(8,128)(2,1)S(1)}, u32[]{:S(2)}, u32[]{:S(2)}) collective-permute-start(bf16[1024,256]{1,0:T(8,128)(2,1)S(1)} %add_convert_fusion.7), channel_id=1, source_target_pairs={{0,48},{8,24},{16,0},{24,40},{32,16},{40,56},{48,32},{56,8},{64,11... | collective-permute-start | bytes 1572872 | tf_op jit(solution)/shard_map/ppermute | solution.py:35
  177.6 14.6 %collective-permute-start.54 = (bf16[1024,256]{1,0:T(8,128)(2,1)S(1)}, bf16[1024,256]{1,0:T(8,128)(2,1)S(1)}, u32[]{:S(2)}, u32[]{:S(2)}) collective-permute-start(bf16[1024,256]{1,0:T(8,128)(2,1)S(1)} %add_convert_fusion.6), channel_id=1, source_target_pairs={{0,48},{8,24},{16,0},{24,40},{32,16},{40,56},{48,32},{56,8},{64,11... | collective-permute-start | bytes 1572872 | tf_op jit(solution)/shard_map/ppermute | solution.py:35
  177.9 19.7 %collective-permute-start.52 = (bf16[1024,256]{1,0:T(8,128)(2,1)S(1)}, bf16[1024,256]{1,0:T(8,128)(2,1)S(1)}, u32[]{:S(2)}, u32[]{:S(2)}) collective-permute-start(bf16[1024,256]{1,0:T(8,128)(2,1)S(1)} %add_convert_fusion.3), channel_id=1, source_target_pairs={{0,64},{8,72},{16,80},{24,88},{32,96},{40,104},{48,112},{56,120},{... | collective-permute-start | bytes 1572872 | tf_op jit(solution)/shard_map/ppermute | solution.py:35
  188.7 9.3 %collective-permute-start.51 = (bf16[1024,256]{1,0:T(8,128)(2,1)S(1)}, bf16[1024,256]{1,0:T(8,128)(2,1)S(1)}, u32[]{:S(2)}, u32[]{:S(2)}) collective-permute-start(bf16[1024,256]{1,0:T(8,128)(2,1)S(1)} %add_convert_fusion.2), channel_id=1, source_target_pairs={{0,48},{8,24},{16,0},{24,40},{32,16},{40,56},{48,32},{56,8},{64,11... | collective-permute-start | bytes 1572872 | tf_op jit(solution)/shard_map/ppermute | solution.py:35
  (30 other events, 325.1 us)

commit v3 on v2

--- a/solution.py
+++ b/solution.py
@@ -8,8 +8,8 @@
 from jax.sharding import PartitionSpec as P
 
 BLK = 128
-UNROLL = 8
 CHUNK = 16
+LONG = 3
 
 
 def both_perms(move):
@@ -113,12 +113,12 @@
     near_b = over(other, OUT, kind)
     near_a, *extra = step(near_a, *extra)
     across = over(near_a, OUT, kind)
-    near_b, far, _ = meet(near_b, far, near_a)
+    near_b, _ = meet(near_b, near_a)
+    across, far, _ = step(across, far, near_b)
+    across_far = over(across, PAIR, kind)
     far_other = over(far, CORE, kind)
     far_a = over(far, OUT, kind)
     far_b = over(far_other, OUT, kind)
-    across, _ = step(across, far_other)
-    across_far = over(across, PAIR, kind)
     near_b_swapped = over(near_b, CORE, kind)
     if kind == "row":
         near_a_swapped = over(near_a, CORE, kind)
@@ -212,23 +212,31 @@
     for copy in piece_copies:
         copy.wait()
 
-    @pl.loop(0, n_chunks)
+    def run(first, n):
+        for slot in range(n):
+            slot = first + slot
+            out_at = pl.multiple_of(rows[slot] * BLK, BLK)
+            in_at = pl.multiple_of(cols[slot] * BLK, BLK)
+            dims = (((0,), (0,)), ((), ())) if transpose else (((1,), (0,)), ((), ()))
+            acc[pl.ds(out_at, BLK), :] += lax.dot_general(
+                blocks[slot],
+                table[pl.ds(in_at, BLK), :],
+                dims,
+                preferred_element_type=jnp.float32,
+            )
+
+    n_long = n_chunks // LONG
+
+    @pl.loop(0, n_long)
+    def _(i):
+        for chunk in range(LONG):
+            block_copy(i * LONG + chunk).wait()
+        run(i * LONG * CHUNK, LONG * CHUNK)
+
+    @pl.loop(n_long * LONG, n_chunks)
     def _(i):
         block_copy(i).wait()
-
-        @pl.loop(0, CHUNK // UNROLL)
-        def _(step):
-            for u in range(UNROLL):
-                slot = i * CHUNK + step * UNROLL + u
-                out_at = pl.multiple_of(rows[slot] * BLK, BLK)
-                in_at = pl.multiple_of(cols[slot] * BLK, BLK)
-                dims = (((0,), (0,)), ((), ())) if transpose else (((1,), (0,)), ((), ()))
-                acc[pl.ds(out_at, BLK), :] += lax.dot_general(
-                    blocks[slot],
-                    table[pl.ds(in_at, BLK), :],
-                    dims,
-                    preferred_element_type=jnp.float32,
-                )
+        run(i * CHUNK, CHUNK)
 
     at = 0
     for out in outs:

time: 200 us -> 188 us (0.940)
  starting transfers between devices: 80.1 us -> 62.8 us
  waiting for transfers between devices: 95.8 us -> 101 us
    ppermute x32, starting transfers between devices: 49.8 us -> 39.3 us  [over(): return lax.ppermute(v, 'row', perm[0])]
    ppermute x25, starting transfers between devices: 30.3 us -> 23.5 us  [over(): return lax.ppermute(v, ('row', 'col'), pairs)]
    ppermute x25, waiting for transfers between devices: 44.4 us -> 47.5 us  [over(): return lax.ppermute(v, ('row', 'col'), pairs)]
    ppermute x32, waiting for transfers between devices: 51.4 us -> 53.8 us  [over(): return lax.ppermute(v, 'row', perm[0])]
  transfers between devices with their start and end apart: 57 -> 57, of which waited for: 31 -> 33; matrix products, arithmetic and copies ran while one was open for 2% -> 3% of each run, Pallas kernels for 0% -> 0%
where the time goes in v3:
time: 188 us
  waiting for transfers between devices  101 us (54%)
  starting transfers between devices  62.8 us (33%)
  Pallas kernels  10.8 us (6%)
  local copies, waits for them, and re-layouts  4.49 us (2%)
  other arithmetic  4.05 us (2%)
  matrix products  3.04 us (2%)
    ppermute x32, waiting for transfers between devices, over(): return lax.ppermute(v, 'row', perm[0])  53.8 us
    ppermute x25, waiting for transfers between devices, over(): return lax.ppermute(v, ('row', 'col'), pairs)  47.5 us
    ppermute x32, starting transfers between devices, over(): return lax.ppermute(v, 'row', perm[0])  39.3 us
    ppermute x25, starting transfers between devices, over(): return lax.ppermute(v, ('row', 'col'), pairs)  23.5 us
    pallas_call x2, Pallas kernels, sparse(): pl.pallas_call(functools.partial(sparse_kernel, transpose, n_in), out_sha...  10.8 us
    unnamed x10, local copies, waits for them, and re-layouts  3.85 us
  transfers between devices with their start and end apart: 57, of which 33 were waited for; matrix products, arithmetic and copies ran while one was open for 3% of the time, Pallas kernels for 0%

profile of v3, /device:TPU:1, one launch (start us, length us, event | category | flops | bytes accessed | tf_op | source)
XLA Modules:
  0.0 188.2 jit_solution(11771968855079639564)
XLA Ops:
  2.1 2.6 %collective-permute-start = (bf16[1024,256]{1,0:T(8,128)(2,1)}, bf16[1024,256]{1,0:T(8,128)(2,1)S(1)}, u32[]{:S(2)}, u32[]{:S(2)}) collective-permute-start(bf16[1024,256]{1,0:T(8,128)(2,1)} %bitcast.25), channel_id=1, source_target_pairs={{0,16},{8,56},{16,32},{24,8},{32,48},{40,24},{48,0},{56,40},{64,80... | collective-permute-start | bytes 1572872 | tf_op jit(solution)/shard_map/ppermute | solution.py:35
  4.7 3.6 %collective-permute-start.3 = (bf16[1024,256]{1,0:T(8,128)(2,1)}, bf16[1024,256]{1,0:T(8,128)(2,1)S(1)}, u32[]{:S(2)}, u32[]{:S(2)}) collective-permute-start(bf16[1024,256]{1,0:T(8,128)(2,1)} %bitcast.26), channel_id=1, source_target_pairs={{0,64},{8,72},{16,80},{24,88},{32,96},{40,104},{48,112},{56,120},{... | collective-permute-start | bytes 1572872 | tf_op jit(solution)/shard_map/ppermute | solution.py:35
  11.2 3.3 %collective-permute-start.2 = (bf16[1024,256]{1,0:T(8,128)(2,1)S(1)}, bf16[1024,256]{1,0:T(8,128)(2,1)S(1)}, u32[]{:S(2)}, u32[]{:S(2)}) collective-permute-start(bf16[1024,256]{1,0:T(8,128)(2,1)S(1)} %collective-permute-done.refs_4_), channel_id=1, source_target_pairs={{0,16},{8,56},{16,32},{24,8},{32,48},{40,24},{48,0},{56,40},{64,80... | collective-permute-start | bytes 1572872 | tf_op jit(solution)/shard_map/ppermute | solution.py:35
  14.5 3.0 %collective-permute-done.4.refs_5_ = bf16[1024,256]{1,0:T(8,128)(2,1)S(1)} collective-permute-done((bf16[1024,256]{1,0:T(8,128)(2,1)S(1)}, bf16[1024,256]{1,0:T(8,128)(2,1)S(1)}, u32[]{:S(2)}, u32[]{:S(2)}) %collective-permute-start.4) | collective-permute-done | bytes 524320 | tf_op jit(solution)/shard_map/ppermute | solution.py:35
  17.4 2.6 %collective-permute-done.3.refs_2_ = bf16[1024,256]{1,0:T(8,128)(2,1)S(1)} collective-permute-done((bf16[1024,256]{1,0:T(8,128)(2,1)}, bf16[1024,256]{1,0:T(8,128)(2,1)S(1)}, u32[]{:S(2)}, u32[]{:S(2)}) %collective-permute-start.3) | collective-permute-done | bytes 524320 | tf_op jit(solution)/shard_map/ppermute | solution.py:35
  20.0 3.0 %collective-permute-done.2.refs_12_ = bf16[1024,256]{1,0:T(8,128)(2,1)S(1)} collective-permute-done((bf16[1024,256]{1,0:T(8,128)(2,1)S(1)}, bf16[1024,256]{1,0:T(8,128)(2,1)S(1)}, u32[]{:S(2)}, u32[]{:S(2)}) %collective-permute-start.2) | collective-permute-done | bytes 524320 | tf_op jit(solution)/shard_map/ppermute | solution.py:35
  25.4 3.6 %collective-permute-start.8 = (bf16[1024,256]{1,0:T(8,128)(2,1)S(1)}, bf16[1024,256]{1,0:T(8,128)(2,1)S(1)}, u32[]{:S(2)}, u32[]{:S(2)}) collective-permute-start(bf16[1024,256]{1,0:T(8,128)(2,1)S(1)} %collective-permute-done.2.refs_12_), channel_id=1, source_target_pairs={{0,64},{8,72},{16,80},{24,88},{32,96},{40,104},{48,112},{56,120},{... | collective-permute-start | bytes 1572872 | tf_op jit(solution)/shard_map/ppermute | solution.py:35
  30.1 2.7 %collective-permute-done.6.refs_6_ = bf16[1024,256]{1,0:T(8,128)(2,1)S(1)} collective-permute-done((bf16[1024,256]{1,0:T(8,128)(2,1)S(1)}, bf16[1024,256]{1,0:T(8,128)(2,1)S(1)}, u32[]{:S(2)}, u32[]{:S(2)}) %collective-permute-start.6) | collective-permute-done | bytes 524320 | tf_op jit(solution)/shard_map/ppermute | solution.py:35
  34.9 5.5 %collective-permute-done.8.refs_13_ = bf16[1024,256]{1,0:T(8,128)(2,1)S(1)} collective-permute-done((bf16[1024,256]{1,0:T(8,128)(2,1)S(1)}, bf16[1024,256]{1,0:T(8,128)(2,1)S(1)}, u32[]{:S(2)}, u32[]{:S(2)}) %collective-permute-start.8) | collective-permute-done | bytes 524320 | tf_op jit(solution)/shard_map/ppermute | solution.py:35
  43.8 2.8 %copy-done.1 = bf16[1,1,192,128,128]{4,3,2,1,0:T(8,128)(2,1)S(1)} copy-done((bf16[1,1,192,128,128]{4,3,2,1,0:T(8,128)(2,1)S(1)}, bf16[1,1,192,128,128]{4,3,2,1,0:T(8,128)(2,1)}, u32[]{:S(2)}) %copy-start.1) | copy-done | bytes 6291480
  47.6 5.0 %sparse_forward.1 = (bf16[1024,256]{1,0:T(8,128)(2,1)S(1)}, bf16[1024,256]{1,0:T(8,128)(2,1)S(1)}, bf16[1024,256]{1,0:T(8,128)(2,1)S(1)}, bf16[1024,256]{1,0:T(8...) custom-call(s32[192]{0:T(256)S(1)} %get-tuple-element.63.rows.cols, ...), custom_call_target="tpu_custom_call" | custom-call | flops 1610612736 | bytes 18874368 | tf_op jit(solution)/shard_map/sparse_forward/pallas_call | solution.py:257
  54.6 3.5 %collective-permute-start.17 = (bf16[1024,256]{1,0:T(8,128)(2,1)S(1)}, bf16[1024,256]{1,0:T(8,128)(2,1)S(1)}, u32[]{:S(2)}, u32[]{:S(2)}) collective-permute-start(bf16[1024,256]{1,0:T(8,128)(2,1)S(1)} %collective-permute-done.16), channel_id=1, source_target_pairs={{0,6},{8,10},{2,0},{10,12},{4,2},{12,14},{6,4},{14,8},{1,7},{9,11}... | collective-permute-start | bytes 1572872 | tf_op jit(solution)/shard_map/ppermute | solution.py:41
  60.3 4.0 %collective-permute-done.17 = bf16[1024,256]{1,0:T(8,128)(2,1)S(1)} collective-permute-done((bf16[1024,256]{1,0:T(8,128)(2,1)S(1)}, bf16[1024,256]{1,0:T(8,128)(2,1)S(1)}, u32[]{:S(2)}, u32[]{:S(2)}) %collective-permute-start.17) | collective-permute-done | bytes 524320 | tf_op jit(solution)/shard_map/ppermute | solution.py:41
  65.7 5.5 %collective-permute-done.15 = bf16[1024,256]{1,0:T(8,128)(2,1)S(1)} collective-permute-done((bf16[1024,256]{1,0:T(8,128)(2,1)S(1)}, bf16[1024,256]{1,0:T(8,128)(2,1)S(1)}, u32[]{:S(2)}, u32[]{:S(2)}) %collective-permute-start.15) | collective-permute-done | bytes 524320 | tf_op jit(solution)/shard_map/ppermute | solution.py:41
  73.7 7.0 %collective-permute-done.18 = bf16[1024,256]{1,0:T(8,128)(2,1)S(1)} collective-permute-done((bf16[1024,256]{1,0:T(8,128)(2,1)S(1)}, bf16[1024,256]{1,0:T(8,128)(2,1)S(1)}, u32[]{:S(2)}, u32[]{:S(2)}) %collective-permute-start.18) | collective-permute-done | bytes 524320 | tf_op jit(solution)/shard_map/ppermute | solution.py:41
  81.5 4.9 %collective-permute-done.24 = bf16[1024,256]{1,0:T(8,128)(2,1)S(1)} collective-permute-done((bf16[1024,256]{1,0:T(8,128)(2,1)S(1)}, bf16[1024,256]{1,0:T(8,128)(2,1)S(1)}, u32[]{:S(2)}, u32[]{:S(2)}) %collective-permute-start.24) | collective-permute-done | bytes 524320 | tf_op jit(solution)/shard_map/ppermute | solution.py:41
  86.6 5.3 %collective-permute-done.22 = bf16[1024,256]{1,0:T(8,128)(2,1)S(1)} collective-permute-done((bf16[1024,256]{1,0:T(8,128)(2,1)S(1)}, bf16[1024,256]{1,0:T(8,128)(2,1)S(1)}, u32[]{:S(2)}, u32[]{:S(2)}) %collective-permute-start.22) | collective-permute-done | bytes 524320 | tf_op jit(solution)/shard_map/ppermute | solution.py:41
  93.9 3.4 %collective-permute-start.27 = (bf16[1024,256]{1,0:T(8,128)(2,1)S(1)}, bf16[1024,256]{1,0:T(8,128)(2,1)S(1)}, u32[]{:S(2)}, u32[]{:S(2)}) collective-permute-start(bf16[1024,256]{1,0:T(8,128)(2,1)S(1)} %get-tuple-element.123.refs_0_), channel_id=1, source_target_pairs={{0,2},{8,14},{2,4},{10,8},{4,6},{12,10},{6,0},{14,12},{1,3},{9,15}... | collective-permute-start | bytes 1572872 | tf_op jit(solution)/shard_map/ppermute | solution.py:41
  99.4 4.0 %collective-permute-done.27.refs_2_ = bf16[1024,256]{1,0:T(8,128)(2,1)S(1)} collective-permute-done((bf16[1024,256]{1,0:T(8,128)(2,1)S(1)}, bf16[1024,256]{1,0:T(8,128)(2,1)S(1)}, u32[]{:S(2)}, u32[]{:S(2)}) %collective-permute-start.27) | collective-permute-done | bytes 524320 | tf_op jit(solution)/shard_map/ppermute | solution.py:41
  103.5 3.1 %collective-permute-start.29 = (bf16[1024,256]{1,0:T(8,128)(2,1)S(1)}, bf16[1024,256]{1,0:T(8,128)(2,1)S(1)}, u32[]{:S(2)}, u32[]{:S(2)}) collective-permute-start(bf16[1024,256]{1,0:T(8,128)(2,1)S(1)} %collective-permute-done.27.refs_2_), channel_id=1, source_target_pairs={{0,2},{8,14},{2,4},{10,8},{4,6},{12,10},{6,0},{14,12},{1,3},{9,15}... | collective-permute-start | bytes 1572872 | tf_op jit(solution)/shard_map/ppermute | solution.py:41
  106.6 3.5 %collective-permute-start.28 = (f32[136,256]{1,0:T(8,128)S(1)}, f32[136,256]{1,0:T(8,128)S(1)}, u32[]{:S(2)}, u32[]{:S(2)}) collective-permute-start(f32[136,256]{1,0:T(8,128)S(1)} %dynamic-slice_add_fusion), channel_id=1, source_target_pairs={{0,64},{8,72},{16,80},{24,88},{32,96},{40,104},{48,112},{56,120},{... | collective-permute-start | bytes 417800 | tf_op jit(solution)/shard_map/ppermute | solution.py:35
  111.1 6.2 %collective-permute-done.28 = f32[136,256]{1,0:T(8,128)S(1)} collective-permute-done((f32[136,256]{1,0:T(8,128)S(1)}, f32[136,256]{1,0:T(8,128)S(1)}, u32[]{:S(2)}, u32[]{:S(2)}) %collective-permute-start.28) | collective-permute-done | bytes 139296 | tf_op jit(solution)/shard_map/ppermute | solution.py:35
  121.5 3.0 %collective-permute-start.33 = (bf16[1024,256]{1,0:T(8,128)(2,1)S(1)}, bf16[1024,256]{1,0:T(8,128)(2,1)S(1)}, u32[]{:S(2)}, u32[]{:S(2)}) collective-permute-start(bf16[1024,256]{1,0:T(8,128)(2,1)S(1)} %collective-permute-done.30.refs_1_), channel_id=1, source_target_pairs={{0,2},{8,14},{2,4},{10,8},{4,6},{12,10},{6,0},{14,12},{1,3},{9,15}... | collective-permute-start | bytes 1572872 | tf_op jit(solution)/shard_map/ppermute | solution.py:41
  125.1 7.0 %collective-permute-done.38.refs_7_ = bf16[1024,256]{1,0:T(8,128)(2,1)S(1)} collective-permute-done((bf16[1024,256]{1,0:T(8,128)(2,1)S(1)}, bf16[1024,256]{1,0:T(8,128)(2,1)S(1)}, u32[]{:S(2)}, u32[]{:S(2)}) %collective-permute-start.38) | collective-permute-done | bytes 524320 | tf_op jit(solution)/shard_map/ppermute | solution.py:41
  134.4 5.8 %sparse_back.1 = (bf16[1024,256]{1,0:T(8,128)(2,1)S(1)}, bf16[1024,256]{1,0:T(8,128)(2,1)S(1)}, bf16[1024,256]{1,0:T(8,128)(2,1)S(1)}, bf16[1024,256]{1,0:T(8,12...) custom-call(s32[192]{0:T(256)S(1)} %get-tuple-element.64.cols.rows, ...), custom_call_target="tpu_custom_call" | custom-call | flops 1610612736 | bytes 18874368 | tf_op jit(solution)/shard_map/sparse_back/pallas_call | solution.py:257
  141.5 2.2 %collective-permute-done.42 = bf16[2048,256]{1,0:T(8,128)(2,1)S(1)} collective-permute-done((bf16[2048,256]{1,0:T(8,128)(2,1)S(1)}, bf16[2048,256]{1,0:T(8,128)(2,1)S(1)}, u32[]{:S(2)}, u32[]{:S(2)}) %collective-permute-start.42) | collective-permute-done | bytes 1048608 | tf_op jit(solution)/shard_map/ppermute | solution.py:35
  143.9 3.8 %collective-permute-start.43 = (bf16[1024,256]{1,0:T(8,128)(2,1)S(1)}, bf16[1024,256]{1,0:T(8,128)(2,1)S(1)}, u32[]{:S(2)}, u32[]{:S(2)}) collective-permute-start(bf16[1024,256]{1,0:T(8,128)(2,1)S(1)} %get-tuple-element.125), channel_id=1, source_target_pairs={{0,48},{8,24},{16,0},{24,40},{32,16},{40,56},{48,32},{56,8},{64,11... | collective-permute-start | bytes 1572872 | tf_op jit(solution)/shard_map/ppermute | solution.py:35
  151.7 7.9 %collective-permute-done.41 = f32[136,256]{1,0:T(8,128)S(1)} collective-permute-done((f32[136,256]{1,0:T(8,128)S(1)}, f32[136,256]{1,0:T(8,128)S(1)}, u32[]{:S(2)}, u32[]{:S(2)}) %collective-permute-start.41) | collective-permute-done | bytes 139296 | tf_op jit(solution)/shard_map/ppermute | solution.py:35
  160.3 4.3 %collective-permute-done.46 = bf16[1024,256]{1,0:T(8,128)(2,1)S(1)} collective-permute-done((bf16[1024,256]{1,0:T(8,128)(2,1)S(1)}, bf16[1024,256]{1,0:T(8,128)(2,1)S(1)}, u32[]{:S(2)}, u32[]{:S(2)}) %collective-permute-start.46) | collective-permute-done | bytes 524320 | tf_op jit(solution)/shard_map/ppermute | solution.py:35
  167.1 2.4 %collective-permute-start.52 = (bf16[1024,256]{1,0:T(8,128)(2,1)S(1)}, bf16[1024,256]{1,0:T(8,128)(2,1)S(1)}, u32[]{:S(2)}, u32[]{:S(2)}) collective-permute-start(bf16[1024,256]{1,0:T(8,128)(2,1)S(1)} %add_convert_fusion.3), channel_id=1, source_target_pairs={{0,64},{8,72},{16,80},{24,88},{32,96},{40,104},{48,112},{56,120},{... | collective-permute-start | bytes 1572872 | tf_op jit(solution)/shard_map/ppermute | solution.py:35
  170.9 5.1 %collective-permute-done.48 = bf16[1024,256]{1,0:T(8,128)(2,1)S(1)} collective-permute-done((bf16[1024,256]{1,0:T(8,128)(2,1)S(1)}, bf16[1024,256]{1,0:T(8,128)(2,1)S(1)}, u32[]{:S(2)}, u32[]{:S(2)}) %collective-permute-start.48) | collective-permute-done | bytes 524320 | tf_op jit(solution)/shard_map/ppermute | solution.py:35
  176.4 5.2 %collective-permute-done.54 = bf16[1024,256]{1,0:T(8,128)(2,1)S(1)} collective-permute-done((bf16[1024,256]{1,0:T(8,128)(2,1)S(1)}, bf16[1024,256]{1,0:T(8,128)(2,1)S(1)}, u32[]{:S(2)}, u32[]{:S(2)}) %collective-permute-start.54) | collective-permute-done | bytes 524320 | tf_op jit(solution)/shard_map/ppermute | solution.py:35
  (123 shorter events, 51.8 us)
Async XLA Ops:
  4.7 15.3 %collective-permute-start.3 = (bf16[1024,256]{1,0:T(8,128)(2,1)}, bf16[1024,256]{1,0:T(8,128)(2,1)S(1)}, u32[]{:S(2)}, u32[]{:S(2)}) collective-permute-start(bf16[1024,256]{1,0:T(8,128)(2,1)} %bitcast.26), channel_id=1, source_target_pairs={{0,64},{8,72},{16,80},{24,88},{32,96},{40,104},{48,112},{56,120},{... | collective-permute-start | bytes 1572872 | tf_op jit(solution)/shard_map/ppermute | solution.py:35
  11.2 11.9 %collective-permute-start.2 = (bf16[1024,256]{1,0:T(8,128)(2,1)S(1)}, bf16[1024,256]{1,0:T(8,128)(2,1)S(1)}, u32[]{:S(2)}, u32[]{:S(2)}) collective-permute-start(bf16[1024,256]{1,0:T(8,128)(2,1)S(1)} %collective-permute-done.refs_4_), channel_id=1, source_target_pairs={{0,16},{8,56},{16,32},{24,8},{32,48},{40,24},{48,0},{56,40},{64,80... | collective-permute-start | bytes 1572872 | tf_op jit(solution)/shard_map/ppermute | solution.py:35
  25.4 15.0 %collective-permute-start.8 = (bf16[1024,256]{1,0:T(8,128)(2,1)S(1)}, bf16[1024,256]{1,0:T(8,128)(2,1)S(1)}, u32[]{:S(2)}, u32[]{:S(2)}) collective-permute-start(bf16[1024,256]{1,0:T(8,128)(2,1)S(1)} %collective-permute-done.2.refs_12_), channel_id=1, source_target_pairs={{0,64},{8,72},{16,80},{24,88},{32,96},{40,104},{48,112},{56,120},{... | collective-permute-start | bytes 1572872 | tf_op jit(solution)/shard_map/ppermute | solution.py:35
  29.0 11.4 %collective-permute-start.7 = (bf16[1024,256]{1,0:T(8,128)(2,1)S(1)}, bf16[1024,256]{1,0:T(8,128)(2,1)S(1)}, u32[]{:S(2)}, u32[]{:S(2)}) collective-permute-start(bf16[1024,256]{1,0:T(8,128)(2,1)S(1)} %collective-permute-done.5.refs_3_), channel_id=1, source_target_pairs={{0,16},{8,56},{16,32},{24,8},{32,48},{40,24},{48,0},{56,40},{64,80... | collective-permute-start | bytes 1572872 | tf_op jit(solution)/shard_map/ppermute | solution.py:35
  29.6 11.3 %collective-permute-start.9 = (bf16[1024,256]{1,0:T(8,128)(2,1)S(1)}, bf16[1024,256]{1,0:T(8,128)(2,1)S(1)}, u32[]{:S(2)}, u32[]{:S(2)}) collective-permute-start(bf16[1024,256]{1,0:T(8,128)(2,1)S(1)} %collective-permute-done.refs_4_), channel_id=1, source_target_pairs={{0,8},{8,0},{16,24},{24,16},{32,40},{40,32},{48,56},{56,48},{64,72... | collective-permute-start | bytes 1572872 | tf_op jit(solution)/shard_map/ppermute | solution.py:35
  29.8 11.8 %collective-permute-start.10 = (bf16[1024,256]{1,0:T(8,128)(2,1)S(1)}, bf16[1024,256]{1,0:T(8,128)(2,1)S(1)}, u32[]{:S(2)}, u32[]{:S(2)}) collective-permute-start(bf16[1024,256]{1,0:T(8,128)(2,1)S(1)} %collective-permute-done.4.refs_5_), channel_id=1, source_target_pairs={{0,8},{8,0},{16,24},{24,16},{32,40},{40,32},{48,56},{56,48},{64,72... | collective-permute-start | bytes 1572872 | tf_op jit(solution)/shard_map/ppermute | solution.py:35
  54.6 9.7 %collective-permute-start.17 = (bf16[1024,256]{1,0:T(8,128)(2,1)S(1)}, bf16[1024,256]{1,0:T(8,128)(2,1)S(1)}, u32[]{:S(2)}, u32[]{:S(2)}) collective-permute-start(bf16[1024,256]{1,0:T(8,128)(2,1)S(1)} %collective-permute-done.16), channel_id=1, source_target_pairs={{0,6},{8,10},{2,0},{10,12},{4,2},{12,14},{6,4},{14,8},{1,7},{9,11}... | collective-permute-start | bytes 1572872 | tf_op jit(solution)/shard_map/ppermute | solution.py:41
  58.2 13.1 %collective-permute-start.15 = (bf16[1024,256]{1,0:T(8,128)(2,1)S(1)}, bf16[1024,256]{1,0:T(8,128)(2,1)S(1)}, u32[]{:S(2)}, u32[]{:S(2)}) collective-permute-start(bf16[1024,256]{1,0:T(8,128)(2,1)S(1)} %get-tuple-element.75), channel_id=1, source_target_pairs={{0,1},{8,9},{2,3},{10,11},{4,5},{12,13},{6,7},{14,15},{1,0},{9,8},... | collective-permute-start | bytes 1572872 | tf_op jit(solution)/shard_map/ppermute | solution.py:41
  59.5 13.5 %collective-permute-start.19 = (bf16[1024,256]{1,0:T(8,128)(2,1)S(1)}, bf16[1024,256]{1,0:T(8,128)(2,1)S(1)}, u32[]{:S(2)}, u32[]{:S(2)}) collective-permute-start(bf16[1024,256]{1,0:T(8,128)(2,1)S(1)} %get-tuple-element.79), channel_id=1, source_target_pairs={{0,8},{8,0},{2,10},{10,2},{4,12},{12,4},{6,14},{14,6},{1,9},{9,1},... | collective-permute-start | bytes 1572872 | tf_op jit(solution)/shard_map/ppermute | solution.py:41
  59.5 13.5 %collective-permute-start.20 = (bf16[1024,256]{1,0:T(8,128)(2,1)S(1)}, bf16[1024,256]{1,0:T(8,128)(2,1)S(1)}, u32[]{:S(2)}, u32[]{:S(2)}) collective-permute-start(bf16[1024,256]{1,0:T(8,128)(2,1)S(1)} %get-tuple-element.80), channel_id=1, source_target_pairs={{0,6},{8,10},{2,0},{10,12},{4,2},{12,14},{6,4},{14,8},{1,7},{9,11}... | collective-permute-start | bytes 1572872 | tf_op jit(solution)/shard_map/ppermute | solution.py:41
  71.4 9.3 %collective-permute-start.18 = (bf16[1024,256]{1,0:T(8,128)(2,1)S(1)}, bf16[1024,256]{1,0:T(8,128)(2,1)S(1)}, u32[]{:S(2)}, u32[]{:S(2)}) collective-permute-start(bf16[1024,256]{1,0:T(8,128)(2,1)S(1)} %add_convert_fusion.13), channel_id=1, source_target_pairs={{0,6},{8,10},{2,0},{10,12},{4,2},{12,14},{6,4},{14,8},{1,7},{9,11}... | collective-permute-start | bytes 1572872 | tf_op jit(solution)/shard_map/ppermute | solution.py:41
  72.9 13.4 %collective-permute-start.24 = (bf16[1024,256]{1,0:T(8,128)(2,1)S(1)}, bf16[1024,256]{1,0:T(8,128)(2,1)S(1)}, u32[]{:S(2)}, u32[]{:S(2)}) collective-permute-start(bf16[1024,256]{1,0:T(8,128)(2,1)S(1)} %collective-permute-done.19), channel_id=1, source_target_pairs={{0,6},{8,10},{2,0},{10,12},{4,2},{12,14},{6,4},{14,8},{1,7},{9,11}... | collective-permute-start | bytes 1572872 | tf_op jit(solution)/shard_map/ppermute | solution.py:41
  73.3 18.7 %collective-permute-start.23 = (bf16[1024,256]{1,0:T(8,128)(2,1)S(1)}, bf16[1024,256]{1,0:T(8,128)(2,1)S(1)}, u32[]{:S(2)}, u32[]{:S(2)}) collective-permute-start(bf16[1024,256]{1,0:T(8,128)(2,1)S(1)} %add_convert_fusion.12), channel_id=1, source_target_pairs={{0,1},{8,9},{2,3},{10,11},{4,5},{12,13},{6,7},{14,15},{1,0},{9,8},... | collective-permute-start | bytes 1572872 | tf_op jit(solution)/shard_map/ppermute | solution.py:41
  80.8 11.1 %collective-permute-start.22 = (bf16[1024,256]{1,0:T(8,128)(2,1)S(1)}, bf16[1024,256]{1,0:T(8,128)(2,1)S(1)}, u32[]{:S(2)}, u32[]{:S(2)}) collective-permute-start(bf16[1024,256]{1,0:T(8,128)(2,1)S(1)} %add_convert_fusion.11), channel_id=1, source_target_pairs={{0,6},{8,10},{2,0},{10,12},{4,2},{12,14},{6,4},{14,8},{1,7},{9,11}... | collective-permute-start | bytes 1572872 | tf_op jit(solution)/shard_map/ppermute | solution.py:41
  93.9 9.5 %collective-permute-start.27 = (bf16[1024,256]{1,0:T(8,128)(2,1)S(1)}, bf16[1024,256]{1,0:T(8,128)(2,1)S(1)}, u32[]{:S(2)}, u32[]{:S(2)}) collective-permute-start(bf16[1024,256]{1,0:T(8,128)(2,1)S(1)} %get-tuple-element.123.refs_0_), channel_id=1, source_target_pairs={{0,2},{8,14},{2,4},{10,8},{4,6},{12,10},{6,0},{14,12},{1,3},{9,15}... | collective-permute-start | bytes 1572872 | tf_op jit(solution)/shard_map/ppermute | solution.py:41
  97.9 13.2 %collective-permute-start.30 = (bf16[1024,256]{1,0:T(8,128)(2,1)S(1)}, bf16[1024,256]{1,0:T(8,128)(2,1)S(1)}, u32[]{:S(2)}, u32[]{:S(2)}) collective-permute-start(bf16[1024,256]{1,0:T(8,128)(2,1)S(1)} %get-tuple-element.123.refs_0_), channel_id=1, source_target_pairs={{0,1},{8,9},{2,3},{10,11},{4,5},{12,13},{6,7},{14,15},{1,0},{9,8},... | collective-permute-start | bytes 1572872 | tf_op jit(solution)/shard_map/ppermute | solution.py:41
  99.1 11.0 %collective-permute-start.32 = (bf16[1024,256]{1,0:T(8,128)(2,1)}, bf16[1024,256]{1,0:T(8,128)(2,1)S(1)}, u32[]{:S(2)}, u32[]{:S(2)}) collective-permute-start(bf16[1024,256]{1,0:T(8,128)(2,1)} %collective-permute-done.31), channel_id=1, source_target_pairs={{0,2},{8,14},{2,4},{10,8},{4,6},{12,10},{6,0},{14,12},{1,3},{9,15}... | collective-permute-start | bytes 1572872 | tf_op jit(solution)/shard_map/ppermute | solution.py:41
  103.5 13.8 %collective-permute-start.29 = (bf16[1024,256]{1,0:T(8,128)(2,1)S(1)}, bf16[1024,256]{1,0:T(8,128)(2,1)S(1)}, u32[]{:S(2)}, u32[]{:S(2)}) collective-permute-start(bf16[1024,256]{1,0:T(8,128)(2,1)S(1)} %collective-permute-done.27.refs_2_), channel_id=1, source_target_pairs={{0,2},{8,14},{2,4},{10,8},{4,6},{12,10},{6,0},{14,12},{1,3},{9,15}... | collective-permute-start | bytes 1572872 | tf_op jit(solution)/shard_map/ppermute | solution.py:41
  106.6 10.7 %collective-permute-start.28 = (f32[136,256]{1,0:T(8,128)S(1)}, f32[136,256]{1,0:T(8,128)S(1)}, u32[]{:S(2)}, u32[]{:S(2)}) collective-permute-start(f32[136,256]{1,0:T(8,128)S(1)} %dynamic-slice_add_fusion), channel_id=1, source_target_pairs={{0,64},{8,72},{16,80},{24,88},{32,96},{40,104},{48,112},{56,120},{... | collective-permute-start | bytes 417800 | tf_op jit(solution)/shard_map/ppermute | solution.py:35
  118.5 13.6 %collective-permute-start.38 = (bf16[1024,256]{1,0:T(8,128)(2,1)S(1)}, bf16[1024,256]{1,0:T(8,128)(2,1)S(1)}, u32[]{:S(2)}, u32[]{:S(2)}) collective-permute-start(bf16[1024,256]{1,0:T(8,128)(2,1)S(1)} %collective-permute-done.29.refs_6_), channel_id=1, source_target_pairs={{0,1},{8,9},{2,3},{10,11},{4,5},{12,13},{6,7},{14,15},{1,0},{9,8},... | collective-permute-start | bytes 1572872 | tf_op jit(solution)/shard_map/ppermute | solution.py:41
  120.1 12.0 %collective-permute-start.37 = (bf16[1024,256]{1,0:T(8,128)(2,1)S(1)}, bf16[1024,256]{1,0:T(8,128)(2,1)S(1)}, u32[]{:S(2)}, u32[]{:S(2)}) collective-permute-start(bf16[1024,256]{1,0:T(8,128)(2,1)S(1)} %collective-permute-done.36), channel_id=1, source_target_pairs={{0,2},{8,14},{2,4},{10,8},{4,6},{12,10},{6,0},{14,12},{1,3},{9,15}... | collective-permute-start | bytes 1572872 | tf_op jit(solution)/shard_map/ppermute | solution.py:41
  121.3 11.5 %collective-permute-start.34 = (bf16[1024,256]{1,0:T(8,128)(2,1)S(1)}, bf16[1024,256]{1,0:T(8,128)(2,1)S(1)}, u32[]{:S(2)}, u32[]{:S(2)}) collective-permute-start(bf16[1024,256]{1,0:T(8,128)(2,1)S(1)} %collective-permute-done.32), channel_id=1, source_target_pairs={{0,8},{8,0},{2,10},{10,2},{4,12},{12,4},{6,14},{14,6},{1,9},{9,1},... | collective-permute-start | bytes 1572872 | tf_op jit(solution)/shard_map/ppermute | solution.py:41
  121.5 12.5 %collective-permute-start.33 = (bf16[1024,256]{1,0:T(8,128)(2,1)S(1)}, bf16[1024,256]{1,0:T(8,128)(2,1)S(1)}, u32[]{:S(2)}, u32[]{:S(2)}) collective-permute-start(bf16[1024,256]{1,0:T(8,128)(2,1)S(1)} %collective-permute-done.30.refs_1_), channel_id=1, source_target_pairs={{0,2},{8,14},{2,4},{10,8},{4,6},{12,10},{6,0},{14,12},{1,3},{9,15}... | collective-permute-start | bytes 1572872 | tf_op jit(solution)/shard_map/ppermute | solution.py:41
  143.9 15.7 %collective-permute-start.43 = (bf16[1024,256]{1,0:T(8,128)(2,1)S(1)}, bf16[1024,256]{1,0:T(8,128)(2,1)S(1)}, u32[]{:S(2)}, u32[]{:S(2)}) collective-permute-start(bf16[1024,256]{1,0:T(8,128)(2,1)S(1)} %get-tuple-element.125), channel_id=1, source_target_pairs={{0,48},{8,24},{16,0},{24,40},{32,16},{40,56},{48,32},{56,8},{64,11... | collective-permute-start | bytes 1572872 | tf_op jit(solution)/shard_map/ppermute | solution.py:35
  147.7 18.7 %collective-permute-start.40 = (bf16[2048,256]{1,0:T(8,128)(2,1)S(1)}, bf16[2048,256]{1,0:T(8,128)(2,1)S(1)}, u32[]{:S(2)}, u32[]{:S(2)}) collective-permute-start(bf16[2048,256]{1,0:T(8,128)(2,1)S(1)} %get-tuple-element.98), channel_id=1, source_target_pairs={{0,8},{8,0},{16,24},{24,16},{32,40},{40,32},{48,56},{56,48},{64,72... | collective-permute-start | bytes 3145736 | tf_op jit(solution)/shard_map/ppermute | solution.py:35
  149.4 15.1 %collective-permute-start.46 = (bf16[1024,256]{1,0:T(8,128)(2,1)S(1)}, bf16[1024,256]{1,0:T(8,128)(2,1)S(1)}, u32[]{:S(2)}, u32[]{:S(2)}) collective-permute-start(bf16[1024,256]{1,0:T(8,128)(2,1)S(1)} %add_convert_fusion.8), channel_id=1, source_target_pairs={{0,64},{8,72},{16,80},{24,88},{32,96},{40,104},{48,112},{56,120},{... | collective-permute-start | bytes 1572872 | tf_op jit(solution)/shard_map/ppermute | solution.py:35
  149.5 10.1 %collective-permute-start.41 = (f32[136,256]{1,0:T(8,128)S(1)}, f32[136,256]{1,0:T(8,128)S(1)}, u32[]{:S(2)}, u32[]{:S(2)}) collective-permute-start(f32[136,256]{1,0:T(8,128)S(1)} %add.222), channel_id=1, source_target_pairs={{0,32},{8,40},{16,48},{24,56},{32,0},{40,8},{48,16},{56,24},{64,96... | collective-permute-start | bytes 417800 | tf_op jit(solution)/shard_map/ppermute | solution.py:35
  150.6 16.1 %collective-permute-start.49 = (bf16[1024,256]{1,0:T(8,128)(2,1)S(1)}, bf16[1024,256]{1,0:T(8,128)(2,1)S(1)}, u32[]{:S(2)}, u32[]{:S(2)}) collective-permute-start(bf16[1024,256]{1,0:T(8,128)(2,1)S(1)} %get-tuple-element.124), channel_id=1, source_target_pairs={{0,48},{8,24},{16,0},{24,40},{32,16},{40,56},{48,32},{56,8},{64,11... | collective-permute-start | bytes 1572872 | tf_op jit(solution)/shard_map/ppermute | solution.py:35
  166.4 9.6 %collective-permute-start.48 = (bf16[1024,256]{1,0:T(8,128)(2,1)S(1)}, bf16[1024,256]{1,0:T(8,128)(2,1)S(1)}, u32[]{:S(2)}, u32[]{:S(2)}) collective-permute-start(bf16[1024,256]{1,0:T(8,128)(2,1)S(1)} %add_convert_fusion.7), channel_id=1, source_target_pairs={{0,48},{8,24},{16,0},{24,40},{32,16},{40,56},{48,32},{56,8},{64,11... | collective-permute-start | bytes 1572872 | tf_op jit(solution)/shard_map/ppermute | solution.py:35
  166.7 14.9 %collective-permute-start.54 = (bf16[1024,256]{1,0:T(8,128)(2,1)S(1)}, bf16[1024,256]{1,0:T(8,128)(2,1)S(1)}, u32[]{:S(2)}, u32[]{:S(2)}) collective-permute-start(bf16[1024,256]{1,0:T(8,128)(2,1)S(1)} %add_convert_fusion.6), channel_id=1, source_target_pairs={{0,48},{8,24},{16,0},{24,40},{32,16},{40,56},{48,32},{56,8},{64,11... | collective-permute-start | bytes 1572872 | tf_op jit(solution)/shard_map/ppermute | solution.py:35
  167.1 19.9 %collective-permute-start.52 = (bf16[1024,256]{1,0:T(8,128)(2,1)S(1)}, bf16[1024,256]{1,0:T(8,128)(2,1)S(1)}, u32[]{:S(2)}, u32[]{:S(2)}) collective-permute-start(bf16[1024,256]{1,0:T(8,128)(2,1)S(1)} %add_convert_fusion.3), channel_id=1, source_target_pairs={{0,64},{8,72},{16,80},{24,88},{32,96},{40,104},{48,112},{56,120},{... | collective-permute-start | bytes 1572872 | tf_op jit(solution)/shard_map/ppermute | solution.py:35
  176.3 10.6 %collective-permute-start.51 = (bf16[1024,256]{1,0:T(8,128)(2,1)S(1)}, bf16[1024,256]{1,0:T(8,128)(2,1)S(1)}, u32[]{:S(2)}, u32[]{:S(2)}) collective-permute-start(bf16[1024,256]{1,0:T(8,128)(2,1)S(1)} %add_convert_fusion.2), channel_id=1, source_target_pairs={{0,48},{8,24},{16,0},{24,40},{32,16},{40,56},{48,32},{56,8},{64,11... | collective-permute-start | bytes 1572872 | tf_op jit(solution)/shard_map/ppermute | solution.py:35
  (30 other events, 305.9 us)

commit v4 on v3

--- a/solution.py
+++ b/solution.py
@@ -166,12 +166,19 @@
     got_far_b = over(far_b, BACK, kind)
     passed_far = over(across_far, PAIR, kind)
     got_far_a = over(far_a, BACK, kind)
-    (got_far_b,) = step(got_far_b)
+    if kind == "col":
+        (got_far_a,) = meet(got_far_a)
+        got_far_b, _ = meet(got_far_b, got_far_a)
+    else:
+        (got_far_b,) = step(got_far_b)
     core_far = over(plus(far_other, got_far_b), CORE, kind)
     passed_far, _ = step(passed_far, got_far_b)
     across_sum = narrow(across_near + wide(passed_far))
     passed = over(across_sum, BACK, kind)
-    near_b, got_far_a, _ = meet(near_b, got_far_a, across_sum)
+    if kind == "row":
+        near_b, got_far_a, _ = meet(near_b, got_far_a, across_sum)
+    else:
+        near_b, _ = meet(near_b, across_sum)
     got_near_b = over(near_b, BACK, kind)
     far_sum = narrow(wide(far) + wide(got_far_a) + wide(core_far))
     back_far = over(far_sum, PAIR, kind)
@@ -205,9 +212,10 @@
     def _(i):
         block_copy(i).start()
 
-    @pl.loop(0, acc.shape[0] // 256)
+    @pl.loop(0, acc.shape[0] // 512)
     def _(i):
-        acc[pl.ds(pl.multiple_of(i * 256, 256), 256), :] = jnp.zeros((256, acc.shape[1]), acc.dtype)
+        here = pl.multiple_of(i * 512, 512)
+        acc[pl.ds(here, 512), :] = jnp.zeros((512, acc.shape[1]), acc.dtype)
 
     for copy in piece_copies:
         copy.wait()
@@ -241,10 +249,10 @@
     at = 0
     for out in outs:
 
-        @pl.loop(0, out.shape[0] // BLK)
+        @pl.loop(0, out.shape[0] // 1024)
         def _(j, at=at, out=out):
-            here = pl.multiple_of(j * BLK, BLK)
-            out[pl.ds(here, BLK), :] = acc[pl.ds(at + here, BLK), :].astype(out.dtype)
+            here = pl.multiple_of(j * 1024, 1024)
+            out[pl.ds(here, 1024), :] = acc[pl.ds(at + here, 1024), :].astype(out.dtype)
 
         at += out.shape[0]
 
@@ -268,7 +276,7 @@
             pltpu.SemaphoreType.DMA((n_in,)),
             pltpu.SemaphoreType.DMA((n_slots // CHUNK,)),
         ],
-        compiler_params=pltpu.CompilerParams(vmem_limit_bytes=(38 if transpose else 30) * 1024 * 1024),
+        compiler_params=pltpu.CompilerParams(vmem_limit_bytes=(38 if transpose else 44) * 1024 * 1024),
         cost_estimate=pl.CostEstimate(
             flops=2 * n_slots * BLK * BLK * width,
             bytes_accessed=n_slots * BLK * BLK * 2 + (in_rows + sum(sizes)) * width * 2,

time: 188 us -> 186 us (0.989)
  starting transfers between devices: 62.8 us -> 73.8 us
  waiting for transfers between devices: 101 us -> 91.4 us
  local copies, waits for them, and re-layouts: 4.49 us -> 2.5 us
    ppermute x25, starting transfers between devices: 23.5 us -> 31.9 us  [over(): return lax.ppermute(v, ('row', 'col'), pairs)]
    ppermute x25, waiting for transfers between devices: 47.5 us -> 41.7 us  [over(): return lax.ppermute(v, ('row', 'col'), pairs)]
    ppermute x32, waiting for transfers between devices: 53.8 us -> 49.7 us  [over(): return lax.ppermute(v, 'row', perm[0])]
    ppermute x32, starting transfers between devices: 39.3 us -> 41.9 us  [over(): return lax.ppermute(v, 'row', perm[0])]
    unnamed x10 -> x18, local copies, waits for them, and re-layouts: 3.85 us -> 1.85 us
  transfers between devices with their start and end apart: 57 -> 57, of which waited for: 33 -> 32; matrix products, arithmetic and copies ran while one was open for 3% -> 3% of each run, Pallas kernels for 0% -> 0%
where the time goes in v4:
time: 186 us; the launch traced here: 185 us
  waiting for transfers between devices  91.4 us (49%)
  starting transfers between devices  73.8 us (40%)
  Pallas kernels  9.01 us (5%)
  other arithmetic  4.06 us (2%)
  matrix products  3.02 us (2%)
  local copies, waits for them, and re-layouts  2.5 us (1%)
    ppermute x32, waiting for transfers between devices, over(): return lax.ppermute(v, 'row', perm[0])  49.7 us
    ppermute x32, starting transfers between devices, over(): return lax.ppermute(v, 'row', perm[0])  41.9 us
    ppermute x25, waiting for transfers between devices, over(): return lax.ppermute(v, ('row', 'col'), pairs)  41.7 us
    ppermute x25, starting transfers between devices, over(): return lax.ppermute(v, ('row', 'col'), pairs)  31.9 us
    pallas_call x2, Pallas kernels, sparse(): pl.pallas_call(functools.partial(sparse_kernel, transpose, n_in), out_sha...  9.01 us
  transfers between devices with their start and end apart: 57, of which 32 were waited for; matrix products, arithmetic and copies ran while one was open for 3% of the time, Pallas kernels for 0%

profile of v4, /device:TPU:1, one launch (start us, length us, event | category | flops | bytes accessed | tf_op | source)
XLA Modules:
  0.0 185.4 jit_solution(1641906897616644813)
XLA Ops:
  2.1 2.6 %collective-permute-start = (bf16[1024,256]{1,0:T(8,128)(2,1)}, bf16[1024,256]{1,0:T(8,128)(2,1)S(1)}, u32[]{:S(2)}, u32[]{:S(2)}) collective-permute-start(bf16[1024,256]{1,0:T(8,128)(2,1)} %bitcast.23), channel_id=1, source_target_pairs={{0,16},{8,56},{16,32},{24,8},{32,48},{40,24},{48,0},{56,40},{64,80... | collective-permute-start | bytes 1572872 | tf_op jit(solution)/shard_map/ppermute | solution.py:35
  4.7 3.6 %collective-permute-start.3 = (bf16[1024,256]{1,0:T(8,128)(2,1)}, bf16[1024,256]{1,0:T(8,128)(2,1)S(1)}, u32[]{:S(2)}, u32[]{:S(2)}) collective-permute-start(bf16[1024,256]{1,0:T(8,128)(2,1)} %bitcast.24), channel_id=1, source_target_pairs={{0,64},{8,72},{16,80},{24,88},{32,96},{40,104},{48,112},{56,120},{... | collective-permute-start | bytes 1572872 | tf_op jit(solution)/shard_map/ppermute | solution.py:35
  11.2 3.3 %collective-permute-start.2 = (bf16[1024,256]{1,0:T(8,128)(2,1)S(1)}, bf16[1024,256]{1,0:T(8,128)(2,1)S(1)}, u32[]{:S(2)}, u32[]{:S(2)}) collective-permute-start(bf16[1024,256]{1,0:T(8,128)(2,1)S(1)} %collective-permute-done.refs_4_), channel_id=1, source_target_pairs={{0,16},{8,56},{16,32},{24,8},{32,48},{40,24},{48,0},{56,40},{64,80... | collective-permute-start | bytes 1572872 | tf_op jit(solution)/shard_map/ppermute | solution.py:35
  14.5 3.0 %collective-permute-done.4.refs_5_ = bf16[1024,256]{1,0:T(8,128)(2,1)S(1)} collective-permute-done((bf16[1024,256]{1,0:T(8,128)(2,1)S(1)}, bf16[1024,256]{1,0:T(8,128)(2,1)S(1)}, u32[]{:S(2)}, u32[]{:S(2)}) %collective-permute-start.4) | collective-permute-done | bytes 524320 | tf_op jit(solution)/shard_map/ppermute | solution.py:35
  17.4 2.6 %collective-permute-done.3.refs_2_ = bf16[1024,256]{1,0:T(8,128)(2,1)S(1)} collective-permute-done((bf16[1024,256]{1,0:T(8,128)(2,1)}, bf16[1024,256]{1,0:T(8,128)(2,1)S(1)}, u32[]{:S(2)}, u32[]{:S(2)}) %collective-permute-start.3) | collective-permute-done | bytes 524320 | tf_op jit(solution)/shard_map/ppermute | solution.py:35
  20.0 3.0 %collective-permute-done.2.refs_12_ = bf16[1024,256]{1,0:T(8,128)(2,1)S(1)} collective-permute-done((bf16[1024,256]{1,0:T(8,128)(2,1)S(1)}, bf16[1024,256]{1,0:T(8,128)(2,1)S(1)}, u32[]{:S(2)}, u32[]{:S(2)}) %collective-permute-start.2) | collective-permute-done | bytes 524320 | tf_op jit(solution)/shard_map/ppermute | solution.py:35
  25.4 3.6 %collective-permute-start.8 = (bf16[1024,256]{1,0:T(8,128)(2,1)S(1)}, bf16[1024,256]{1,0:T(8,128)(2,1)S(1)}, u32[]{:S(2)}, u32[]{:S(2)}) collective-permute-start(bf16[1024,256]{1,0:T(8,128)(2,1)S(1)} %collective-permute-done.2.refs_12_), channel_id=1, source_target_pairs={{0,64},{8,72},{16,80},{24,88},{32,96},{40,104},{48,112},{56,120},{... | collective-permute-start | bytes 1572872 | tf_op jit(solution)/shard_map/ppermute | solution.py:35
  30.1 2.7 %collective-permute-done.6.refs_6_ = bf16[1024,256]{1,0:T(8,128)(2,1)S(1)} collective-permute-done((bf16[1024,256]{1,0:T(8,128)(2,1)S(1)}, bf16[1024,256]{1,0:T(8,128)(2,1)S(1)}, u32[]{:S(2)}, u32[]{:S(2)}) %collective-permute-start.6) | collective-permute-done | bytes 524320 | tf_op jit(solution)/shard_map/ppermute | solution.py:35
  34.9 5.5 %collective-permute-done.8.refs_13_ = bf16[1024,256]{1,0:T(8,128)(2,1)S(1)} collective-permute-done((bf16[1024,256]{1,0:T(8,128)(2,1)S(1)}, bf16[1024,256]{1,0:T(8,128)(2,1)S(1)}, u32[]{:S(2)}, u32[]{:S(2)}) %collective-permute-start.8) | collective-permute-done | bytes 524320 | tf_op jit(solution)/shard_map/ppermute | solution.py:35
  45.7 4.7 %sparse_forward.1 = (bf16[1024,256]{1,0:T(8,128)(2,1)S(1)}, bf16[1024,256]{1,0:T(8,128)(2,1)S(1)}, bf16[1024,256]{1,0:T(8,128)(2,1)S(1)}, bf16[1024,256]{1,0:T(8...) custom-call(s32[192]{0:T(256)S(1)} %get-tuple-element.63.rows.cols, ...), custom_call_target="tpu_custom_call" | custom-call | flops 1610612736 | bytes 18874368 | tf_op jit(solution)/shard_map/sparse_forward/pallas_call | solution.py:265
  50.6 2.2 %collective-permute-start.18 = (bf16[1024,256]{1,0:T(8,128)(2,1)S(1)}, bf16[1024,256]{1,0:T(8,128)(2,1)S(1)}, u32[]{:S(2)}, u32[]{:S(2)}) collective-permute-start(bf16[1024,256]{1,0:T(8,128)(2,1)S(1)} %get-tuple-element.77), channel_id=1, source_target_pairs={{0,6},{8,10},{2,0},{10,12},{4,2},{12,14},{6,4},{14,8},{1,7},{9,11}... | collective-permute-start | bytes 1572872 | tf_op jit(solution)/shard_map/ppermute | solution.py:41
  54.7 3.3 %collective-permute-start.15 = (bf16[1024,256]{1,0:T(8,128)(2,1)S(1)}, bf16[1024,256]{1,0:T(8,128)(2,1)S(1)}, u32[]{:S(2)}, u32[]{:S(2)}) collective-permute-start(bf16[1024,256]{1,0:T(8,128)(2,1)S(1)} %get-tuple-element.75), channel_id=1, source_target_pairs={{0,1},{8,9},{2,3},{10,11},{4,5},{12,13},{6,7},{14,15},{1,0},{9,8},... | collective-permute-start | bytes 1572872 | tf_op jit(solution)/shard_map/ppermute | solution.py:41
  60.1 2.8 %collective-permute-done.18 = bf16[1024,256]{1,0:T(8,128)(2,1)S(1)} collective-permute-done((bf16[1024,256]{1,0:T(8,128)(2,1)S(1)}, bf16[1024,256]{1,0:T(8,128)(2,1)S(1)}, u32[]{:S(2)}, u32[]{:S(2)}) %collective-permute-start.18) | collective-permute-done | bytes 524320 | tf_op jit(solution)/shard_map/ppermute | solution.py:41
  62.9 5.6 %collective-permute-done.17 = bf16[1024,256]{1,0:T(8,128)(2,1)S(1)} collective-permute-done((bf16[1024,256]{1,0:T(8,128)(2,1)S(1)}, bf16[1024,256]{1,0:T(8,128)(2,1)S(1)}, u32[]{:S(2)}, u32[]{:S(2)}) %collective-permute-start.17) | collective-permute-done | bytes 524320 | tf_op jit(solution)/shard_map/ppermute | solution.py:41
  74.7 4.8 %collective-permute-done.19 = bf16[1024,256]{1,0:T(8,128)(2,1)S(1)} collective-permute-done((bf16[1024,256]{1,0:T(8,128)(2,1)S(1)}, bf16[1024,256]{1,0:T(8,128)(2,1)S(1)}, u32[]{:S(2)}, u32[]{:S(2)}) %collective-permute-start.19) | collective-permute-done | bytes 524320 | tf_op jit(solution)/shard_map/ppermute | solution.py:41
  79.7 5.4 %collective-permute-done.24 = bf16[1024,256]{1,0:T(8,128)(2,1)S(1)} collective-permute-done((bf16[1024,256]{1,0:T(8,128)(2,1)S(1)}, bf16[1024,256]{1,0:T(8,128)(2,1)S(1)}, u32[]{:S(2)}, u32[]{:S(2)}) %collective-permute-start.24) | collective-permute-done | bytes 524320 | tf_op jit(solution)/shard_map/ppermute | solution.py:41
  85.9 4.8 %collective-permute-done.21 = bf16[1024,256]{1,0:T(8,128)(2,1)S(1)} collective-permute-done((bf16[1024,256]{1,0:T(8,128)(2,1)S(1)}, bf16[1024,256]{1,0:T(8,128)(2,1)S(1)}, u32[]{:S(2)}, u32[]{:S(2)}) %collective-permute-start.21) | collective-permute-done | bytes 524320 | tf_op jit(solution)/shard_map/ppermute | solution.py:41
  93.3 3.1 %collective-permute-start.27 = (bf16[1024,256]{1,0:T(8,128)(2,1)S(1)}, bf16[1024,256]{1,0:T(8,128)(2,1)S(1)}, u32[]{:S(2)}, u32[]{:S(2)}) collective-permute-start(bf16[1024,256]{1,0:T(8,128)(2,1)S(1)} %get-tuple-element.123.refs_0_), channel_id=1, source_target_pairs={{0,2},{8,14},{2,4},{10,8},{4,6},{12,10},{6,0},{14,12},{1,3},{9,15}... | collective-permute-start | bytes 1572872 | tf_op jit(solution)/shard_map/ppermute | solution.py:41
  98.5 4.0 %collective-permute-done.27.refs_2_ = bf16[1024,256]{1,0:T(8,128)(2,1)S(1)} collective-permute-done((bf16[1024,256]{1,0:T(8,128)(2,1)S(1)}, bf16[1024,256]{1,0:T(8,128)(2,1)S(1)}, u32[]{:S(2)}, u32[]{:S(2)}) %collective-permute-start.27) | collective-permute-done | bytes 524320 | tf_op jit(solution)/shard_map/ppermute | solution.py:41
  102.5 3.1 %collective-permute-start.29 = (bf16[1024,256]{1,0:T(8,128)(2,1)S(1)}, bf16[1024,256]{1,0:T(8,128)(2,1)S(1)}, u32[]{:S(2)}, u32[]{:S(2)}) collective-permute-start(bf16[1024,256]{1,0:T(8,128)(2,1)S(1)} %collective-permute-done.27.refs_2_), channel_id=1, source_target_pairs={{0,2},{8,14},{2,4},{10,8},{4,6},{12,10},{6,0},{14,12},{1,3},{9,15}... | collective-permute-start | bytes 1572872 | tf_op jit(solution)/shard_map/ppermute | solution.py:41
  105.6 3.1 %collective-permute-start.28 = (f32[136,256]{1,0:T(8,128)S(1)}, f32[136,256]{1,0:T(8,128)S(1)}, u32[]{:S(2)}, u32[]{:S(2)}) collective-permute-start(f32[136,256]{1,0:T(8,128)S(1)} %dynamic-slice_add_fusion), channel_id=1, source_target_pairs={{0,64},{8,72},{16,80},{24,88},{32,96},{40,104},{48,112},{56,120},{... | collective-permute-start | bytes 417800 | tf_op jit(solution)/shard_map/ppermute | solution.py:35
  110.1 4.7 %collective-permute-done.28 = f32[136,256]{1,0:T(8,128)S(1)} collective-permute-done((f32[136,256]{1,0:T(8,128)S(1)}, f32[136,256]{1,0:T(8,128)S(1)}, u32[]{:S(2)}, u32[]{:S(2)}) %collective-permute-start.28) | collective-permute-done | bytes 139296 | tf_op jit(solution)/shard_map/ppermute | solution.py:35
  120.2 3.0 %collective-permute-start.33 = (bf16[1024,256]{1,0:T(8,128)(2,1)S(1)}, bf16[1024,256]{1,0:T(8,128)(2,1)S(1)}, u32[]{:S(2)}, u32[]{:S(2)}) collective-permute-start(bf16[1024,256]{1,0:T(8,128)(2,1)S(1)} %collective-permute-done.30.refs_1_), channel_id=1, source_target_pairs={{0,2},{8,14},{2,4},{10,8},{4,6},{12,10},{6,0},{14,12},{1,3},{9,15}... | collective-permute-start | bytes 1572872 | tf_op jit(solution)/shard_map/ppermute | solution.py:41
  124.3 5.2 %collective-permute-done.38.refs_7_ = bf16[1024,256]{1,0:T(8,128)(2,1)S(1)} collective-permute-done((bf16[1024,256]{1,0:T(8,128)(2,1)S(1)}, bf16[1024,256]{1,0:T(8,128)(2,1)S(1)}, u32[]{:S(2)}, u32[]{:S(2)}) %collective-permute-start.38) | collective-permute-done | bytes 524320 | tf_op jit(solution)/shard_map/ppermute | solution.py:41
  131.9 4.3 %sparse_back.1 = (bf16[1024,256]{1,0:T(8,128)(2,1)S(1)}, bf16[1024,256]{1,0:T(8,128)(2,1)S(1)}, bf16[1024,256]{1,0:T(8,128)(2,1)S(1)}, bf16[1024,256]{1,0:T(8,12...) custom-call(s32[192]{0:T(256)S(1)} %get-tuple-element.64.cols.rows, ...), custom_call_target="tpu_custom_call" | custom-call | flops 1610612736 | bytes 18874368 | tf_op jit(solution)/shard_map/sparse_back/pallas_call | solution.py:265
  142.8 2.6 %collective-permute-start.40 = (bf16[2048,256]{1,0:T(8,128)(2,1)S(1)}, bf16[2048,256]{1,0:T(8,128)(2,1)S(1)}, u32[]{:S(2)}, u32[]{:S(2)}) collective-permute-start(bf16[2048,256]{1,0:T(8,128)(2,1)S(1)} %get-tuple-element.98), channel_id=1, source_target_pairs={{0,8},{8,0},{16,24},{24,16},{32,40},{40,32},{48,56},{56,48},{64,72... | collective-permute-start | bytes 3145736 | tf_op jit(solution)/shard_map/ppermute | solution.py:35
  145.6 3.2 %collective-permute-start.46 = (bf16[1024,256]{1,0:T(8,128)(2,1)S(1)}, bf16[1024,256]{1,0:T(8,128)(2,1)S(1)}, u32[]{:S(2)}, u32[]{:S(2)}) collective-permute-start(bf16[1024,256]{1,0:T(8,128)(2,1)S(1)} %add_convert_fusion.8), channel_id=1, source_target_pairs={{0,64},{8,72},{16,80},{24,88},{32,96},{40,104},{48,112},{56,120},{... | collective-permute-start | bytes 1572872 | tf_op jit(solution)/shard_map/ppermute | solution.py:35
  149.9 5.9 %collective-permute-done.41 = f32[136,256]{1,0:T(8,128)S(1)} collective-permute-done((f32[136,256]{1,0:T(8,128)S(1)}, f32[136,256]{1,0:T(8,128)S(1)}, u32[]{:S(2)}, u32[]{:S(2)}) %collective-permute-start.41) | collective-permute-done | bytes 139296 | tf_op jit(solution)/shard_map/ppermute | solution.py:35
  157.6 3.3 %collective-permute-done.46 = bf16[1024,256]{1,0:T(8,128)(2,1)S(1)} collective-permute-done((bf16[1024,256]{1,0:T(8,128)(2,1)S(1)}, bf16[1024,256]{1,0:T(8,128)(2,1)S(1)}, u32[]{:S(2)}, u32[]{:S(2)}) %collective-permute-start.46) | collective-permute-done | bytes 524320 | tf_op jit(solution)/shard_map/ppermute | solution.py:35
  165.8 2.3 %collective-permute-done.47 = f32[136,256]{1,0:T(8,128)S(1)} collective-permute-done((f32[136,256]{1,0:T(8,128)S(1)}, f32[136,256]{1,0:T(8,128)S(1)}, u32[]{:S(2)}, u32[]{:S(2)}) %collective-permute-start.47) | collective-permute-done | bytes 139296 | tf_op jit(solution)/shard_map/ppermute | solution.py:41
  168.1 5.1 %collective-permute-done.48 = bf16[1024,256]{1,0:T(8,128)(2,1)S(1)} collective-permute-done((bf16[1024,256]{1,0:T(8,128)(2,1)S(1)}, bf16[1024,256]{1,0:T(8,128)(2,1)S(1)}, u32[]{:S(2)}, u32[]{:S(2)}) %collective-permute-start.48) | collective-permute-done | bytes 524320 | tf_op jit(solution)/shard_map/ppermute | solution.py:35
  173.6 5.2 %collective-permute-done.54 = bf16[1024,256]{1,0:T(8,128)(2,1)S(1)} collective-permute-done((bf16[1024,256]{1,0:T(8,128)(2,1)S(1)}, bf16[1024,256]{1,0:T(8,128)(2,1)S(1)}, u32[]{:S(2)}, u32[]{:S(2)}) %collective-permute-start.54) | collective-permute-done | bytes 524320 | tf_op jit(solution)/shard_map/ppermute | solution.py:35
  (131 shorter events, 62.2 us)
Async XLA Ops:
  2.1 9.0 %collective-permute-start = (bf16[1024,256]{1,0:T(8,128)(2,1)}, bf16[1024,256]{1,0:T(8,128)(2,1)S(1)}, u32[]{:S(2)}, u32[]{:S(2)}) collective-permute-start(bf16[1024,256]{1,0:T(8,128)(2,1)} %bitcast.23), channel_id=1, source_target_pairs={{0,16},{8,56},{16,32},{24,8},{32,48},{40,24},{48,0},{56,40},{64,80... | collective-permute-start | bytes 1572872 | tf_op jit(solution)/shard_map/ppermute | solution.py:35
  4.7 15.3 %collective-permute-start.3 = (bf16[1024,256]{1,0:T(8,128)(2,1)}, bf16[1024,256]{1,0:T(8,128)(2,1)S(1)}, u32[]{:S(2)}, u32[]{:S(2)}) collective-permute-start(bf16[1024,256]{1,0:T(8,128)(2,1)} %bitcast.24), channel_id=1, source_target_pairs={{0,64},{8,72},{16,80},{24,88},{32,96},{40,104},{48,112},{56,120},{... | collective-permute-start | bytes 1572872 | tf_op jit(solution)/shard_map/ppermute | solution.py:35
  11.2 11.9 %collective-permute-start.2 = (bf16[1024,256]{1,0:T(8,128)(2,1)S(1)}, bf16[1024,256]{1,0:T(8,128)(2,1)S(1)}, u32[]{:S(2)}, u32[]{:S(2)}) collective-permute-start(bf16[1024,256]{1,0:T(8,128)(2,1)S(1)} %collective-permute-done.refs_4_), channel_id=1, source_target_pairs={{0,16},{8,56},{16,32},{24,8},{32,48},{40,24},{48,0},{56,40},{64,80... | collective-permute-start | bytes 1572872 | tf_op jit(solution)/shard_map/ppermute | solution.py:35
  25.4 15.0 %collective-permute-start.8 = (bf16[1024,256]{1,0:T(8,128)(2,1)S(1)}, bf16[1024,256]{1,0:T(8,128)(2,1)S(1)}, u32[]{:S(2)}, u32[]{:S(2)}) collective-permute-start(bf16[1024,256]{1,0:T(8,128)(2,1)S(1)} %collective-permute-done.2.refs_12_), channel_id=1, source_target_pairs={{0,64},{8,72},{16,80},{24,88},{32,96},{40,104},{48,112},{56,120},{... | collective-permute-start | bytes 1572872 | tf_op jit(solution)/shard_map/ppermute | solution.py:35
  29.0 11.4 %collective-permute-start.7 = (bf16[1024,256]{1,0:T(8,128)(2,1)S(1)}, bf16[1024,256]{1,0:T(8,128)(2,1)S(1)}, u32[]{:S(2)}, u32[]{:S(2)}) collective-permute-start(bf16[1024,256]{1,0:T(8,128)(2,1)S(1)} %collective-permute-done.5.refs_3_), channel_id=1, source_target_pairs={{0,16},{8,56},{16,32},{24,8},{32,48},{40,24},{48,0},{56,40},{64,80... | collective-permute-start | bytes 1572872 | tf_op jit(solution)/shard_map/ppermute | solution.py:35
  29.6 11.3 %collective-permute-start.9 = (bf16[1024,256]{1,0:T(8,128)(2,1)S(1)}, bf16[1024,256]{1,0:T(8,128)(2,1)S(1)}, u32[]{:S(2)}, u32[]{:S(2)}) collective-permute-start(bf16[1024,256]{1,0:T(8,128)(2,1)S(1)} %collective-permute-done.refs_4_), channel_id=1, source_target_pairs={{0,8},{8,0},{16,24},{24,16},{32,40},{40,32},{48,56},{56,48},{64,72... | collective-permute-start | bytes 1572872 | tf_op jit(solution)/shard_map/ppermute | solution.py:35
  29.8 11.9 %collective-permute-start.10 = (bf16[1024,256]{1,0:T(8,128)(2,1)S(1)}, bf16[1024,256]{1,0:T(8,128)(2,1)S(1)}, u32[]{:S(2)}, u32[]{:S(2)}) collective-permute-start(bf16[1024,256]{1,0:T(8,128)(2,1)S(1)} %collective-permute-done.4.refs_5_), channel_id=1, source_target_pairs={{0,8},{8,0},{16,24},{24,16},{32,40},{40,32},{48,56},{56,48},{64,72... | collective-permute-start | bytes 1572872 | tf_op jit(solution)/shard_map/ppermute | solution.py:35
  50.6 12.2 %collective-permute-start.18 = (bf16[1024,256]{1,0:T(8,128)(2,1)S(1)}, bf16[1024,256]{1,0:T(8,128)(2,1)S(1)}, u32[]{:S(2)}, u32[]{:S(2)}) collective-permute-start(bf16[1024,256]{1,0:T(8,128)(2,1)S(1)} %get-tuple-element.77), channel_id=1, source_target_pairs={{0,6},{8,10},{2,0},{10,12},{4,2},{12,14},{6,4},{14,8},{1,7},{9,11}... | collective-permute-start | bytes 1572872 | tf_op jit(solution)/shard_map/ppermute | solution.py:41
  52.9 15.6 %collective-permute-start.17 = (bf16[1024,256]{1,0:T(8,128)(2,1)S(1)}, bf16[1024,256]{1,0:T(8,128)(2,1)S(1)}, u32[]{:S(2)}, u32[]{:S(2)}) collective-permute-start(bf16[1024,256]{1,0:T(8,128)(2,1)S(1)} %collective-permute-done.16), channel_id=1, source_target_pairs={{0,6},{8,10},{2,0},{10,12},{4,2},{12,14},{6,4},{14,8},{1,7},{9,11}... | collective-permute-start | bytes 1572872 | tf_op jit(solution)/shard_map/ppermute | solution.py:41
  54.7 14.6 %collective-permute-start.15 = (bf16[1024,256]{1,0:T(8,128)(2,1)S(1)}, bf16[1024,256]{1,0:T(8,128)(2,1)S(1)}, u32[]{:S(2)}, u32[]{:S(2)}) collective-permute-start(bf16[1024,256]{1,0:T(8,128)(2,1)S(1)} %get-tuple-element.75), channel_id=1, source_target_pairs={{0,1},{8,9},{2,3},{10,11},{4,5},{12,13},{6,7},{14,15},{1,0},{9,8},... | collective-permute-start | bytes 1572872 | tf_op jit(solution)/shard_map/ppermute | solution.py:41
  58.0 12.2 %collective-permute-start.23 = (bf16[1024,256]{1,0:T(8,128)(2,1)S(1)}, bf16[1024,256]{1,0:T(8,128)(2,1)S(1)}, u32[]{:S(2)}, u32[]{:S(2)}) collective-permute-start(bf16[1024,256]{1,0:T(8,128)(2,1)S(1)} %get-tuple-element.82), channel_id=1, source_target_pairs={{0,8},{8,0},{2,10},{10,2},{4,12},{12,4},{6,14},{14,6},{1,9},{9,1},... | collective-permute-start | bytes 1572872 | tf_op jit(solution)/shard_map/ppermute | solution.py:41
  69.5 10.1 %collective-permute-start.19 = (bf16[1024,256]{1,0:T(8,128)(2,1)S(1)}, bf16[1024,256]{1,0:T(8,128)(2,1)S(1)}, u32[]{:S(2)}, u32[]{:S(2)}) collective-permute-start(bf16[1024,256]{1,0:T(8,128)(2,1)S(1)} %add_convert_fusion.13), channel_id=1, source_target_pairs={{0,6},{8,10},{2,0},{10,12},{4,2},{12,14},{6,4},{14,8},{1,7},{9,11}... | collective-permute-start | bytes 1572872 | tf_op jit(solution)/shard_map/ppermute | solution.py:41
  70.2 14.9 %collective-permute-start.24 = (bf16[1024,256]{1,0:T(8,128)(2,1)S(1)}, bf16[1024,256]{1,0:T(8,128)(2,1)S(1)}, u32[]{:S(2)}, u32[]{:S(2)}) collective-permute-start(bf16[1024,256]{1,0:T(8,128)(2,1)S(1)} %collective-permute-done.23), channel_id=1, source_target_pairs={{0,6},{8,10},{2,0},{10,12},{4,2},{12,14},{6,4},{14,8},{1,7},{9,11}... | collective-permute-start | bytes 1572872 | tf_op jit(solution)/shard_map/ppermute | solution.py:41
  72.7 18.1 %collective-permute-start.22 = (bf16[1024,256]{1,0:T(8,128)(2,1)S(1)}, bf16[1024,256]{1,0:T(8,128)(2,1)S(1)}, u32[]{:S(2)}, u32[]{:S(2)}) collective-permute-start(bf16[1024,256]{1,0:T(8,128)(2,1)S(1)} %add_convert_fusion.12), channel_id=1, source_target_pairs={{0,1},{8,9},{2,3},{10,11},{4,5},{12,13},{6,7},{14,15},{1,0},{9,8},... | collective-permute-start | bytes 1572872 | tf_op jit(solution)/shard_map/ppermute | solution.py:41
  79.7 11.1 %collective-permute-start.21 = (bf16[1024,256]{1,0:T(8,128)(2,1)S(1)}, bf16[1024,256]{1,0:T(8,128)(2,1)S(1)}, u32[]{:S(2)}, u32[]{:S(2)}) collective-permute-start(bf16[1024,256]{1,0:T(8,128)(2,1)S(1)} %add_convert_fusion.11), channel_id=1, source_target_pairs={{0,6},{8,10},{2,0},{10,12},{4,2},{12,14},{6,4},{14,8},{1,7},{9,11}... | collective-permute-start | bytes 1572872 | tf_op jit(solution)/shard_map/ppermute | solution.py:41
  93.3 9.2 %collective-permute-start.27 = (bf16[1024,256]{1,0:T(8,128)(2,1)S(1)}, bf16[1024,256]{1,0:T(8,128)(2,1)S(1)}, u32[]{:S(2)}, u32[]{:S(2)}) collective-permute-start(bf16[1024,256]{1,0:T(8,128)(2,1)S(1)} %get-tuple-element.123.refs_0_), channel_id=1, source_target_pairs={{0,2},{8,14},{2,4},{10,8},{4,6},{12,10},{6,0},{14,12},{1,3},{9,15}... | collective-permute-start | bytes 1572872 | tf_op jit(solution)/shard_map/ppermute | solution.py:41
  96.9 13.2 %collective-permute-start.30 = (bf16[1024,256]{1,0:T(8,128)(2,1)S(1)}, bf16[1024,256]{1,0:T(8,128)(2,1)S(1)}, u32[]{:S(2)}, u32[]{:S(2)}) collective-permute-start(bf16[1024,256]{1,0:T(8,128)(2,1)S(1)} %get-tuple-element.123.refs_0_), channel_id=1, source_target_pairs={{0,1},{8,9},{2,3},{10,11},{4,5},{12,13},{6,7},{14,15},{1,0},{9,8},... | collective-permute-start | bytes 1572872 | tf_op jit(solution)/shard_map/ppermute | solution.py:41
  98.3 10.5 %collective-permute-start.32 = (bf16[1024,256]{1,0:T(8,128)(2,1)}, bf16[1024,256]{1,0:T(8,128)(2,1)S(1)}, u32[]{:S(2)}, u32[]{:S(2)}) collective-permute-start(bf16[1024,256]{1,0:T(8,128)(2,1)} %collective-permute-done.31), channel_id=1, source_target_pairs={{0,2},{8,14},{2,4},{10,8},{4,6},{12,10},{6,0},{14,12},{1,3},{9,15}... | collective-permute-start | bytes 1572872 | tf_op jit(solution)/shard_map/ppermute | solution.py:41
  102.5 12.3 %collective-permute-start.29 = (bf16[1024,256]{1,0:T(8,128)(2,1)S(1)}, bf16[1024,256]{1,0:T(8,128)(2,1)S(1)}, u32[]{:S(2)}, u32[]{:S(2)}) collective-permute-start(bf16[1024,256]{1,0:T(8,128)(2,1)S(1)} %collective-permute-done.27.refs_2_), channel_id=1, source_target_pairs={{0,2},{8,14},{2,4},{10,8},{4,6},{12,10},{6,0},{14,12},{1,3},{9,15}... | collective-permute-start | bytes 1572872 | tf_op jit(solution)/shard_map/ppermute | solution.py:41
  105.6 9.1 %collective-permute-start.28 = (f32[136,256]{1,0:T(8,128)S(1)}, f32[136,256]{1,0:T(8,128)S(1)}, u32[]{:S(2)}, u32[]{:S(2)}) collective-permute-start(f32[136,256]{1,0:T(8,128)S(1)} %dynamic-slice_add_fusion), channel_id=1, source_target_pairs={{0,64},{8,72},{16,80},{24,88},{32,96},{40,104},{48,112},{56,120},{... | collective-permute-start | bytes 417800 | tf_op jit(solution)/shard_map/ppermute | solution.py:35
  116.0 13.6 %collective-permute-start.38 = (bf16[1024,256]{1,0:T(8,128)(2,1)S(1)}, bf16[1024,256]{1,0:T(8,128)(2,1)S(1)}, u32[]{:S(2)}, u32[]{:S(2)}) collective-permute-start(bf16[1024,256]{1,0:T(8,128)(2,1)S(1)} %collective-permute-done.29.refs_6_), channel_id=1, source_target_pairs={{0,1},{8,9},{2,3},{10,11},{4,5},{12,13},{6,7},{14,15},{1,0},{9,8},... | collective-permute-start | bytes 1572872 | tf_op jit(solution)/shard_map/ppermute | solution.py:41
  117.6 12.0 %collective-permute-start.37 = (bf16[1024,256]{1,0:T(8,128)(2,1)S(1)}, bf16[1024,256]{1,0:T(8,128)(2,1)S(1)}, u32[]{:S(2)}, u32[]{:S(2)}) collective-permute-start(bf16[1024,256]{1,0:T(8,128)(2,1)S(1)} %collective-permute-done.36), channel_id=1, source_target_pairs={{0,2},{8,14},{2,4},{10,8},{4,6},{12,10},{6,0},{14,12},{1,3},{9,15}... | collective-permute-start | bytes 1572872 | tf_op jit(solution)/shard_map/ppermute | solution.py:41
  120.1 10.2 %collective-permute-start.34 = (bf16[1024,256]{1,0:T(8,128)(2,1)S(1)}, bf16[1024,256]{1,0:T(8,128)(2,1)S(1)}, u32[]{:S(2)}, u32[]{:S(2)}) collective-permute-start(bf16[1024,256]{1,0:T(8,128)(2,1)S(1)} %collective-permute-done.32), channel_id=1, source_target_pairs={{0,8},{8,0},{2,10},{10,2},{4,12},{12,4},{6,14},{14,6},{1,9},{9,1},... | collective-permute-start | bytes 1572872 | tf_op jit(solution)/shard_map/ppermute | solution.py:41
  120.2 11.3 %collective-permute-start.33 = (bf16[1024,256]{1,0:T(8,128)(2,1)S(1)}, bf16[1024,256]{1,0:T(8,128)(2,1)S(1)}, u32[]{:S(2)}, u32[]{:S(2)}) collective-permute-start(bf16[1024,256]{1,0:T(8,128)(2,1)S(1)} %collective-permute-done.30.refs_1_), channel_id=1, source_target_pairs={{0,2},{8,14},{2,4},{10,8},{4,6},{12,10},{6,0},{14,12},{1,3},{9,15}... | collective-permute-start | bytes 1572872 | tf_op jit(solution)/shard_map/ppermute | solution.py:41
  140.9 14.9 %collective-permute-start.43 = (bf16[1024,256]{1,0:T(8,128)(2,1)S(1)}, bf16[1024,256]{1,0:T(8,128)(2,1)S(1)}, u32[]{:S(2)}, u32[]{:S(2)}) collective-permute-start(bf16[1024,256]{1,0:T(8,128)(2,1)S(1)} %get-tuple-element.125), channel_id=1, source_target_pairs={{0,48},{8,24},{16,0},{24,40},{32,16},{40,56},{48,32},{56,8},{64,11... | collective-permute-start | bytes 1572872 | tf_op jit(solution)/shard_map/ppermute | solution.py:35
  142.8 20.8 %collective-permute-start.40 = (bf16[2048,256]{1,0:T(8,128)(2,1)S(1)}, bf16[2048,256]{1,0:T(8,128)(2,1)S(1)}, u32[]{:S(2)}, u32[]{:S(2)}) collective-permute-start(bf16[2048,256]{1,0:T(8,128)(2,1)S(1)} %get-tuple-element.98), channel_id=1, source_target_pairs={{0,8},{8,0},{16,24},{24,16},{32,40},{40,32},{48,56},{56,48},{64,72... | collective-permute-start | bytes 3145736 | tf_op jit(solution)/shard_map/ppermute | solution.py:35
  145.6 15.3 %collective-permute-start.46 = (bf16[1024,256]{1,0:T(8,128)(2,1)S(1)}, bf16[1024,256]{1,0:T(8,128)(2,1)S(1)}, u32[]{:S(2)}, u32[]{:S(2)}) collective-permute-start(bf16[1024,256]{1,0:T(8,128)(2,1)S(1)} %add_convert_fusion.8), channel_id=1, source_target_pairs={{0,64},{8,72},{16,80},{24,88},{32,96},{40,104},{48,112},{56,120},{... | collective-permute-start | bytes 1572872 | tf_op jit(solution)/shard_map/ppermute | solution.py:35
  149.4 14.4 %collective-permute-start.49 = (bf16[1024,256]{1,0:T(8,128)(2,1)S(1)}, bf16[1024,256]{1,0:T(8,128)(2,1)S(1)}, u32[]{:S(2)}, u32[]{:S(2)}) collective-permute-start(bf16[1024,256]{1,0:T(8,128)(2,1)S(1)} %get-tuple-element.124), channel_id=1, source_target_pairs={{0,48},{8,24},{16,0},{24,40},{32,16},{40,56},{48,32},{56,8},{64,11... | collective-permute-start | bytes 1572872 | tf_op jit(solution)/shard_map/ppermute | solution.py:35
  163.3 9.8 %collective-permute-start.48 = (bf16[1024,256]{1,0:T(8,128)(2,1)S(1)}, bf16[1024,256]{1,0:T(8,128)(2,1)S(1)}, u32[]{:S(2)}, u32[]{:S(2)}) collective-permute-start(bf16[1024,256]{1,0:T(8,128)(2,1)S(1)} %add_convert_fusion.7), channel_id=1, source_target_pairs={{0,48},{8,24},{16,0},{24,40},{32,16},{40,56},{48,32},{56,8},{64,11... | collective-permute-start | bytes 1572872 | tf_op jit(solution)/shard_map/ppermute | solution.py:35
  163.9 14.9 %collective-permute-start.54 = (bf16[1024,256]{1,0:T(8,128)(2,1)S(1)}, bf16[1024,256]{1,0:T(8,128)(2,1)S(1)}, u32[]{:S(2)}, u32[]{:S(2)}) collective-permute-start(bf16[1024,256]{1,0:T(8,128)(2,1)S(1)} %add_convert_fusion.6), channel_id=1, source_target_pairs={{0,48},{8,24},{16,0},{24,40},{32,16},{40,56},{48,32},{56,8},{64,11... | collective-permute-start | bytes 1572872 | tf_op jit(solution)/shard_map/ppermute | solution.py:35
  164.5 19.6 %collective-permute-start.52 = (bf16[1024,256]{1,0:T(8,128)(2,1)S(1)}, bf16[1024,256]{1,0:T(8,128)(2,1)S(1)}, u32[]{:S(2)}, u32[]{:S(2)}) collective-permute-start(bf16[1024,256]{1,0:T(8,128)(2,1)S(1)} %add_convert_fusion.3), channel_id=1, source_target_pairs={{0,64},{8,72},{16,80},{24,88},{32,96},{40,104},{48,112},{56,120},{... | collective-permute-start | bytes 1572872 | tf_op jit(solution)/shard_map/ppermute | solution.py:35
  173.5 10.6 %collective-permute-start.51 = (bf16[1024,256]{1,0:T(8,128)(2,1)S(1)}, bf16[1024,256]{1,0:T(8,128)(2,1)S(1)}, u32[]{:S(2)}, u32[]{:S(2)}) collective-permute-start(bf16[1024,256]{1,0:T(8,128)(2,1)S(1)} %add_convert_fusion.2), channel_id=1, source_target_pairs={{0,48},{8,24},{16,0},{24,40},{32,16},{40,56},{48,32},{56,8},{64,11... | collective-permute-start | bytes 1572872 | tf_op jit(solution)/shard_map/ppermute | solution.py:35
  (34 other events, 329.0 us)

commit v5 on v4

--- a/solution.py
+++ b/solution.py
@@ -111,10 +111,10 @@
     near_a = over(own, OUT, kind)
     other = over(own, CORE, kind)
     near_b = over(other, OUT, kind)
-    near_a, *extra = step(near_a, *extra)
+    (near_a,) = step(near_a)
     across = over(near_a, OUT, kind)
     near_b, _ = meet(near_b, near_a)
-    across, far, _ = step(across, far, near_b)
+    across, far, _, *extra = step(across, far, near_b, *extra)
     across_far = over(across, PAIR, kind)
     far_other = over(far, CORE, kind)
     far_a = over(far, OUT, kind)

time: 186 us -> 186 us (level)
  starting transfers between devices: 73.8 us -> 67.7 us
  waiting for transfers between devices: 91.4 us -> 95.3 us
  Pallas kernels: 9.01 us -> 11 us
    ppermute x25, starting transfers between devices: 31.9 us -> 26.5 us  [over(): return lax.ppermute(v, ('row', 'col'), pairs)]
    ppermute x25, waiting for transfers between devices: 41.7 us -> 44.9 us  [over(): return lax.ppermute(v, ('row', 'col'), pairs)]
    pallas_call x2, Pallas kernels: 9.01 us -> 11 us  [sparse(): pl.pallas_call(functools.partial(sparse_kernel, transpose, n_in), out_sha...]
where the time goes in v5:
time: 186 us; the launch traced here: 185 us
  waiting for transfers between devices  95.3 us (51%)
  starting transfers between devices  67.7 us (36%)
  Pallas kernels  11 us (6%)
  other arithmetic  4.06 us (2%)
  matrix products  3.03 us (2%)
  local copies, waits for them, and re-layouts  2.5 us (1%)
    ppermute x32, waiting for transfers between devices, over(): return lax.ppermute(v, 'row', perm[0])  50.4 us
    ppermute x25, waiting for transfers between devices, over(): return lax.ppermute(v, ('row', 'col'), pairs)  44.9 us
    ppermute x32, starting transfers between devices, over(): return lax.ppermute(v, 'row', perm[0])  41.2 us
    ppermute x25, starting transfers between devices, over(): return lax.ppermute(v, ('row', 'col'), pairs)  26.5 us
    pallas_call x2, Pallas kernels, sparse(): pl.pallas_call(functools.partial(sparse_kernel, transpose, n_in), out_sha...  11 us
  transfers between devices with their start and end apart: 57, of which 32 were waited for; matrix products, arithmetic and copies ran while one was open for 3% of the time, Pallas kernels for 0%

profile of v5, /device:TPU:1, one launch (start us, length us, event | category | flops | bytes accessed | tf_op | source)
XLA Modules:
  0.0 185.2 jit_solution(11409523833281256109)
XLA Ops:
  2.1 2.6 %collective-permute-start = (bf16[1024,256]{1,0:T(8,128)(2,1)}, bf16[1024,256]{1,0:T(8,128)(2,1)S(1)}, u32[]{:S(2)}, u32[]{:S(2)}) collective-permute-start(bf16[1024,256]{1,0:T(8,128)(2,1)} %bitcast.23), channel_id=1, source_target_pairs={{0,16},{8,56},{16,32},{24,8},{32,48},{40,24},{48,0},{56,40},{64,80... | collective-permute-start | bytes 1572872 | tf_op jit(solution)/shard_map/ppermute | solution.py:35
  6.5 3.6 %collective-permute-start.2 = (bf16[1024,256]{1,0:T(8,128)(2,1)}, bf16[1024,256]{1,0:T(8,128)(2,1)S(1)}, u32[]{:S(2)}, u32[]{:S(2)}) collective-permute-start(bf16[1024,256]{1,0:T(8,128)(2,1)} %bitcast.24), channel_id=1, source_target_pairs={{0,64},{8,72},{16,80},{24,88},{32,96},{40,104},{48,112},{56,120},{... | collective-permute-start | bytes 1572872 | tf_op jit(solution)/shard_map/ppermute | solution.py:35
  11.2 3.3 %collective-permute-start.1 = (bf16[1024,256]{1,0:T(8,128)(2,1)S(1)}, bf16[1024,256]{1,0:T(8,128)(2,1)S(1)}, u32[]{:S(2)}, u32[]{:S(2)}) collective-permute-start(bf16[1024,256]{1,0:T(8,128)(2,1)S(1)} %collective-permute-done.refs_4_), channel_id=1, source_target_pairs={{0,16},{8,56},{16,32},{24,8},{32,48},{40,24},{48,0},{56,40},{64,80... | collective-permute-start | bytes 1572872 | tf_op jit(solution)/shard_map/ppermute | solution.py:35
  16.7 5.4 %collective-permute-done.2.refs_2_ = bf16[1024,256]{1,0:T(8,128)(2,1)S(1)} collective-permute-done((bf16[1024,256]{1,0:T(8,128)(2,1)}, bf16[1024,256]{1,0:T(8,128)(2,1)S(1)}, u32[]{:S(2)}, u32[]{:S(2)}) %collective-permute-start.2) | collective-permute-done | bytes 524320 | tf_op jit(solution)/shard_map/ppermute | solution.py:35
  25.4 3.6 %collective-permute-start.8 = (bf16[1024,256]{1,0:T(8,128)(2,1)S(1)}, bf16[1024,256]{1,0:T(8,128)(2,1)S(1)}, u32[]{:S(2)}, u32[]{:S(2)}) collective-permute-start(bf16[1024,256]{1,0:T(8,128)(2,1)S(1)} %collective-permute-done.1.refs_12_), channel_id=1, source_target_pairs={{0,64},{8,72},{16,80},{24,88},{32,96},{40,104},{48,112},{56,120},{... | collective-permute-start | bytes 1572872 | tf_op jit(solution)/shard_map/ppermute | solution.py:35
  30.1 2.3 %collective-permute-done.6.refs_6_ = bf16[1024,256]{1,0:T(8,128)(2,1)S(1)} collective-permute-done((bf16[1024,256]{1,0:T(8,128)(2,1)S(1)}, bf16[1024,256]{1,0:T(8,128)(2,1)S(1)}, u32[]{:S(2)}, u32[]{:S(2)}) %collective-permute-start.6) | collective-permute-done | bytes 524320 | tf_op jit(solution)/shard_map/ppermute | solution.py:35
  32.4 2.1 %collective-permute-start.13 = (bf16[1024,256]{1,0:T(8,128)(2,1)S(1)}, bf16[1024,256]{1,0:T(8,128)(2,1)S(1)}, u32[]{:S(2)}, u32[]{:S(2)}) collective-permute-start(bf16[1024,256]{1,0:T(8,128)(2,1)S(1)} %collective-permute-done.1.refs_12_), channel_id=1, source_target_pairs={{0,8},{8,0},{16,24},{24,16},{32,40},{40,32},{48,56},{56,48},{64,72... | collective-permute-start | bytes 1572872 | tf_op jit(solution)/shard_map/ppermute | solution.py:35
  34.5 5.9 %collective-permute-done.8.refs_13_ = bf16[1024,256]{1,0:T(8,128)(2,1)S(1)} collective-permute-done((bf16[1024,256]{1,0:T(8,128)(2,1)S(1)}, bf16[1024,256]{1,0:T(8,128)(2,1)S(1)}, u32[]{:S(2)}, u32[]{:S(2)}) %collective-permute-start.8) | collective-permute-done | bytes 524320 | tf_op jit(solution)/shard_map/ppermute | solution.py:35
  45.7 5.7 %sparse_forward.1 = (bf16[1024,256]{1,0:T(8,128)(2,1)S(1)}, bf16[1024,256]{1,0:T(8,128)(2,1)S(1)}, bf16[1024,256]{1,0:T(8,128)(2,1)S(1)}, bf16[1024,256]{1,0:T(8...) custom-call(s32[192]{0:T(256)S(1)} %get-tuple-element.63.rows.cols, ...), custom_call_target="tpu_custom_call" | custom-call | flops 1610612736 | bytes 18874368 | tf_op jit(solution)/shard_map/sparse_forward/pallas_call | solution.py:265
  51.5 3.4 %collective-permute-start.18 = (bf16[1024,256]{1,0:T(8,128)(2,1)S(1)}, bf16[1024,256]{1,0:T(8,128)(2,1)S(1)}, u32[]{:S(2)}, u32[]{:S(2)}) collective-permute-start(bf16[1024,256]{1,0:T(8,128)(2,1)S(1)} %get-tuple-element.75), channel_id=1, source_target_pairs={{0,6},{8,10},{2,0},{10,12},{4,2},{12,14},{6,4},{14,8},{1,7},{9,11}... | collective-permute-start | bytes 1572872 | tf_op jit(solution)/shard_map/ppermute | solution.py:41
  58.0 3.1 %collective-permute-done.18 = bf16[1024,256]{1,0:T(8,128)(2,1)S(1)} collective-permute-done((bf16[1024,256]{1,0:T(8,128)(2,1)S(1)}, bf16[1024,256]{1,0:T(8,128)(2,1)S(1)}, u32[]{:S(2)}, u32[]{:S(2)}) %collective-permute-start.18) | collective-permute-done | bytes 524320 | tf_op jit(solution)/shard_map/ppermute | solution.py:41
  61.0 5.6 %collective-permute-done.17 = bf16[1024,256]{1,0:T(8,128)(2,1)S(1)} collective-permute-done((bf16[1024,256]{1,0:T(8,128)(2,1)S(1)}, bf16[1024,256]{1,0:T(8,128)(2,1)S(1)}, u32[]{:S(2)}, u32[]{:S(2)}) %collective-permute-start.17) | collective-permute-done | bytes 524320 | tf_op jit(solution)/shard_map/ppermute | solution.py:41
  72.5 6.7 %collective-permute-done.19 = bf16[1024,256]{1,0:T(8,128)(2,1)S(1)} collective-permute-done((bf16[1024,256]{1,0:T(8,128)(2,1)S(1)}, bf16[1024,256]{1,0:T(8,128)(2,1)S(1)}, u32[]{:S(2)}, u32[]{:S(2)}) %collective-permute-start.19) | collective-permute-done | bytes 524320 | tf_op jit(solution)/shard_map/ppermute | solution.py:41
  79.7 5.1 %collective-permute-done.24 = bf16[1024,256]{1,0:T(8,128)(2,1)S(1)} collective-permute-done((bf16[1024,256]{1,0:T(8,128)(2,1)S(1)}, bf16[1024,256]{1,0:T(8,128)(2,1)S(1)}, u32[]{:S(2)}, u32[]{:S(2)}) %collective-permute-start.24) | collective-permute-done | bytes 524320 | tf_op jit(solution)/shard_map/ppermute | solution.py:41
  85.9 4.5 %collective-permute-done.21 = bf16[1024,256]{1,0:T(8,128)(2,1)S(1)} collective-permute-done((bf16[1024,256]{1,0:T(8,128)(2,1)S(1)}, bf16[1024,256]{1,0:T(8,128)(2,1)S(1)}, u32[]{:S(2)}, u32[]{:S(2)}) %collective-permute-start.21) | collective-permute-done | bytes 524320 | tf_op jit(solution)/shard_map/ppermute | solution.py:41
  93.3 2.3 %collective-permute-start.27 = (bf16[1024,256]{1,0:T(8,128)(2,1)S(1)}, bf16[1024,256]{1,0:T(8,128)(2,1)S(1)}, u32[]{:S(2)}, u32[]{:S(2)}) collective-permute-start(bf16[1024,256]{1,0:T(8,128)(2,1)S(1)} %get-tuple-element.121.refs_0_), channel_id=1, source_target_pairs={{0,2},{8,14},{2,4},{10,8},{4,6},{12,10},{6,0},{14,12},{1,3},{9,15}... | collective-permute-start | bytes 1572872 | tf_op jit(solution)/shard_map/ppermute | solution.py:41
  98.3 3.4 %collective-permute-done.27.refs_2_ = bf16[1024,256]{1,0:T(8,128)(2,1)S(1)} collective-permute-done((bf16[1024,256]{1,0:T(8,128)(2,1)S(1)}, bf16[1024,256]{1,0:T(8,128)(2,1)S(1)}, u32[]{:S(2)}, u32[]{:S(2)}) %collective-permute-start.27) | collective-permute-done | bytes 524320 | tf_op jit(solution)/shard_map/ppermute | solution.py:41
  101.7 3.1 %collective-permute-start.29 = (bf16[1024,256]{1,0:T(8,128)(2,1)S(1)}, bf16[1024,256]{1,0:T(8,128)(2,1)S(1)}, u32[]{:S(2)}, u32[]{:S(2)}) collective-permute-start(bf16[1024,256]{1,0:T(8,128)(2,1)S(1)} %collective-permute-done.27.refs_2_), channel_id=1, source_target_pairs={{0,2},{8,14},{2,4},{10,8},{4,6},{12,10},{6,0},{14,12},{1,3},{9,15}... | collective-permute-start | bytes 1572872 | tf_op jit(solution)/shard_map/ppermute | solution.py:41
  104.8 3.5 %collective-permute-start.28 = (f32[136,256]{1,0:T(8,128)S(1)}, f32[136,256]{1,0:T(8,128)S(1)}, u32[]{:S(2)}, u32[]{:S(2)}) collective-permute-start(f32[136,256]{1,0:T(8,128)S(1)} %dynamic-slice_add_fusion), channel_id=1, source_target_pairs={{0,64},{8,72},{16,80},{24,88},{32,96},{40,104},{48,112},{56,120},{... | collective-permute-start | bytes 417800 | tf_op jit(solution)/shard_map/ppermute | solution.py:35
  109.3 6.4 %collective-permute-done.28 = f32[136,256]{1,0:T(8,128)S(1)} collective-permute-done((f32[136,256]{1,0:T(8,128)S(1)}, f32[136,256]{1,0:T(8,128)S(1)}, u32[]{:S(2)}, u32[]{:S(2)}) %collective-permute-start.28) | collective-permute-done | bytes 139296 | tf_op jit(solution)/shard_map/ppermute | solution.py:35
  122.0 2.1 %collective-permute-done.35 = f32[136,256]{1,0:T(8,128)S(1)} collective-permute-done((f32[136,256]{1,0:T(8,128)S(1)}, f32[136,256]{1,0:T(8,128)S(1)}, u32[]{:S(2)}, u32[]{:S(2)}) %collective-permute-start.35) | collective-permute-done | bytes 139296 | tf_op jit(solution)/shard_map/ppermute | solution.py:35
  124.1 6.4 %collective-permute-done.38.refs_7_ = bf16[1024,256]{1,0:T(8,128)(2,1)S(1)} collective-permute-done((bf16[1024,256]{1,0:T(8,128)(2,1)S(1)}, bf16[1024,256]{1,0:T(8,128)(2,1)S(1)}, u32[]{:S(2)}, u32[]{:S(2)}) %collective-permute-start.38) | collective-permute-done | bytes 524320 | tf_op jit(solution)/shard_map/ppermute | solution.py:41
  132.8 5.3 %sparse_back.1 = (bf16[1024,256]{1,0:T(8,128)(2,1)S(1)}, bf16[1024,256]{1,0:T(8,128)(2,1)S(1)}, bf16[1024,256]{1,0:T(8,128)(2,1)S(1)}, bf16[1024,256]{1,0:T(8,12...) custom-call(s32[192]{0:T(256)S(1)} %get-tuple-element.64.cols.rows, ...), custom_call_target="tpu_custom_call" | custom-call | flops 1610612736 | bytes 18874368 | tf_op jit(solution)/shard_map/sparse_back/pallas_call | solution.py:265
  139.8 2.2 %collective-permute-done.42 = bf16[2048,256]{1,0:T(8,128)(2,1)S(1)} collective-permute-done((bf16[2048,256]{1,0:T(8,128)(2,1)S(1)}, bf16[2048,256]{1,0:T(8,128)(2,1)S(1)}, u32[]{:S(2)}, u32[]{:S(2)}) %collective-permute-start.42) | collective-permute-done | bytes 1048608 | tf_op jit(solution)/shard_map/ppermute | solution.py:35
  142.4 3.0 %collective-permute-start.40 = (bf16[2048,256]{1,0:T(8,128)(2,1)S(1)}, bf16[2048,256]{1,0:T(8,128)(2,1)S(1)}, u32[]{:S(2)}, u32[]{:S(2)}) collective-permute-start(bf16[2048,256]{1,0:T(8,128)(2,1)S(1)} %get-tuple-element.96), channel_id=1, source_target_pairs={{0,8},{8,0},{16,24},{24,16},{32,40},{40,32},{48,56},{56,48},{64,72... | collective-permute-start | bytes 3145736 | tf_op jit(solution)/shard_map/ppermute | solution.py:35
  147.8 8.0 %collective-permute-done.41 = f32[136,256]{1,0:T(8,128)S(1)} collective-permute-done((f32[136,256]{1,0:T(8,128)S(1)}, f32[136,256]{1,0:T(8,128)S(1)}, u32[]{:S(2)}, u32[]{:S(2)}) %collective-permute-start.41) | collective-permute-done | bytes 139296 | tf_op jit(solution)/shard_map/ppermute | solution.py:35
  157.9 2.8 %collective-permute-done.46 = bf16[1024,256]{1,0:T(8,128)(2,1)S(1)} collective-permute-done((bf16[1024,256]{1,0:T(8,128)(2,1)S(1)}, bf16[1024,256]{1,0:T(8,128)(2,1)S(1)}, u32[]{:S(2)}, u32[]{:S(2)}) %collective-permute-start.46) | collective-permute-done | bytes 524320 | tf_op jit(solution)/shard_map/ppermute | solution.py:35
  160.7 2.3 %collective-permute-done.44 = f32[136,256]{1,0:T(8,128)S(1)} collective-permute-done((f32[136,256]{1,0:T(8,128)S(1)}, f32[136,256]{1,0:T(8,128)S(1)}, u32[]{:S(2)}, u32[]{:S(2)}) %collective-permute-start.44) | collective-permute-done | bytes 139296 | tf_op jit(solution)/shard_map/ppermute | solution.py:41
  165.5 1.9 %collective-permute-start.52 = (bf16[1024,256]{1,0:T(8,128)(2,1)S(1)}, bf16[1024,256]{1,0:T(8,128)(2,1)S(1)}, u32[]{:S(2)}, u32[]{:S(2)}) collective-permute-start(bf16[1024,256]{1,0:T(8,128)(2,1)S(1)} %add_convert_fusion.3), channel_id=1, source_target_pairs={{0,64},{8,72},{16,80},{24,88},{32,96},{40,104},{48,112},{56,120},{... | collective-permute-start | bytes 1572872 | tf_op jit(solution)/shard_map/ppermute | solution.py:35
  167.4 2.0 %collective-permute-done.47 = f32[136,256]{1,0:T(8,128)S(1)} collective-permute-done((f32[136,256]{1,0:T(8,128)S(1)}, f32[136,256]{1,0:T(8,128)S(1)}, u32[]{:S(2)}, u32[]{:S(2)}) %collective-permute-start.47) | collective-permute-done | bytes 139296 | tf_op jit(solution)/shard_map/ppermute | solution.py:41
  169.3 3.7 %collective-permute-done.48 = bf16[1024,256]{1,0:T(8,128)(2,1)S(1)} collective-permute-done((bf16[1024,256]{1,0:T(8,128)(2,1)S(1)}, bf16[1024,256]{1,0:T(8,128)(2,1)S(1)}, u32[]{:S(2)}, u32[]{:S(2)}) %collective-permute-start.48) | collective-permute-done | bytes 524320 | tf_op jit(solution)/shard_map/ppermute | solution.py:35
  173.6 5.0 %collective-permute-done.54 = bf16[1024,256]{1,0:T(8,128)(2,1)S(1)} collective-permute-done((bf16[1024,256]{1,0:T(8,128)(2,1)S(1)}, bf16[1024,256]{1,0:T(8,128)(2,1)S(1)}, u32[]{:S(2)}, u32[]{:S(2)}) %collective-permute-start.54) | collective-permute-done | bytes 524320 | tf_op jit(solution)/shard_map/ppermute | solution.py:35
  (131 shorter events, 57.6 us)
Async XLA Ops:
  4.7 12.0 %collective-permute-start.4 = (bf16[1024,256]{1,0:T(8,128)(2,1)S(1)}, bf16[1024,256]{1,0:T(8,128)(2,1)S(1)}, u32[]{:S(2)}, u32[]{:S(2)}) collective-permute-start(bf16[1024,256]{1,0:T(8,128)(2,1)S(1)} %collective-permute-done.3.refs_1_), channel_id=1, source_target_pairs={{0,16},{8,56},{16,32},{24,8},{32,48},{40,24},{48,0},{56,40},{64,80... | collective-permute-start | bytes 1572872 | tf_op jit(solution)/shard_map/ppermute | solution.py:35
  6.5 15.6 %collective-permute-start.2 = (bf16[1024,256]{1,0:T(8,128)(2,1)}, bf16[1024,256]{1,0:T(8,128)(2,1)S(1)}, u32[]{:S(2)}, u32[]{:S(2)}) collective-permute-start(bf16[1024,256]{1,0:T(8,128)(2,1)} %bitcast.24), channel_id=1, source_target_pairs={{0,64},{8,72},{16,80},{24,88},{32,96},{40,104},{48,112},{56,120},{... | collective-permute-start | bytes 1572872 | tf_op jit(solution)/shard_map/ppermute | solution.py:35
  11.2 11.1 %collective-permute-start.1 = (bf16[1024,256]{1,0:T(8,128)(2,1)S(1)}, bf16[1024,256]{1,0:T(8,128)(2,1)S(1)}, u32[]{:S(2)}, u32[]{:S(2)}) collective-permute-start(bf16[1024,256]{1,0:T(8,128)(2,1)S(1)} %collective-permute-done.refs_4_), channel_id=1, source_target_pairs={{0,16},{8,56},{16,32},{24,8},{32,48},{40,24},{48,0},{56,40},{64,80... | collective-permute-start | bytes 1572872 | tf_op jit(solution)/shard_map/ppermute | solution.py:35
  25.4 15.0 %collective-permute-start.8 = (bf16[1024,256]{1,0:T(8,128)(2,1)S(1)}, bf16[1024,256]{1,0:T(8,128)(2,1)S(1)}, u32[]{:S(2)}, u32[]{:S(2)}) collective-permute-start(bf16[1024,256]{1,0:T(8,128)(2,1)S(1)} %collective-permute-done.1.refs_12_), channel_id=1, source_target_pairs={{0,64},{8,72},{16,80},{24,88},{32,96},{40,104},{48,112},{56,120},{... | collective-permute-start | bytes 1572872 | tf_op jit(solution)/shard_map/ppermute | solution.py:35
  29.0 11.4 %collective-permute-start.7 = (bf16[1024,256]{1,0:T(8,128)(2,1)S(1)}, bf16[1024,256]{1,0:T(8,128)(2,1)S(1)}, u32[]{:S(2)}, u32[]{:S(2)}) collective-permute-start(bf16[1024,256]{1,0:T(8,128)(2,1)S(1)} %collective-permute-done.5.refs_3_), channel_id=1, source_target_pairs={{0,16},{8,56},{16,32},{24,8},{32,48},{40,24},{48,0},{56,40},{64,80... | collective-permute-start | bytes 1572872 | tf_op jit(solution)/shard_map/ppermute | solution.py:35
  29.6 11.3 %collective-permute-start.9 = (bf16[1024,256]{1,0:T(8,128)(2,1)S(1)}, bf16[1024,256]{1,0:T(8,128)(2,1)S(1)}, u32[]{:S(2)}, u32[]{:S(2)}) collective-permute-start(bf16[1024,256]{1,0:T(8,128)(2,1)S(1)} %collective-permute-done.refs_4_), channel_id=1, source_target_pairs={{0,8},{8,0},{16,24},{24,16},{32,40},{40,32},{48,56},{56,48},{64,72... | collective-permute-start | bytes 1572872 | tf_op jit(solution)/shard_map/ppermute | solution.py:35
  29.8 11.8 %collective-permute-start.10 = (bf16[1024,256]{1,0:T(8,128)(2,1)S(1)}, bf16[1024,256]{1,0:T(8,128)(2,1)S(1)}, u32[]{:S(2)}, u32[]{:S(2)}) collective-permute-start(bf16[1024,256]{1,0:T(8,128)(2,1)S(1)} %collective-permute-done.4.refs_5_), channel_id=1, source_target_pairs={{0,8},{8,0},{16,24},{24,16},{32,40},{40,32},{48,56},{56,48},{64,72... | collective-permute-start | bytes 1572872 | tf_op jit(solution)/shard_map/ppermute | solution.py:35
  32.4 9.3 %collective-permute-start.13 = (bf16[1024,256]{1,0:T(8,128)(2,1)S(1)}, bf16[1024,256]{1,0:T(8,128)(2,1)S(1)}, u32[]{:S(2)}, u32[]{:S(2)}) collective-permute-start(bf16[1024,256]{1,0:T(8,128)(2,1)S(1)} %collective-permute-done.1.refs_12_), channel_id=1, source_target_pairs={{0,8},{8,0},{16,24},{24,16},{32,40},{40,32},{48,56},{56,48},{64,72... | collective-permute-start | bytes 1572872 | tf_op jit(solution)/shard_map/ppermute | solution.py:35
  51.5 9.5 %collective-permute-start.18 = (bf16[1024,256]{1,0:T(8,128)(2,1)S(1)}, bf16[1024,256]{1,0:T(8,128)(2,1)S(1)}, u32[]{:S(2)}, u32[]{:S(2)}) collective-permute-start(bf16[1024,256]{1,0:T(8,128)(2,1)S(1)} %get-tuple-element.75), channel_id=1, source_target_pairs={{0,6},{8,10},{2,0},{10,12},{4,2},{12,14},{6,4},{14,8},{1,7},{9,11}... | collective-permute-start | bytes 1572872 | tf_op jit(solution)/shard_map/ppermute | solution.py:41
  54.9 11.7 %collective-permute-start.17 = (bf16[1024,256]{1,0:T(8,128)(2,1)S(1)}, bf16[1024,256]{1,0:T(8,128)(2,1)S(1)}, u32[]{:S(2)}, u32[]{:S(2)}) collective-permute-start(bf16[1024,256]{1,0:T(8,128)(2,1)S(1)} %collective-permute-done.16), channel_id=1, source_target_pairs={{0,6},{8,10},{2,0},{10,12},{4,2},{12,14},{6,4},{14,8},{1,7},{9,11}... | collective-permute-start | bytes 1572872 | tf_op jit(solution)/shard_map/ppermute | solution.py:41
  56.4 13.3 %collective-permute-start.15 = (bf16[1024,256]{1,0:T(8,128)(2,1)S(1)}, bf16[1024,256]{1,0:T(8,128)(2,1)S(1)}, u32[]{:S(2)}, u32[]{:S(2)}) collective-permute-start(bf16[1024,256]{1,0:T(8,128)(2,1)S(1)} %get-tuple-element.73), channel_id=1, source_target_pairs={{0,1},{8,9},{2,3},{10,11},{4,5},{12,13},{6,7},{14,15},{1,0},{9,8},... | collective-permute-start | bytes 1572872 | tf_op jit(solution)/shard_map/ppermute | solution.py:41
  58.0 13.2 %collective-permute-start.23 = (bf16[1024,256]{1,0:T(8,128)(2,1)S(1)}, bf16[1024,256]{1,0:T(8,128)(2,1)S(1)}, u32[]{:S(2)}, u32[]{:S(2)}) collective-permute-start(bf16[1024,256]{1,0:T(8,128)(2,1)S(1)} %get-tuple-element.80), channel_id=1, source_target_pairs={{0,8},{8,0},{2,10},{10,2},{4,12},{12,4},{6,14},{14,6},{1,9},{9,1},... | collective-permute-start | bytes 1572872 | tf_op jit(solution)/shard_map/ppermute | solution.py:41
  69.8 9.3 %collective-permute-start.19 = (bf16[1024,256]{1,0:T(8,128)(2,1)S(1)}, bf16[1024,256]{1,0:T(8,128)(2,1)S(1)}, u32[]{:S(2)}, u32[]{:S(2)}) collective-permute-start(bf16[1024,256]{1,0:T(8,128)(2,1)S(1)} %add_convert_fusion.13), channel_id=1, source_target_pairs={{0,6},{8,10},{2,0},{10,12},{4,2},{12,14},{6,4},{14,8},{1,7},{9,11}... | collective-permute-start | bytes 1572872 | tf_op jit(solution)/shard_map/ppermute | solution.py:41
  71.1 13.6 %collective-permute-start.24 = (bf16[1024,256]{1,0:T(8,128)(2,1)S(1)}, bf16[1024,256]{1,0:T(8,128)(2,1)S(1)}, u32[]{:S(2)}, u32[]{:S(2)}) collective-permute-start(bf16[1024,256]{1,0:T(8,128)(2,1)S(1)} %collective-permute-done.23), channel_id=1, source_target_pairs={{0,6},{8,10},{2,0},{10,12},{4,2},{12,14},{6,4},{14,8},{1,7},{9,11}... | collective-permute-start | bytes 1572872 | tf_op jit(solution)/shard_map/ppermute | solution.py:41
  71.8 18.6 %collective-permute-start.22 = (bf16[1024,256]{1,0:T(8,128)(2,1)S(1)}, bf16[1024,256]{1,0:T(8,128)(2,1)S(1)}, u32[]{:S(2)}, u32[]{:S(2)}) collective-permute-start(bf16[1024,256]{1,0:T(8,128)(2,1)S(1)} %add_convert_fusion.12), channel_id=1, source_target_pairs={{0,1},{8,9},{2,3},{10,11},{4,5},{12,13},{6,7},{14,15},{1,0},{9,8},... | collective-permute-start | bytes 1572872 | tf_op jit(solution)/shard_map/ppermute | solution.py:41
  79.3 11.1 %collective-permute-start.21 = (bf16[1024,256]{1,0:T(8,128)(2,1)S(1)}, bf16[1024,256]{1,0:T(8,128)(2,1)S(1)}, u32[]{:S(2)}, u32[]{:S(2)}) collective-permute-start(bf16[1024,256]{1,0:T(8,128)(2,1)S(1)} %add_convert_fusion.11), channel_id=1, source_target_pairs={{0,6},{8,10},{2,0},{10,12},{4,2},{12,14},{6,4},{14,8},{1,7},{9,11}... | collective-permute-start | bytes 1572872 | tf_op jit(solution)/shard_map/ppermute | solution.py:41
  96.1 13.2 %collective-permute-start.30 = (bf16[1024,256]{1,0:T(8,128)(2,1)S(1)}, bf16[1024,256]{1,0:T(8,128)(2,1)S(1)}, u32[]{:S(2)}, u32[]{:S(2)}) collective-permute-start(bf16[1024,256]{1,0:T(8,128)(2,1)S(1)} %get-tuple-element.121.refs_0_), channel_id=1, source_target_pairs={{0,1},{8,9},{2,3},{10,11},{4,5},{12,13},{6,7},{14,15},{1,0},{9,8},... | collective-permute-start | bytes 1572872 | tf_op jit(solution)/shard_map/ppermute | solution.py:41
  97.4 10.9 %collective-permute-start.32 = (bf16[1024,256]{1,0:T(8,128)(2,1)}, bf16[1024,256]{1,0:T(8,128)(2,1)S(1)}, u32[]{:S(2)}, u32[]{:S(2)}) collective-permute-start(bf16[1024,256]{1,0:T(8,128)(2,1)} %collective-permute-done.31), channel_id=1, source_target_pairs={{0,2},{8,14},{2,4},{10,8},{4,6},{12,10},{6,0},{14,12},{1,3},{9,15}... | collective-permute-start | bytes 1572872 | tf_op jit(solution)/shard_map/ppermute | solution.py:41
  101.7 14.0 %collective-permute-start.29 = (bf16[1024,256]{1,0:T(8,128)(2,1)S(1)}, bf16[1024,256]{1,0:T(8,128)(2,1)S(1)}, u32[]{:S(2)}, u32[]{:S(2)}) collective-permute-start(bf16[1024,256]{1,0:T(8,128)(2,1)S(1)} %collective-permute-done.27.refs_2_), channel_id=1, source_target_pairs={{0,2},{8,14},{2,4},{10,8},{4,6},{12,10},{6,0},{14,12},{1,3},{9,15}... | collective-permute-start | bytes 1572872 | tf_op jit(solution)/shard_map/ppermute | solution.py:41
  104.8 10.9 %collective-permute-start.28 = (f32[136,256]{1,0:T(8,128)S(1)}, f32[136,256]{1,0:T(8,128)S(1)}, u32[]{:S(2)}, u32[]{:S(2)}) collective-permute-start(f32[136,256]{1,0:T(8,128)S(1)} %dynamic-slice_add_fusion), channel_id=1, source_target_pairs={{0,64},{8,72},{16,80},{24,88},{32,96},{40,104},{48,112},{56,120},{... | collective-permute-start | bytes 417800 | tf_op jit(solution)/shard_map/ppermute | solution.py:35
  117.0 13.6 %collective-permute-start.38 = (bf16[1024,256]{1,0:T(8,128)(2,1)S(1)}, bf16[1024,256]{1,0:T(8,128)(2,1)S(1)}, u32[]{:S(2)}, u32[]{:S(2)}) collective-permute-start(bf16[1024,256]{1,0:T(8,128)(2,1)S(1)} %collective-permute-done.29.refs_6_), channel_id=1, source_target_pairs={{0,1},{8,9},{2,3},{10,11},{4,5},{12,13},{6,7},{14,15},{1,0},{9,8},... | collective-permute-start | bytes 1572872 | tf_op jit(solution)/shard_map/ppermute | solution.py:41
  118.5 12.0 %collective-permute-start.37 = (bf16[1024,256]{1,0:T(8,128)(2,1)S(1)}, bf16[1024,256]{1,0:T(8,128)(2,1)S(1)}, u32[]{:S(2)}, u32[]{:S(2)}) collective-permute-start(bf16[1024,256]{1,0:T(8,128)(2,1)S(1)} %collective-permute-done.36), channel_id=1, source_target_pairs={{0,2},{8,14},{2,4},{10,8},{4,6},{12,10},{6,0},{14,12},{1,3},{9,15}... | collective-permute-start | bytes 1572872 | tf_op jit(solution)/shard_map/ppermute | solution.py:41
  120.2 11.1 %collective-permute-start.34 = (bf16[1024,256]{1,0:T(8,128)(2,1)S(1)}, bf16[1024,256]{1,0:T(8,128)(2,1)S(1)}, u32[]{:S(2)}, u32[]{:S(2)}) collective-permute-start(bf16[1024,256]{1,0:T(8,128)(2,1)S(1)} %collective-permute-done.32), channel_id=1, source_target_pairs={{0,8},{8,0},{2,10},{10,2},{4,12},{12,4},{6,14},{14,6},{1,9},{9,1},... | collective-permute-start | bytes 1572872 | tf_op jit(solution)/shard_map/ppermute | solution.py:41
  120.2 12.3 %collective-permute-start.33 = (bf16[1024,256]{1,0:T(8,128)(2,1)S(1)}, bf16[1024,256]{1,0:T(8,128)(2,1)S(1)}, u32[]{:S(2)}, u32[]{:S(2)}) collective-permute-start(bf16[1024,256]{1,0:T(8,128)(2,1)S(1)} %collective-permute-done.30.refs_1_), channel_id=1, source_target_pairs={{0,2},{8,14},{2,4},{10,8},{4,6},{12,10},{6,0},{14,12},{1,3},{9,15}... | collective-permute-start | bytes 1572872 | tf_op jit(solution)/shard_map/ppermute | solution.py:41
  142.3 13.5 %collective-permute-start.43 = (bf16[1024,256]{1,0:T(8,128)(2,1)S(1)}, bf16[1024,256]{1,0:T(8,128)(2,1)S(1)}, u32[]{:S(2)}, u32[]{:S(2)}) collective-permute-start(bf16[1024,256]{1,0:T(8,128)(2,1)S(1)} %get-tuple-element.123), channel_id=1, source_target_pairs={{0,48},{8,24},{16,0},{24,40},{32,16},{40,56},{48,32},{56,8},{64,11... | collective-permute-start | bytes 1572872 | tf_op jit(solution)/shard_map/ppermute | solution.py:35
  142.4 22.5 %collective-permute-start.40 = (bf16[2048,256]{1,0:T(8,128)(2,1)S(1)}, bf16[2048,256]{1,0:T(8,128)(2,1)S(1)}, u32[]{:S(2)}, u32[]{:S(2)}) collective-permute-start(bf16[2048,256]{1,0:T(8,128)(2,1)S(1)} %get-tuple-element.96), channel_id=1, source_target_pairs={{0,8},{8,0},{16,24},{24,16},{32,40},{40,32},{48,56},{56,48},{64,72... | collective-permute-start | bytes 3145736 | tf_op jit(solution)/shard_map/ppermute | solution.py:35
  145.5 15.1 %collective-permute-start.46 = (bf16[1024,256]{1,0:T(8,128)(2,1)S(1)}, bf16[1024,256]{1,0:T(8,128)(2,1)S(1)}, u32[]{:S(2)}, u32[]{:S(2)}) collective-permute-start(bf16[1024,256]{1,0:T(8,128)(2,1)S(1)} %add_convert_fusion.8), channel_id=1, source_target_pairs={{0,64},{8,72},{16,80},{24,88},{32,96},{40,104},{48,112},{56,120},{... | collective-permute-start | bytes 1572872 | tf_op jit(solution)/shard_map/ppermute | solution.py:35
  147.3 17.7 %collective-permute-start.49 = (bf16[1024,256]{1,0:T(8,128)(2,1)S(1)}, bf16[1024,256]{1,0:T(8,128)(2,1)S(1)}, u32[]{:S(2)}, u32[]{:S(2)}) collective-permute-start(bf16[1024,256]{1,0:T(8,128)(2,1)S(1)} %get-tuple-element.122), channel_id=1, source_target_pairs={{0,48},{8,24},{16,0},{24,40},{32,16},{40,56},{48,32},{56,8},{64,11... | collective-permute-start | bytes 1572872 | tf_op jit(solution)/shard_map/ppermute | solution.py:35
  163.2 9.8 %collective-permute-start.48 = (bf16[1024,256]{1,0:T(8,128)(2,1)S(1)}, bf16[1024,256]{1,0:T(8,128)(2,1)S(1)}, u32[]{:S(2)}, u32[]{:S(2)}) collective-permute-start(bf16[1024,256]{1,0:T(8,128)(2,1)S(1)} %add_convert_fusion.7), channel_id=1, source_target_pairs={{0,48},{8,24},{16,0},{24,40},{32,16},{40,56},{48,32},{56,8},{64,11... | collective-permute-start | bytes 1572872 | tf_op jit(solution)/shard_map/ppermute | solution.py:35
  165.1 13.5 %collective-permute-start.54 = (bf16[1024,256]{1,0:T(8,128)(2,1)S(1)}, bf16[1024,256]{1,0:T(8,128)(2,1)S(1)}, u32[]{:S(2)}, u32[]{:S(2)}) collective-permute-start(bf16[1024,256]{1,0:T(8,128)(2,1)S(1)} %add_convert_fusion.6), channel_id=1, source_target_pairs={{0,48},{8,24},{16,0},{24,40},{32,16},{40,56},{48,32},{56,8},{64,11... | collective-permute-start | bytes 1572872 | tf_op jit(solution)/shard_map/ppermute | solution.py:35
  165.5 18.5 %collective-permute-start.52 = (bf16[1024,256]{1,0:T(8,128)(2,1)S(1)}, bf16[1024,256]{1,0:T(8,128)(2,1)S(1)}, u32[]{:S(2)}, u32[]{:S(2)}) collective-permute-start(bf16[1024,256]{1,0:T(8,128)(2,1)S(1)} %add_convert_fusion.3), channel_id=1, source_target_pairs={{0,64},{8,72},{16,80},{24,88},{32,96},{40,104},{48,112},{56,120},{... | collective-permute-start | bytes 1572872 | tf_op jit(solution)/shard_map/ppermute | solution.py:35
  173.4 10.6 %collective-permute-start.51 = (bf16[1024,256]{1,0:T(8,128)(2,1)S(1)}, bf16[1024,256]{1,0:T(8,128)(2,1)S(1)}, u32[]{:S(2)}, u32[]{:S(2)}) collective-permute-start(bf16[1024,256]{1,0:T(8,128)(2,1)S(1)} %add_convert_fusion.2), channel_id=1, source_target_pairs={{0,48},{8,24},{16,0},{24,40},{32,16},{40,56},{48,32},{56,8},{64,11... | collective-permute-start | bytes 1572872 | tf_op jit(solution)/shard_map/ppermute | solution.py:35
  (34 other events, 324.6 us)
